TPU v7x, 128 devices: a whole 4x4x4 slice. The times are simulated.
128 devices in a mesh: wide: 16 (over x, y_lo, core), narrow: 8 (over y_hi, z).
Axes of the slice: x: 4, y: 4 (y_hi: 2, y_lo: 2; y = y_hi * 2 + y_lo), z: 4, core: 2. Of those that a mesh axis runs over, the one named last changes fastest.
Arguments:
- object_field: float32 [2, 4096, 16384], P(None, 'narrow', 'wide'), may hold values from -6 to 6
- probe_modes: float32 [4, 2, 256, 256], replicated, may hold values from -4 to 4
- amplitudes: float32 [8, 16, 6, 256, 256], P('narrow', 'wide'), may hold values from 0.5 to 4
- offsets: int32 [2, 8, 16, 6], P(None, 'narrow', 'wide'), may hold values from 0 to 1024, as said below
- counts: int32 [8, 16], P('narrow', 'wide'), may hold values from 1 to 6, as said below
Outputs:
- new_object: float32 [2, 4096, 16384], P(None, 'narrow', 'wide')
- new_probe: float32 [4, 2, 256, 256], replicated
Inputs may be any that keep to these rules, and one draw needn't show every extreme that they name: `offsets`: row 0: a window's top edge relative to the tile's margin-extended frame, at most 512; row 1: its left edge, at most 1024. Entries of slots that are not live carry no meaning. Live slots of a tile are its first counts slots; some tile holds 6 and some tile holds 1.
All inputs are finite; a program needn't handle non-finite values.
Results may differ from a plain program's by a relative error of at most 0.0001.
Values sent between devices are 32-bit elements; how exact they have to be, the bound alone decides.
No kernel may reach another device: no remote copies, remote signals or barrier semaphores. Data moves between devices by JAX's collectives and lax.ppermute only.
A program may use at most 128 MiB of HBM per device.

v0:
```python
import jax
import jax.numpy as jnp
from jax import lax
from jax.sharding import PartitionSpec as P

amp_floor = 0.25
step_floor = 1.0


def padded(cells, sides, width):
    for axis, dim in sides:
        count = lax.axis_size(axis)
        ends = count - 1
        head = lax.slice_in_dim(cells, 0, width, axis=dim)
        tail = lax.slice_in_dim(cells, cells.shape[dim] - width, cells.shape[dim], axis=dim)
        cells = jnp.concatenate(
            [
                lax.ppermute(tail, axis, [(i, (i + 1) % count) for i in range(ends)]),
                cells,
                lax.ppermute(head, axis, [((i + 1) % count, i) for i in range(ends)]),
            ],
            axis=dim,
        )
    return cells


def shifted(block, axis, distance):
    devices = range(lax.axis_size(axis))
    route = [(i - distance, i) for i in devices if i - distance in devices]
    return lax.ppermute(block, axis, route)


def tables(length):
    pixel_index = jnp.arange(length, dtype=jnp.int32)
    phase_int = pixel_index[:, None] * pixel_index[None, :] % length
    angle_rad = phase_int.astype(jnp.float32) * (2.0 * jnp.pi / length)
    norm_scale = 1.0 / jnp.sqrt(jnp.float32(length))
    return (jnp.cos(angle_rad) * norm_scale, -jnp.sin(angle_rad) * norm_scale)


def transform(part_re, part_im, cosine, sine_table):
    length = cosine.shape[0]
    highest = lax.Precision.HIGHEST
    stacked = jnp.concatenate([cosine, sine_table], axis=0)
    left_re = jnp.einsum("ux,mxy->muy", stacked, part_re, precision=highest)
    left_im = jnp.einsum("ux,mxy->muy", stacked, part_im, precision=highest)
    mid_re = left_re[:, :length] - left_im[:, length:]
    mid_im = left_im[:, :length] + left_re[:, length:]
    across = jnp.concatenate([cosine, sine_table], axis=1)
    right_re = jnp.einsum("muy,yv->muv", mid_re, across, precision=highest)
    right_im = jnp.einsum("muy,yv->muv", mid_im, across, precision=highest)
    out_re = right_re[..., :length] - right_im[..., length:]
    out_im = right_im[..., :length] + right_re[..., length:]
    return (out_re, out_im)


def position_terms(window, measured, probe_modes, cosine, sine_table):
    probe_re = probe_modes[:, 0]
    probe_im = probe_modes[:, 1]
    window_re = window[0]
    window_im = window[1]
    wave_re = probe_re * window_re - probe_im * window_im
    wave_im = probe_re * window_im + probe_im * window_re
    far_re, far_im = transform(wave_re, wave_im, cosine, sine_table)
    model_amp = jnp.sqrt(jnp.sum(far_re * far_re + far_im * far_im, axis=0) + amp_floor)
    factor = 1.0 - measured / model_amp
    back_re, back_im = transform(far_re * factor, far_im * factor, cosine, -sine_table)
    object_re = jnp.sum(probe_re * back_re + probe_im * back_im, axis=0)
    object_im = jnp.sum(probe_re * back_im - probe_im * back_re, axis=0)
    grad_re = window_re * back_re + window_im * back_im
    grad_im = window_re * back_im - window_im * back_re
    window_power = window_re * window_re + window_im * window_im
    return (jnp.stack([object_re, object_im]), jnp.stack([grad_re, grad_im], axis=1), window_power)


def on_device(object_field, probe_modes, amplitudes, offsets, counts):
    extent = probe_modes.shape[-1]
    margin = extent // 2
    rows_tile = object_field.shape[1]
    cols_tile = object_field.shape[2]
    cosine, sine_table = tables(extent)
    extended = padded(object_field, (("wide", 2), ("narrow", 1)), margin)
    illum_one = jnp.sum(probe_modes * probe_modes, axis=(0, 1))
    my_count = counts[0, 0]
    my_offsets = offsets[:, 0, 0]
    my_amps = amplitudes[0, 0]
    zero_idx = jnp.zeros((), jnp.int32)

    def cut_window(slot_index):
        return lax.dynamic_slice(
            extended,
            (zero_idx, my_offsets[0, slot_index], my_offsets[1, slot_index]),
            (2, extent, extent),
        )

    def add_window(totals, slot_index, values):
        start = (zero_idx, my_offsets[0, slot_index], my_offsets[1, slot_index])
        current = lax.dynamic_slice(totals, start, values.shape)
        return lax.dynamic_update_slice(totals, current + values, start)

    totals = jnp.zeros((3, extended.shape[1], extended.shape[2]), jnp.float32)
    probe_sum = jnp.zeros(probe_modes.shape, jnp.float32)
    power_sum = jnp.zeros((extent, extent), jnp.float32)

    def visit_own(slot_index, carry):
        totals, probe_sum, power_sum = carry
        obj_grad, probe_grad, window_power = position_terms(
            cut_window(slot_index), my_amps[slot_index], probe_modes, cosine, sine_table
        )
        stacked = jnp.concatenate([obj_grad, illum_one[None]], axis=0)
        return (
            add_window(totals, slot_index, stacked),
            probe_sum + probe_grad,
            power_sum + window_power,
        )

    totals, probe_sum, power_sum = lax.fori_loop(
        0, my_count, visit_own, (totals, probe_sum, power_sum)
    )
    top_strip = totals[:, :margin]
    bottom_strip = totals[:, margin + rows_tile :]
    from_below = shifted(top_strip, "narrow", -1)
    from_above = shifted(bottom_strip, "narrow", 1)
    middle = totals[:, margin : margin + rows_tile]
    middle = middle.at[:, rows_tile - margin :].add(from_below)
    middle = middle.at[:, :margin].add(from_above)
    left_strip = middle[:, :, :margin]
    right_strip = middle[:, :, margin + cols_tile :]
    from_right = shifted(left_strip, "wide", -1)
    from_left = shifted(right_strip, "wide", 1)
    core_cells = middle[:, :, margin : margin + cols_tile]
    core_cells = core_cells.at[:, :, cols_tile - margin :].add(from_right)
    core_cells = core_cells.at[:, :, :margin].add(from_left)
    grad_core = core_cells[:2]
    illum_core = core_cells[2]
    probe_sum, power_sum = lax.psum((probe_sum, power_sum), ("wide", "narrow"))
    new_object = object_field - grad_core / (illum_core + step_floor)
    new_probe = probe_modes - probe_sum / (power_sum + step_floor)
    return (new_object, new_probe)


def solution(mesh):
    return jax.shard_map(
        on_device,
        mesh=mesh,
        in_specs=(
            P(None, "narrow", "wide"),
            P(),
            P("narrow", "wide", None, None, None),
            P(None, "narrow", "wide", None),
            P("narrow", "wide"),
        ),
        out_specs=(P(None, "narrow", "wide"), P()),
        check_vma=False,
    )
```

profile of v0, /device:TPU:1, one launch (start us, length us, event | category | flops | bytes accessed | tf_op | source)
XLA Modules:
  0.0 594.0 jit_solution(9242890393716330235)
XLA Ops:
  7.2 1.3 fusion.53
  8.5 4.6 collective-permute-start
  13.1 1.9 collective-permute-start.1
  15.0 9.8 %collective-permute-done = f32[2,512,128]{2,1,0:T(8,128)S(1)} collective-permute-done((f32[2,512,128]{2,1,0:T(8,128)S(1)}, f32[2,512,128]{2,1,0:T(8,128)S(1)}, u32[]{:S(2)}, u32[]{:S(2)}) %collective-permute-start) | collective-permute-done | bytes 524320 | tf_op jit(solution)/shard_map/ppermute | solution.py:18
  24.9 2.5 constant_dynamic-update-slice_fusion.1
  27.5 1.8 fusion.52
  29.3 1.3 copy-done.3
  30.6 4.6 collective-permute-start.2
  35.2 1.3 collective-permute-start.3
  36.5 2.0 copy.15
  38.5 1.0 fusion.49
  39.5 1.1 negate_multiply_fusion
  41.5 1.1 pad_maximum_fusion.1
  43.4 9.6 %collective-permute-done.2 = f32[2,128,1280]{2,1,0:T(8,128)} collective-permute-done((f32[2,128,1280]{2,1,0:T(8,128)}, f32[2,128,1280]{2,1,0:T(8,128)}, u32[]{:S(2)}, u32[]{:S(2)}) %collective-permute-start.2) | collective-permute-done | bytes 1310752 | tf_op jit(solution)/shard_map/ppermute | solution.py:18
  53.0 5.2 collective-permute-done.3
  58.2 4.6 pad_maximum_fusion
  63.5 1.5 broadcast_in_dim.21
  65.0 5.3 broadcast_in_dim.20
  70.3 102.8 %while.20 = (s32[]{:T(128)}, f32[3,768,1280]{2,1,0:T(8,128)}, f32[4,2,256,256]{3,2,0,1:T(8,128)}, f32[256,256]{1,0:T(8,128)}, s32[]{:T(128)}, /*index=5*/s32[2,6...) while((s32[]{:T(128)}, f32[3,768,1280]{2,1,0:T(8,128)}, ...), condition=%wide.region_5.6_spmd, body=%wide.region_1.5_spmd.sunk | while | flops 12896239616 | bytes 70517080 | solution.py:117
  75.4 2.1 add_add_fusion.2
  77.6 4.5 convolution_bitcast_fusion.9
  82.0 4.5 convolution_bitcast_fusion.8
  86.5 2.9 fusion.85
  89.5 2.9 fusion.84
  92.7 1.0 fusion.86
  93.7 4.5 convolution_bitcast_fusion.11
  98.2 4.5 convolution_bitcast_fusion.10
  102.7 1.9 fusion.88
  104.6 1.9 fusion.87
  107.3 1.7 maximum_add_fusion.4
  109.0 3.2 maximum_add_fusion.5
  112.2 9.5 %dynamic_update_slice.6 = f32[3,768,1280]{2,1,0:T(8,128)} dynamic-update-slice(f32[3,768,1280]{2,1,0:T(8,128)} %get-tuple-element.407, f32[3,256,256]{2,1,0:T(8,128)S(1)} %maximum_add_fusion.4, s32[]{:T(128)} %constant.159.clone.1..sunk, s32[]{:T(128)S(6)} %select_n.60, s32[]{:T(128)S(6)} %select_n.61) | dynamic-update-slice | bytes 1572868 | tf_op jit(solution)/shard_map/while/body/dynamic_update_slice | solution.py:99
  126.7 2.1 add_add_fusion.2
  128.8 4.5 convolution_bitcast_fusion.9
  133.3 4.5 convolution_bitcast_fusion.8
  137.8 2.9 fusion.85
  140.7 2.9 fusion.84
  143.9 1.0 fusion.86
  144.9 4.5 convolution_bitcast_fusion.11
  149.4 4.5 convolution_bitcast_fusion.10
  154.0 1.9 fusion.88
  155.9 1.9 fusion.87
  158.6 1.7 maximum_add_fusion.4
  160.3 3.2 maximum_add_fusion.5
  163.5 8.8 %dynamic_update_slice.6 = f32[3,768,1280]{2,1,0:T(8,128)} dynamic-update-slice(f32[3,768,1280]{2,1,0:T(8,128)} %get-tuple-element.407, f32[3,256,256]{2,1,0:T(8,128)S(1)} %maximum_add_fusion.4, s32[]{:T(128)} %constant.159.clone.1..sunk, s32[]{:T(128)S(6)} %select_n.60, s32[]{:T(128)S(6)} %select_n.61) | dynamic-update-slice | bytes 1572868 | tf_op jit(solution)/shard_map/while/body/dynamic_update_slice | solution.py:99
  173.1 4.5 fusion.50
  177.6 1.3 collective-permute-start.4
  178.9 106.0 %collective-permute-start.5 = (f32[3,128,1280]{2,1,0:T(8,128)}, f32[3,128,1280]{2,1,0:T(8,128)S(1)}, u32[]{:S(2)}, u32[]{:S(2)}) collective-permute-start(f32[3,128,1280]{2,1,0:T(8,128)} %get-tuple-element.264), channel_id=1, source_target_pairs={{0,1},{1,2},{2,3},{3,4},{4,5},{5,6},{6,7},{8,9},{9,10},{10,11},{11... | collective-permute-start | bytes 5898248 | tf_op jit(solution)/shard_map/ppermute | solution.py:30
  285.0 6.8 %slice.238 = f32[3,512,1280]{2,1,0:T(8,128)} slice(f32[3,768,1280]{2,1,0:T(8,128)} %get-tuple-element.206), slice={[0:3], [128:640], [0:1280]} | slice | bytes 15728640 | tf_op jit(solution)/shard_map/slice | solution.py:124
  291.8 3.0 copy.16
  294.9 10.4 %collective-permute-done.4 = f32[3,128,1280]{2,1,0:T(8,128)} collective-permute-done((f32[3,128,1280]{2,1,0:T(8,128)}, f32[3,128,1280]{2,1,0:T(8,128)}, u32[]{:S(2)}, u32[]{:S(2)}) %collective-permute-start.4) | collective-permute-done | bytes 1966112 | tf_op jit(solution)/shard_map/ppermute | solution.py:30
  305.2 3.6 add_dynamic-update-slice_fusion
  308.9 3.1 fusion.40
  311.9 2.5 fusion.51
  314.5 95.5 %collective-permute-start.6 = (f32[3,512,128]{2,1,0:T(8,128)}, f32[3,512,128]{2,1,0:T(8,128)}, u32[]{:S(2)}, u32[]{:S(2)}) collective-permute-start(f32[3,512,128]{2,1,0:T(8,128)} %get-tuple-element.267), channel_id=1, source_target_pairs={{8,0},{16,8},{24,16},{32,24},{40,32},{48,40},{56,48},{64,56},{72,6... | collective-permute-start | bytes 2359304 | tf_op jit(solution)/shard_map/ppermute | solution.py:30
  410.0 1.9 collective-permute-start.7
  411.9 159.4 %all-reduce.3.cloned.1.call-done = (f32[4,2,256,256]{3,2,1,0:T(8,128)}, f32[256,256]{1,0:T(8,128)}) async-done(((f32[4,2,256,256]{3,2,1,0:T(8,128)}, f32[256,256]{1,0:T(8,128)}), (f32[4,2,256,256]{3,2,1,0:T(8,128)}, f32[256,256]{1,0:T(8,128)})) %all-reduce.3.cloned.1.call-update) | async-done | bytes 2359312 | tf_op jit(solution)/shard_map/psum | solution.py:136
  571.3 1.0 broadcast_add_fusion
  572.3 3.2 divide_subtract_fusion
  575.5 3.4 slice.269
  578.9 1.5 fusion.42
  580.4 1.3 fusion.41
  582.0 1.9 copy-done
  583.9 3.2 fusion.38
  (30 shorter events, 6.4 us)
Async XLA Ops:
  7.2 564.1 %all-reduce.3.cloned.1.call-start = ((), (), s32[]{:S(2)}) async-start(), calls=%async_computation | async-start | bytes 4718592 | tf_op jit(solution)/shard_map/psum | solution.py:136
  8.5 16.3 %collective-permute-start = (f32[2,512,128]{2,1,0:T(8,128)S(1)}, f32[2,512,128]{2,1,0:T(8,128)S(1)}, u32[]{:S(2)}, u32[]{:S(2)}) collective-permute-start(f32[2,512,128]{2,1,0:T(8,128)S(1)} %get-tuple-element.271), channel_id=1, source_target_pairs={{0,8},{8,16},{16,24},{24,32},{32,40},{40,48},{48,56},{56,64},{64,7... | collective-permute-start | bytes 1572872 | tf_op jit(solution)/shard_map/ppermute | solution.py:18
  13.1 14.3 %collective-permute-start.1 = (f32[2,512,128]{2,1,0:T(8,128)S(1)}, f32[2,512,128]{2,1,0:T(8,128)S(1)}, u32[]{:S(2)}, u32[]{:S(2)}) collective-permute-start(f32[2,512,128]{2,1,0:T(8,128)S(1)} %get-tuple-element.270), channel_id=1, source_target_pairs={{8,0},{16,8},{24,16},{32,24},{40,32},{48,40},{56,48},{64,56},{72,6... | collective-permute-start | bytes 1572872 | tf_op jit(solution)/shard_map/ppermute | solution.py:20
  27.5 3.1 copy-start.3
  30.6 22.4 %collective-permute-start.2 = (f32[2,128,1280]{2,1,0:T(8,128)}, f32[2,128,1280]{2,1,0:T(8,128)}, u32[]{:S(2)}, u32[]{:S(2)}) collective-permute-start(f32[2,128,1280]{2,1,0:T(8,128)} %get-tuple-element.268), channel_id=1, source_target_pairs={{0,1},{1,2},{2,3},{3,4},{4,5},{5,6},{6,7},{8,9},{9,10},{10,11},{11... | collective-permute-start | bytes 3932168 | tf_op jit(solution)/shard_map/ppermute | solution.py:18
  35.2 22.9 %collective-permute-start.3 = (f32[2,128,1280]{2,1,0:T(8,128)}, f32[2,128,1280]{2,1,0:T(8,128)}, u32[]{:S(2)}, u32[]{:S(2)}) collective-permute-start(f32[2,128,1280]{2,1,0:T(8,128)} %get-tuple-element.269), channel_id=1, source_target_pairs={{1,0},{2,1},{3,2},{4,3},{5,4},{6,5},{7,6},{9,8},{10,9},{11,10},{12... | collective-permute-start | bytes 3932168 | tf_op jit(solution)/shard_map/ppermute | solution.py:20
  36.5 21.6 %copy-start.4 = (f32[2,512,1280]{2,1,0:T(8,128)S(1)}, f32[2,512,1280]{2,1,0:T(8,128)}, u32[]{:S(2)}) copy-start(f32[2,512,1280]{2,1,0:T(8,128)} %copy-done.3) | copy-start | bytes 15728644
  39.5 3.1 copy-start.1
  65.0 5.3 copy-start.5
  177.6 127.6 %collective-permute-start.4 = (f32[3,128,1280]{2,1,0:T(8,128)}, f32[3,128,1280]{2,1,0:T(8,128)}, u32[]{:S(2)}, u32[]{:S(2)}) collective-permute-start(f32[3,128,1280]{2,1,0:T(8,128)} %get-tuple-element.265), channel_id=1, source_target_pairs={{1,0},{2,1},{3,2},{4,3},{5,4},{6,5},{7,6},{9,8},{10,9},{11,10},{12... | collective-permute-start | bytes 5898248 | tf_op jit(solution)/shard_map/ppermute | solution.py:30
  178.9 130.0 %collective-permute-start.5 = (f32[3,128,1280]{2,1,0:T(8,128)}, f32[3,128,1280]{2,1,0:T(8,128)S(1)}, u32[]{:S(2)}, u32[]{:S(2)}) collective-permute-start(f32[3,128,1280]{2,1,0:T(8,128)} %get-tuple-element.264), channel_id=1, source_target_pairs={{0,1},{1,2},{2,3},{3,4},{4,5},{5,6},{6,7},{8,9},{9,10},{10,11},{11... | collective-permute-start | bytes 5898248 | tf_op jit(solution)/shard_map/ppermute | solution.py:30
  311.9 260.3 %copy-start.2 = (f32[4,2,256,256]{3,2,1,0:T(8,128)S(1)}, f32[4,2,256,256]{3,2,1,0:T(8,128)}, u32[]{:S(2)}) copy-start(f32[4,2,256,256]{3,2,1,0:T(8,128)} %param.16) | copy-start | bytes 6291460
  314.5 264.4 %collective-permute-start.6 = (f32[3,512,128]{2,1,0:T(8,128)}, f32[3,512,128]{2,1,0:T(8,128)}, u32[]{:S(2)}, u32[]{:S(2)}) collective-permute-start(f32[3,512,128]{2,1,0:T(8,128)} %get-tuple-element.267), channel_id=1, source_target_pairs={{8,0},{16,8},{24,16},{32,24},{40,32},{48,40},{56,48},{64,56},{72,6... | collective-permute-start | bytes 2359304 | tf_op jit(solution)/shard_map/ppermute | solution.py:30
  410.0 170.4 %collective-permute-start.7 = (f32[3,512,128]{2,1,0:T(8,128)S(1)}, f32[3,512,128]{2,1,0:T(8,128)}, u32[]{:S(2)}, u32[]{:S(2)}) collective-permute-start(f32[3,512,128]{2,1,0:T(8,128)S(1)} %get-tuple-element.266), channel_id=1, source_target_pairs={{0,8},{8,16},{16,24},{24,32},{32,40},{40,48},{48,56},{56,64},{64,7... | collective-permute-start | bytes 2359304 | tf_op jit(solution)/shard_map/ppermute | solution.py:30
  581.7 2.2 copy-start
Sparse Core Ops, SparseCore 0:
  295.0 276.2 all-reduce.2
where the time goes:
time: 599 us; the launch traced here: 594 us
  starting transfers between devices  217 us (36%)
  waiting for transfers between devices  194 us (32%)
  local copies, waits for them, and re-layouts  58.2 us (10%)
  matrix products  55.1 us (9%)
  other arithmetic  45 us (8%)
  between operations  14.2 us (2%)
  loops' own time  9.84 us (2%)
    ppermute x4, starting transfers between devices, shifted(): return lax.ppermute(block, axis, route)  205 us
    psum x1, waiting for transfers between devices, on_device(): probe_sum, power_sum = lax.psum((probe_sum, power_sum), ('wide', 'narrow'))  159 us
    ppermute x2, waiting for transfers between devices, padded(): lax.ppermute(tail, axis, [(i, (i + 1) % count) for i in range(ends)])  19.4 us
    dynamic_update_slice x2, local copies, waits for them, and re-layouts, add_window(): return lax.dynamic_update_slice(totals, current + values, start)  18.3 us
    dot_general x4, matrix products, transform(): left_re = jnp.einsum('ux,mxy->muy', stacked, part_re, precision=highest)  18 us
    dot_general x4, matrix products, transform(): left_im = jnp.einsum('ux,mxy->muy', stacked, part_im, precision=highest)  18 us
  transfers between devices with their start and end apart: 9, of which 5 were waited for; matrix products, arithmetic and copies ran while one was open for 6% of the time, Pallas kernels for 0%

commit v1 on v0

v1 whole, which is shorter than its diff:
```python
import functools

import jax
import jax.numpy as jnp
import numpy as np
from jax import lax
from jax.experimental import pallas as pl
from jax.experimental.pallas import tpu as pltpu
from jax.sharding import PartitionSpec as P

amp_floor = 0.25
step_floor = 1.0
F32 = jnp.float32
BF16 = jnp.bfloat16
BOTH = ("wide", "narrow")
MIB = 1024 * 1024


def tables(length):
    half = length // 2
    row = np.arange(half)[:, None]
    col = np.arange(half)[None, :]
    pairs = []
    for odd in (0, 1):
        angle = -2.0 * np.pi * (row * (2 * col + odd) % length) / length
        re = np.cos(angle) / np.sqrt(length)
        im = np.sin(angle) / np.sqrt(length)
        matrix = np.block([[re, im], [-im, re]]).astype(np.float32)
        for table in (matrix, matrix.T):
            high = table.astype(jnp.bfloat16)
            low = (table - high.astype(np.float32)).astype(jnp.bfloat16)
            pairs.append((high, low))
    m0, m0t, m1, m1t = pairs
    after = np.stack([np.concatenate([h, h, l], 0) for h, l in (m0, m1, m0t, m1t)])
    before = np.stack([np.concatenate([h, h, l], 1) for h, l in (m0t, m1t, m0, m1)])
    order = np.zeros((length, length), np.float32)
    for k in range(half):
        order[2 * k, k] = 1
        order[2 * k + 1, half + k] = 1
    order = np.concatenate([order, order], 0).astype(jnp.bfloat16)
    return jnp.asarray(after), jnp.asarray(before), jnp.asarray(order)


def split(x):
    high = x.astype(BF16)
    return high, (x - high.astype(F32)).astype(BF16)


def dot(a, b):
    return jnp.dot(a, b, preferred_element_type=F32)


def grads_kernel(
    count, offs, obj, left, right, up, down, cup, cdown, probe, amps, after, before, order,
    core_o, left_o, right_o, up_o, down_o, cup_o, cdown_o, pg,
    ext, tot, win, zs, zd, p0, p1, u, ap, illum, sems, *, modes, n, tr, tc,
):
    h = n // 2
    ch = 64
    nb = ch // 8

    def places(big, core, left, right, up, down, cup, cdown):
        rows, cols = pl.ds(h, tr), pl.ds(h, tc)
        lo, hi = pl.ds(0, h), pl.ds(h + tc, h)
        top, bot = pl.ds(0, h), pl.ds(h + tr, h)
        return [
            (core, big.at[:, rows, cols]),
            (left, big.at[:, rows, lo]),
            (right, big.at[:, rows, hi]),
            (up, big.at[:, top, cols]),
            (down, big.at[:, bot, cols]),
            (cup.at[0], big.at[:, top, lo]),
            (cup.at[1], big.at[:, top, hi]),
            (cdown.at[0], big.at[:, bot, lo]),
            (cdown.at[1], big.at[:, bot, hi]),
        ]

    loads = [
        pltpu.make_async_copy(a, b, sems.at[i])
        for i, (a, b) in enumerate(places(ext, obj, left, right, up, down, cup, cdown))
    ]
    for copy in loads:
        copy.start()
    tot[...] = jnp.zeros_like(tot)
    pg[...] = jnp.zeros_like(pg)
    for r0 in range(0, n, ch):
        rs = pl.ds(r0, ch)
        acc = jnp.zeros((ch, n), F32)
        for k in range(modes):
            for c in range(2):
                v = probe[k, c, rs, :]
                acc = acc + v * v
        illum[rs, :] = acc
    for copy in loads:
        copy.wait()

    lane = lax.broadcasted_iota(jnp.int32, (ch + 8, h), 1)
    sub = lax.broadcasted_iota(jnp.int32, (nb, 8, h), 1)
    sub9 = lax.broadcasted_iota(jnp.int32, (nb + 1, 8, h), 1)

    def after_dot(z, i):
        return dot(jnp.concatenate([z[...], z[:, :n]], axis=1), after[i])

    def before_dot(i, y):
        high, low = split(y)
        return dot(before[i], jnp.concatenate([high, low, high], axis=0))

    def slot(s, carry):
        r = offs[0, s]
        c = offs[1, s]
        q = jnp.minimum(c // h, (ext.shape[2] - 3 * h) // h)
        rem = c - q * h
        q = pl.multiple_of(q * h, h)
        back_lanes = jnp.where((rem == 0) | (rem == h), 0, h - rem)
        fwd_lanes = jnp.where(rem == h, 0, rem)
        r8 = jnp.minimum(r // 8, (ext.shape[1] - n - 8) // 8)
        rr = r - r8 * 8
        r8 = pl.multiple_of(r8 * 8, 8)
        back_rows = jnp.where((rr == 0) | (rr == 8), 0, 8 - rr)
        fwd_rows = jnp.where(rr == 8, 0, rr)
        for r0 in range(0, n, ch):
            rs = pl.ds(r0, ch)
            w = []
            for comp in range(2):
                blk = ext[comp, pl.ds(r8 + r0, ch + 8), pl.ds(q, 3 * h)]
                t = [pltpu.roll(blk[:, j * h : (j + 1) * h], back_lanes, axis=1) for j in range(3)]
                keep = lane < h - rem
                sides = []
                for x, y in ((t[0], t[1]), (t[1], t[2])):
                    g = jnp.where(keep, x, y).reshape(nb + 1, 8, h)
                    g = pltpu.roll(g, back_rows, axis=1)
                    sides.append(jnp.where(sub < 8 - rr, g[:-1], g[1:]).reshape(ch, h))
                v = jnp.concatenate(sides, axis=1)
                win[comp, rs, :] = v
                w.append(v)
            pg[pl.ds(r0 // 8, nb), 2 * modes] += (w[0] * w[0] + w[1] * w[1]).reshape(nb, 8, n)
        for k in range(modes):
            for r0 in range(0, n, ch):
                rs = pl.ds(r0, ch)
                ks = pl.ds(k * n + r0, ch)
                ar, ai = win[0, rs, :], win[1, rs, :]
                pr, pi = probe[k, 0, rs, :], probe[k, 1, rs, :]
                wr = pr * ar - pi * ai
                wi = pr * ai + pi * ar
                z = jnp.concatenate([wr[:, :h] + wr[:, h:], wi[:, :h] + wi[:, h:]], axis=1)
                zs[ks, :n], zs[ks, n:] = split(z)
                z = jnp.concatenate([wr[:, :h] - wr[:, h:], wi[:, :h] - wi[:, h:]], axis=1)
                zd[ks, :n], zd[ks, n:] = split(z)
        p0[...] = after_dot(zs, 0)
        p1[...] = after_dot(zd, 1)
        for k in range(modes):
            top, bot = pl.ds(k * n, h), pl.ds(k * n + h, h)

            def folded(sign):
                parts = []
                for ls in (slice(0, h), slice(h, n)):
                    parts.append(
                        jnp.concatenate([p[top, ls] + sign * p[bot, ls] for p in (p0, p1)], axis=1)
                    )
                return jnp.concatenate(parts, axis=0)

            u[k, 0] = before_dot(0, folded(1.0))
            u[k, 1] = before_dot(1, folded(-1.0))
        am = dot(jnp.concatenate(split(amps[s]), axis=1), order[...])
        ap[0] = am[:, :h]
        ap[1] = am[:, h:]
        factor = []
        for e in range(2):
            power = jnp.zeros((h, n), F32)
            for k in range(modes):
                a, b = u[k, e, :h, :], u[k, e, h:, :]
                power = power + (a * a + b * b)
            am = jnp.concatenate([ap[j, pl.ds(e, h, stride=2), :] for j in range(2)], axis=1)
            factor.append(1.0 - am * lax.rsqrt(power + amp_floor))
        for k in range(modes):
            y = [
                jnp.concatenate([u[k, e, :h, :] * factor[e], u[k, e, h:, :] * factor[e]], axis=0)
                for e in range(2)
            ]
            even, odd = before_dot(2, y[0]), before_dot(3, y[1])
            for half, v in ((0, even + odd), (1, even - odd)):
                ks = pl.ds(k * n + half * h, h)
                for ref, ls in ((zs, slice(0, h)), (zd, slice(h, n))):
                    z = jnp.concatenate([v[:h, ls], v[h:, ls]], axis=1)
                    ref[ks, :n], ref[ks, n:] = split(z)
        p0[...] = after_dot(zs, 2)
        p1[...] = after_dot(zd, 3)
        for r0 in range(0, n, ch):
            rs = pl.ds(r0, ch)
            bs = pl.ds(r0 // 8, nb)
            ar, ai = win[0, rs, :], win[1, rs, :]
            o_re = jnp.zeros((ch, n), F32)
            o_im = jnp.zeros((ch, n), F32)
            for k in range(modes):
                ks = pl.ds(k * n + r0, ch)
                e, o = p0[ks, :], p1[ks, :]
                lhs, rhs = e + o, e - o
                br = jnp.concatenate([lhs[:, :h], rhs[:, :h]], axis=1)
                bi = jnp.concatenate([lhs[:, h:], rhs[:, h:]], axis=1)
                pr, pi = probe[k, 0, rs, :], probe[k, 1, rs, :]
                o_re = o_re + (pr * br + pi * bi)
                o_im = o_im + (pr * bi - pi * br)
                pg[bs, 2 * k] += (ar * br + ai * bi).reshape(nb, 8, n)
                pg[bs, 2 * k + 1] += (ar * bi - ai * br).reshape(nb, 8, n)

            def lowered(v):
                g = pltpu.roll(v.reshape(nb, 8, h), fwd_rows, axis=1)
                zero = jnp.zeros((1, 8, h), F32)
                here = jnp.concatenate([g, zero], axis=0)
                above = jnp.concatenate([zero, g], axis=0)
                return jnp.where(sub9 >= rr, here, above).reshape(ch + 8, h)

            past = lane >= rem
            for comp, v in ((0, o_re), (1, o_im), (2, illum[rs, :])):
                t0 = pltpu.roll(lowered(v[:, :h]), fwd_lanes, axis=1)
                t1 = pltpu.roll(lowered(v[:, h:]), fwd_lanes, axis=1)
                zero = jnp.zeros_like(t0)
                full = [
                    jnp.where(past, t0, zero),
                    jnp.where(past, t1, t0),
                    jnp.where(past, zero, t1),
                ]
                tot[comp, pl.ds(r8 + r0, ch + 8), pl.ds(q, 3 * h)] += jnp.concatenate(full, axis=1)
        return carry

    lax.fori_loop(0, count[0], slot, 0)
    stores = [
        pltpu.make_async_copy(b, a, sems.at[i])
        for i, (a, b) in enumerate(
            places(tot, core_o, left_o, right_o, up_o, down_o, cup_o, cdown_o)
        )
    ]
    for copy in stores:
        copy.start()
    for copy in stores:
        copy.wait()


def tile_grads(count, offs, obj, halos, probe, amps):
    modes, _, n, _ = probe.shape
    h = n // 2
    _, tr, tc = obj.shape
    vmem = pl.BlockSpec(memory_space=pltpu.VMEM)
    smem = pl.BlockSpec(memory_space=pltpu.SMEM)
    anyw = pl.BlockSpec(memory_space=pl.ANY)
    shape = lambda *dims: jax.ShapeDtypeStruct(dims, F32)
    rows, cols = tr + n, tc + n
    return pl.pallas_call(
        functools.partial(grads_kernel, modes=modes, n=n, tr=tr, tc=tc),
        out_shape=(
            shape(3, tr, tc), shape(3, tr, h), shape(3, tr, h), shape(3, h, tc), shape(3, h, tc),
            shape(2, 3, h, h), shape(2, 3, h, h), shape(n // 8, 2 * modes + 1, 8, n),
        ),
        in_specs=[smem, smem] + [anyw] * 7 + [vmem] * 5,
        out_specs=[anyw] * 7 + [vmem],
        scratch_shapes=[
            pltpu.VMEM((2, rows, cols), F32),
            pltpu.VMEM((3, rows, cols), F32),
            pltpu.VMEM((2, n, n), F32),
            pltpu.VMEM((modes * n, 2 * n), BF16),
            pltpu.VMEM((modes * n, 2 * n), BF16),
            pltpu.VMEM((modes * n, n), F32),
            pltpu.VMEM((modes * n, n), F32),
            pltpu.VMEM((modes, 2, n, n), F32),
            pltpu.VMEM((2, n, h), F32),
            pltpu.VMEM((n, n), F32),
            pltpu.SemaphoreType.DMA((9,)),
        ],
        compiler_params=pltpu.CompilerParams(vmem_limit_bytes=56 * MIB),
        cost_estimate=pl.CostEstimate(flops=40_000_000_000, bytes_accessed=30_000_000, transcendentals=0),
        name="tile_grads",
    )(count, offs, obj, *halos, probe, amps, *tables(n))


def object_update(obj, core, left, right, up, down):
    h = left.shape[-1]
    total = core + jnp.pad(left, ((0, 0), (0, 0), (0, core.shape[2] - h)))
    total = total + jnp.pad(right, ((0, 0), (0, 0), (core.shape[2] - h, 0)))
    total = total + jnp.pad(up, ((0, 0), (0, core.shape[1] - h), (0, 0)))
    total = total + jnp.pad(down, ((0, 0), (core.shape[1] - h, 0), (0, 0)))
    return obj - total[:2] / (total[2] + step_floor)


def moved(block, axis, distance):
    count = lax.axis_size(axis)
    route = [(i, i + distance) for i in range(count) if 0 <= i + distance < count]
    return lax.ppermute(block, axis, route)


def place(flat):
    w, n = flat // 8, flat % 8
    return {"core": w % 2, "x": w // 4, "y": (n // 4) * 2 + (w // 2) % 2, "z": n % 4}


def flat_of(at):
    w = at["x"] * 4 + (at["y"] % 2) * 2 + at["core"]
    n = (at["y"] // 2) * 4 + at["z"]
    return w * 8 + n


def route(step):
    pairs = []
    for i in range(128):
        at = place(i)
        if step == "core":
            at["core"] ^= 1
        else:
            axis = step[at["core"]]
            at[axis] = at[axis] ^ 1 if step[2] == 0 else 3 - at[axis]
        pairs.append((i, flat_of(at)))
    return pairs


def probe_update(pg, probe):
    w, n = lax.axis_index("wide"), lax.axis_index("narrow")
    core, x, y = w % 2, w // 4, (n // 4) * 2 + (w // 2) % 2

    def bit(step):
        if step == "core":
            return core
        t = jnp.where(core == 0, {"x": x, "y": y}[step[0]], {"x": x, "y": y}[step[1]])
        high = t // 2
        return high ^ (t % 2) if step[2] == 0 else high

    steps = ["core", ("x", "y", 0), ("x", "y", 1), ("y", "x", 0), ("y", "x", 1)]
    v = pg
    block = jnp.zeros((), jnp.int32)
    for step in steps:
        half = v.shape[0] // 2
        b = bit(step)
        block = block * 2 + b
        give = lax.dynamic_slice_in_dim(v, (1 - b) * half, half, 0)
        keep = lax.dynamic_slice_in_dim(v, b * half, half, 0)
        v = keep + lax.ppermute(give, BOTH, route(step))
    for which in (0, 1):
        v = v + lax.ppermute(v, BOTH, route(("z", "z", which)))
    v = v[0]
    modes, _, size, _ = probe.shape
    mine = lax.dynamic_slice_in_dim(probe.reshape(2 * modes, size, size), block * 8, 8, 1)
    mine = mine - v[: 2 * modes] / (v[2 * modes] + step_floor)
    for step in reversed(steps):
        got = lax.ppermute(mine, BOTH, route(step))
        b = bit(step)
        mine = jnp.where(
            b == 0, jnp.concatenate([mine, got], 1), jnp.concatenate([got, mine], 1)
        )
    return mine.reshape(probe.shape)


def on_device(object_field, probe_modes, amplitudes, offsets, counts):
    h = probe_modes.shape[-1] // 2
    _, tr, tc = object_field.shape
    up = moved(object_field[:, tr - h :], "narrow", 1)
    down = moved(object_field[:, :h], "narrow", -1)
    left = moved(object_field[:, :, tc - h :], "wide", 1)
    right = moved(object_field[:, :, :h], "wide", -1)
    cup = moved(jnp.stack([left[:, tr - h :], right[:, tr - h :]]), "narrow", 1)
    cdown = moved(jnp.stack([left[:, :h], right[:, :h]]), "narrow", -1)
    core, left_g, right_g, up_g, down_g, cup_g, cdown_g, pg = tile_grads(
        counts[0], offsets[:, 0, 0], object_field, (left, right, up, down, cup, cdown),
        probe_modes, amplitudes[0, 0],
    )
    from_below = moved(up_g, "narrow", -1)
    from_above = moved(down_g, "narrow", 1)
    corner_below = moved(cup_g, "narrow", -1)
    corner_above = moved(cdown_g, "narrow", 1)
    sides = []
    for i, strip in enumerate((left_g, right_g)):
        strip = strip + jnp.pad(corner_above[i], ((0, 0), (0, tr - h), (0, 0)))
        strip = strip + jnp.pad(corner_below[i], ((0, 0), (tr - h, 0), (0, 0)))
        sides.append(strip)
    from_right = moved(sides[0], "wide", -1)
    from_left = moved(sides[1], "wide", 1)
    new_probe = probe_update(pg, probe_modes)
    new_object = object_update(object_field, core, from_left, from_right, from_above, from_below)
    return (new_object, new_probe)


def solution(mesh):
    return jax.shard_map(
        on_device,
        mesh=mesh,
        in_specs=(
            P(None, "narrow", "wide"),
            P(),
            P("narrow", "wide", None, None, None),
            P(None, "narrow", "wide", None),
            P("narrow", "wide"),
        ),
        out_specs=(P(None, "narrow", "wide"), P()),
        check_vma=False,
    )
```

time: 599 us -> 231 us (0.39)
  starting transfers between devices: 217 us -> 88.7 us
  waiting for transfers between devices: 194 us -> 80.1 us
  matrix products: 55.1 us -> 0 us
  local copies, waits for them, and re-layouts: 58.2 us -> 7.81 us
  Pallas kernels: 0 us -> 31.4 us
  other arithmetic: 45 us -> 20.3 us
  between operations: 14.2 us -> 1.65 us
  loops' own time: 9.84 us -> 0 us
    psum x1 -> x0, waiting for transfers between devices: 159 us -> none  [on_device(): probe_sum, power_sum = lax.psum((probe_sum, power_sum), ('wide', 'narrow'))]
    ppermute x8 -> x24, starting transfers between devices: 217 us -> 88.7 us  [the longest x12 45.1 us: moved(): return lax.ppermute(block, axis, route)]
    dot_general x16 -> x0, matrix products: 55.1 us -> none  [the longest x4 18 us: transform(): left_re = jnp.einsum('ux,mxy->muy', stacked, part_re, precision=highest)]
    ppermute x8 -> x24, waiting for transfers between devices: 34.9 us -> 80.1 us  [the longest x2 30 us: probe_update(): v = v + lax.ppermute(v, BOTH, route(('z', 'z', which)))]
    pallas_call x0 -> x1, Pallas kernels: none -> 31.4 us  [tile_grads(): pl.pallas_call(functools.partial(grads_kernel, modes=modes, n=n, tr=tr, t...]
    dynamic_update_slice x2 -> x0, local copies, waits for them, and re-layouts: 18.3 us -> none  [add_window(): return lax.dynamic_update_slice(totals, current + values, start)]
    slice x6 -> x2, local copies, waits for them, and re-layouts: 20.3 us -> 2.96 us  [the longest x1 1.68 us: on_device(): down = moved(object_field[:, :h], 'narrow', -1)]
    another operation x1 -> x0, loops' own time: 9.84 us -> none  [on_device(): lax.fori_loop(0, my_count, visit_own, (totals, probe_sum, power_sum))]
  transfers between devices with their start and end apart: 9 -> 24, of which waited for: 5 -> 10; matrix products, arithmetic and copies ran while one was open for 6% -> 9% of each run, Pallas kernels for 0% -> 0%
where the time goes in v1:
time: 231 us; the launch traced here: 230 us
  starting transfers between devices  88.7 us (38%)
  waiting for transfers between devices  80.1 us (35%)
  Pallas kernels  31.4 us (14%)
  other arithmetic  20.3 us (9%)
  local copies, waits for them, and re-layouts  7.81 us (3%)
    ppermute x12, starting transfers between devices, moved(): return lax.ppermute(block, axis, route)  45.1 us
    pallas_call x1, Pallas kernels, tile_grads(): pl.pallas_call(functools.partial(grads_kernel, modes=modes, n=n, tr=tr, t...  31.4 us
    ppermute x2, waiting for transfers between devices, probe_update(): v = v + lax.ppermute(v, BOTH, route(('z', 'z', which)))  30 us
    ppermute x5, starting transfers between devices, probe_update(): v = keep + lax.ppermute(give, BOTH, route(step))  24.2 us
    ppermute x12, waiting for transfers between devices, moved(): return lax.ppermute(block, axis, route)  21 us
    ppermute x5, waiting for transfers between devices, probe_update(): v = keep + lax.ppermute(give, BOTH, route(step))  17.4 us
    ppermute x5, starting transfers between devices, probe_update(): got = lax.ppermute(mine, BOTH, route(step))  16.4 us
    ppermute x5, waiting for transfers between devices, probe_update(): got = lax.ppermute(mine, BOTH, route(step))  11.8 us
  transfers between devices with their start and end apart: 24, of which 10 were waited for; matrix products, arithmetic and copies ran while one was open for 9% of the time, Pallas kernels for 0%

profile of v1, /device:TPU:1, one launch (start us, length us, event | category | flops | bytes accessed | tf_op | source)
XLA Modules:
  0.0 230.0 jit_solution(4521825436521651533)
XLA Ops:
  0.6 1.3 fusion.6
  1.9 3.3 %collective-permute-start.1 = (f32[2,512,128]{2,1,0:T(8,128)S(1)}, f32[2,512,128]{2,1,0:T(8,128)S(1)}, u32[]{:S(2)}, u32[]{:S(2)}) collective-permute-start(f32[2,512,128]{2,1,0:T(8,128)S(1)} %get-tuple-element.20), channel_id=1, source_target_pairs={{8,0},{16,8},{24,16},{32,24},{40,32},{48,40},{56,48},{64,56},{72,6... | collective-permute-start | bytes 1572872 | tf_op jit(solution)/shard_map/ppermute | solution.py:287
  5.2 3.2 %collective-permute-start = (f32[2,512,128]{2,1,0:T(8,128)S(1)}, f32[2,512,128]{2,1,0:T(8,128)S(1)}, u32[]{:S(2)}, u32[]{:S(2)}) collective-permute-start(f32[2,512,128]{2,1,0:T(8,128)S(1)} %get-tuple-element.21), channel_id=1, source_target_pairs={{0,8},{8,16},{16,24},{24,32},{32,40},{40,48},{48,56},{56,64},{64,7... | collective-permute-start | bytes 1572872 | tf_op jit(solution)/shard_map/ppermute | solution.py:287
  8.4 1.7 fusion.5
  10.1 1.3 collective-permute-start.3
  11.4 5.2 %collective-permute-start.2 = (f32[2,128,1024]{2,1,0:T(8,128)S(1)}, f32[2,128,1024]{2,1,0:T(8,128)}, u32[]{:S(2)}, u32[]{:S(2)}) collective-permute-start(f32[2,128,1024]{2,1,0:T(8,128)S(1)} %get-tuple-element.19), channel_id=1, source_target_pairs={{0,1},{1,2},{2,3},{3,4},{4,5},{5,6},{6,7},{8,9},{9,10},{10,11},{11... | collective-permute-start | bytes 3145736 | tf_op jit(solution)/shard_map/ppermute | solution.py:287
  16.7 0.0 collective-permute-done.1.right
  16.7 2.5 %collective-permute-done.left = f32[2,512,128]{2,1,0:T(8,128)S(1)} collective-permute-done((f32[2,512,128]{2,1,0:T(8,128)S(1)}, f32[2,512,128]{2,1,0:T(8,128)S(1)}, u32[]{:S(2)}, u32[]{:S(2)}) %collective-permute-start) | collective-permute-done | bytes 524320 | tf_op jit(solution)/shard_map/ppermute | solution.py:287
  19.2 0.8 copy-done.4
  20.0 3.6 %collective-permute-start.4 = (f32[2,2,128,128]{3,2,1,0:T(8,128)S(1)}, f32[2,2,128,128]{3,2,1,0:T(8,128)S(1)}, u32[]{:S(2)}, u32[]{:S(2)}) collective-permute-start(f32[2,2,128,128]{3,2,1,0:T(8,128)S(1)} %pad_maximum_fusion), channel_id=1, source_target_pairs={{0,1},{1,2},{2,3},{3,4},{4,5},{5,6},{6,7},{8,9},{9,10},{10,11},{11... | collective-permute-start | bytes 786440 | tf_op jit(solution)/shard_map/ppermute | solution.py:287
  23.6 1.3 collective-permute-start.5
  25.5 18.5 %collective-permute-done.4.cup = f32[2,2,128,128]{3,2,1,0:T(8,128)S(1)} collective-permute-done((f32[2,2,128,128]{3,2,1,0:T(8,128)S(1)}, f32[2,2,128,128]{3,2,1,0:T(8,128)S(1)}, u32[]{:S(2)}, u32[]{:S(2)}) %collective-permute-start.4) | collective-permute-done | bytes 262176 | tf_op jit(solution)/shard_map/ppermute | solution.py:287
  44.1 0.7 copy-done.5
  44.7 31.4 %tile_grads.1 = (f32[3,512,1024]{2,1,0:T(8,128)}, f32[3,512,128]{2,1,0:T(8,128)}, f32[3,512,128]{2,1,0:T(8,128)}, f32[3,128,1024]{2,1,0:T(8,128)}, f32[3,128,102...) custom-call(s32[1]{0:T(128)} %bitcast.35.count, ...), custom_call_target="tpu_custom_call" | custom-call | flops 40000000000 | bytes 30000000 | tf_op jit(solution)/shard_map/tile_grads/pallas_call | solution.py:248
  76.1 0.0 copy-start.1
  76.1 1.5 constant_dynamic-slice_fusion.4
  77.6 0.3 collective-permute-start.12
  77.9 2.8 %collective-permute-done.12 = f32[16,9,8,256]{3,2,1,0:T(8,128)} collective-permute-done((f32[16,9,8,256]{3,2,1,0:T(8,128)S(1)}, f32[16,9,8,256]{3,2,1,0:T(8,128)}, u32[]{:S(2)}, u32[]{:S(2)}) %collective-permute-start.12) | collective-permute-done | bytes 1179680 | tf_op jit(solution)/shard_map/ppermute | solution.py:334
  80.7 1.4 dynamic-slice_add_fusion
  82.2 0.5 collective-permute-start.13
  82.7 8.6 %collective-permute-done.13 = f32[8,9,8,256]{3,2,1,0:T(8,128)S(1)} collective-permute-done((f32[8,9,8,256]{3,2,1,0:T(8,128)S(1)}, f32[8,9,8,256]{3,2,1,0:T(8,128)S(1)}, u32[]{:S(2)}, u32[]{:S(2)}) %collective-permute-start.13) | collective-permute-done | bytes 589856 | tf_op jit(solution)/shard_map/ppermute | solution.py:334
  91.3 0.1 dynamic-slice_add_fusion.1
  91.4 9.4 %collective-permute-start.14 = (f32[4,9,8,256]{3,2,1,0:T(8,128)S(1)}, f32[4,9,8,256]{3,2,1,0:T(8,128)S(1)}, u32[]{:S(2)}, u32[]{:S(2)}) collective-permute-start(f32[4,9,8,256]{3,2,1,0:T(8,128)S(1)} %constant_dynamic-slice_fusion.2), channel_id=1, source_target_pairs={{0,96},{1,97},{2,98},{3,99},{4,100},{5,101},{6,102},{7,103},{8,28}... | collective-permute-start | bytes 884744 | tf_op jit(solution)/shard_map/ppermute | solution.py:334
  100.8 4.4 %collective-permute-done.14 = f32[4,9,8,256]{3,2,1,0:T(8,128)S(1)} collective-permute-done((f32[4,9,8,256]{3,2,1,0:T(8,128)S(1)}, f32[4,9,8,256]{3,2,1,0:T(8,128)S(1)}, u32[]{:S(2)}, u32[]{:S(2)}) %collective-permute-start.14) | collective-permute-done | bytes 294944 | tf_op jit(solution)/shard_map/ppermute | solution.py:334
  105.3 0.7 constant_dynamic-slice_fusion.1
  106.0 12.1 %collective-permute-start.15 = (f32[2,9,8,256]{3,2,1,0:T(8,128)}, f32[2,9,8,256]{3,2,1,0:T(8,128)}, u32[]{:S(2)}, u32[]{:S(2)}) collective-permute-start(f32[2,9,8,256]{3,2,1,0:T(8,128)} %constant_dynamic-slice_fusion.1), channel_id=1, source_target_pairs={{0,16},{1,17},{2,18},{3,19},{4,20},{5,21},{6,22},{7,23},{8,40},{9,... | collective-permute-start | bytes 442376 | tf_op jit(solution)/shard_map/ppermute | solution.py:334
  118.1 2.0 collective-permute-start.6
  120.1 1.3 collective-permute-start.7
  121.4 4.1 %collective-permute-start.10 = (f32[3,128,1024]{2,1,0:T(8,128)}, f32[3,128,1024]{2,1,0:T(8,128)S(1)}, u32[]{:S(2)}, u32[]{:S(2)}) collective-permute-start(f32[3,128,1024]{2,1,0:T(8,128)} %get-tuple-element.15), channel_id=1, source_target_pairs={{0,1},{1,2},{2,3},{3,4},{4,5},{5,6},{6,7},{8,9},{9,10},{10,11},{11... | collective-permute-start | bytes 4718600 | tf_op jit(solution)/shard_map/ppermute | solution.py:287
  125.5 1.3 collective-permute-start.11
  126.8 0.9 dynamic-slice_add_fusion.3
  127.8 1.8 collective-permute-start.16
  129.6 0.0 collective-permute-done.6
  129.6 1.0 slice_bitcast_fusion.3
  130.7 1.6 collective-permute-done.16
  132.3 2.2 collective-permute-start.17
  134.5 30.0 %collective-permute-done.17 = f32[1,9,8,256]{3,2,1,0:T(8,128)S(1)} collective-permute-done((f32[1,9,8,256]{3,2,1,0:T(8,128)S(1)}, f32[1,9,8,256]{3,2,1,0:T(8,128)S(1)}, u32[]{:S(2)}, u32[]{:S(2)}) %collective-permute-start.17) | collective-permute-done | bytes 73760 | tf_op jit(solution)/shard_map/ppermute | solution.py:336
  164.5 0.8 collective-permute-start.18
  165.3 2.1 pad_add_fusion.2
  167.4 16.6 %collective-permute-start.8 = (f32[3,512,128]{2,1,0:T(8,128)}, f32[3,512,128]{2,1,0:T(8,128)}, u32[]{:S(2)}, u32[]{:S(2)}) collective-permute-start(f32[3,512,128]{2,1,0:T(8,128)} %pad_add_fusion.2), channel_id=1, source_target_pairs={{0,8},{8,16},{16,24},{24,32},{32,40},{40,48},{48,56},{56,64},{64,7... | collective-permute-start | bytes 2359304 | tf_op jit(solution)/shard_map/ppermute | solution.py:287
  184.0 0.0 collective-permute-done.18
  184.0 0.9 fusion.3
  184.9 1.8 collective-permute-start.19
  186.7 0.9 pad_add_fusion.1
  187.7 1.9 collective-permute-start.9
  189.6 0.1 collective-permute-start.20
  189.7 5.4 %collective-permute-done.20 = f32[8,16,256]{2,1,0:T(8,128)} collective-permute-done((f32[8,16,256]{2,1,0:T(8,128)S(1)}, f32[8,16,256]{2,1,0:T(8,128)}, u32[]{:S(2)}, u32[]{:S(2)}) %collective-permute-start.20) | collective-permute-done | bytes 131104 | tf_op jit(solution)/shard_map/ppermute | solution.py:342
  195.1 1.0 maximum_select_fusion.6
  196.1 2.5 %collective-permute-start.21 = (f32[8,32,256]{2,1,0:T(8,128)S(1)}, f32[8,32,256]{2,1,0:T(8,128)}, u32[]{:S(2)}, u32[]{:S(2)}) collective-permute-start(f32[8,32,256]{2,1,0:T(8,128)S(1)} %maximum_select_fusion.6), channel_id=1, source_target_pairs={{0,96},{1,97},{2,98},{3,99},{4,100},{5,101},{6,102},{7,103},{8,28}... | collective-permute-start | bytes 786440 | tf_op jit(solution)/shard_map/ppermute | solution.py:342
  198.6 4.1 %collective-permute-done.21 = f32[8,32,256]{2,1,0:T(8,128)} collective-permute-done((f32[8,32,256]{2,1,0:T(8,128)S(1)}, f32[8,32,256]{2,1,0:T(8,128)}, u32[]{:S(2)}, u32[]{:S(2)}) %collective-permute-start.21) | collective-permute-done | bytes 262176 | tf_op jit(solution)/shard_map/ppermute | solution.py:342
  202.7 1.1 maximum_select_fusion.4
  203.8 1.4 collective-permute-start.22
  205.2 0.0 collective-permute-done.10
  205.2 4.3 %pad_add_fusion = f32[3,512,1024]{2,1,0:T(8,128)S(1)} fusion(f32[3,128,1024]{2,1,0:T(8,128)S(1)} %collective-permute-done.11, f32[3,128,1024]{2,1,0:T(8,128)S(1)} %collective-permute-done.10, f32[3,512,128]{2,1,0:T(8,128)} %collective-permute-done.9, f32[3,512,1024]{2,1,0:T(8,128)} %get-tuple-element.10, f32[3,512,128]{2,1,0:T(8,128)} %collective-permute-done.8), kind=kLoop, calls=%fused_computation | loop fusion | flops 6291456 | bytes 17301504 | tf_op jit(solution)/shard_map/add | solution.py:280
  209.5 0.0 copy-start
  209.5 0.3 fusion.1
  209.8 2.3 collective-permute-done.22
  212.1 0.1 maximum_select_fusion.2
  212.2 10.7 %collective-permute-start.23 = (f32[8,128,256]{2,1,0:T(8,128)S(1)}, f32[8,128,256]{2,1,0:T(8,128)S(1)}, u32[]{:S(2)}, u32[]{:S(2)}) collective-permute-start(f32[8,128,256]{2,1,0:T(8,128)S(1)} %maximum_select_fusion.2), channel_id=1, source_target_pairs={{0,8},{1,9},{2,10},{3,11},{4,12},{5,13},{6,14},{7,15},{8,0},{9,1},... | collective-permute-start | bytes 3145736 | tf_op jit(solution)/shard_map/ppermute | solution.py:342
  222.9 3.3 %fusion = f32[2,512,1024]{2,1,0:T(8,128)} fusion(f32[2,512,1024]{2,1,0:T(8,128)S(1)} %copy-done, f32[3,512,1024]{2,1,0:T(8,128)S(1)} %pad_add_fusion, f32[512,1024]{1,0:T(8,128)S(1)} %fusion.1), kind=kLoop, calls=%fused_computation.2 | loop fusion | flops 2097152 | bytes 14680064 | tf_op jit(solution)/shard_map/sub | solution.py:281
  226.1 1.0 maximum_select_fusion.5
  227.1 1.1 maximum_select_fusion.3
  228.2 0.1 maximum_select_fusion.1
  228.3 1.6 maximum_select_fusion
  (32 shorter events, 0.3 us)
Async XLA Ops:
  1.9 14.7 %collective-permute-start.1 = (f32[2,512,128]{2,1,0:T(8,128)S(1)}, f32[2,512,128]{2,1,0:T(8,128)S(1)}, u32[]{:S(2)}, u32[]{:S(2)}) collective-permute-start(f32[2,512,128]{2,1,0:T(8,128)S(1)} %get-tuple-element.20), channel_id=1, source_target_pairs={{8,0},{16,8},{24,16},{32,24},{40,32},{48,40},{56,48},{64,56},{72,6... | collective-permute-start | bytes 1572872 | tf_op jit(solution)/shard_map/ppermute | solution.py:287
  5.2 13.9 %collective-permute-start = (f32[2,512,128]{2,1,0:T(8,128)S(1)}, f32[2,512,128]{2,1,0:T(8,128)S(1)}, u32[]{:S(2)}, u32[]{:S(2)}) collective-permute-start(f32[2,512,128]{2,1,0:T(8,128)S(1)} %get-tuple-element.21), channel_id=1, source_target_pairs={{0,8},{8,16},{16,24},{24,32},{32,40},{40,48},{48,56},{56,64},{64,7... | collective-permute-start | bytes 1572872 | tf_op jit(solution)/shard_map/ppermute | solution.py:287
  10.1 33.9 %collective-permute-start.3 = (f32[2,128,1024]{2,1,0:T(8,128)S(1)}, f32[2,128,1024]{2,1,0:T(8,128)}, u32[]{:S(2)}, u32[]{:S(2)}) collective-permute-start(f32[2,128,1024]{2,1,0:T(8,128)S(1)} %get-tuple-element.18), channel_id=1, source_target_pairs={{1,0},{2,1},{3,2},{4,3},{5,4},{6,5},{7,6},{9,8},{10,9},{11,10},{12... | collective-permute-start | bytes 3145736 | tf_op jit(solution)/shard_map/ppermute | solution.py:287
  11.4 32.6 %collective-permute-start.2 = (f32[2,128,1024]{2,1,0:T(8,128)S(1)}, f32[2,128,1024]{2,1,0:T(8,128)}, u32[]{:S(2)}, u32[]{:S(2)}) collective-permute-start(f32[2,128,1024]{2,1,0:T(8,128)S(1)} %get-tuple-element.19), channel_id=1, source_target_pairs={{0,1},{1,2},{2,3},{3,4},{4,5},{5,6},{6,7},{8,9},{9,10},{10,11},{11... | collective-permute-start | bytes 3145736 | tf_op jit(solution)/shard_map/ppermute | solution.py:287
  16.7 27.4 %copy-start.3 = (f32[2,512,128]{2,1,0:T(8,128)}, f32[2,512,128]{2,1,0:T(8,128)S(1)}, u32[]{:S(2)}) copy-start(f32[2,512,128]{2,1,0:T(8,128)S(1)} %collective-permute-done.1.right) | copy-start | bytes 1572868
  19.1 0.8 copy-start.4
  20.0 24.1 %collective-permute-start.4 = (f32[2,2,128,128]{3,2,1,0:T(8,128)S(1)}, f32[2,2,128,128]{3,2,1,0:T(8,128)S(1)}, u32[]{:S(2)}, u32[]{:S(2)}) collective-permute-start(f32[2,2,128,128]{3,2,1,0:T(8,128)S(1)} %pad_maximum_fusion), channel_id=1, source_target_pairs={{0,1},{1,2},{2,3},{3,4},{4,5},{5,6},{6,7},{8,9},{9,10},{10,11},{11... | collective-permute-start | bytes 786440 | tf_op jit(solution)/shard_map/ppermute | solution.py:287
  23.6 20.5 %collective-permute-start.5 = (f32[2,2,128,128]{3,2,1,0:T(8,128)S(1)}, f32[2,2,128,128]{3,2,1,0:T(8,128)}, u32[]{:S(2)}, u32[]{:S(2)}) collective-permute-start(f32[2,2,128,128]{3,2,1,0:T(8,128)S(1)} %pad_maximum_fusion.1), channel_id=1, source_target_pairs={{1,0},{2,1},{3,2},{4,3},{5,4},{6,5},{7,6},{9,8},{10,9},{11,10},{12... | collective-permute-start | bytes 786440 | tf_op jit(solution)/shard_map/ppermute | solution.py:287
  44.0 0.7 copy-start.5
  76.1 4.6 %copy-start.1 = (f32[32,9,8,256]{3,2,1,0:T(8,128)S(1)}, f32[32,9,8,256]{3,2,1,0:T(8,128)}, u32[]{:S(2)}) copy-start(f32[32,9,8,256]{3,2,1,0:T(8,128)} %get-tuple-element.17) | copy-start | bytes 7077892
  77.6 3.1 %collective-permute-start.12 = (f32[16,9,8,256]{3,2,1,0:T(8,128)S(1)}, f32[16,9,8,256]{3,2,1,0:T(8,128)}, u32[]{:S(2)}, u32[]{:S(2)}) collective-permute-start(f32[16,9,8,256]{3,2,1,0:T(8,128)S(1)} %constant_dynamic-slice_fusion.4), channel_id=1, source_target_pairs={{0,8},{1,9},{2,10},{3,11},{4,12},{5,13},{6,14},{7,15},{8,0},{9,1},... | collective-permute-start | bytes 3538952 | tf_op jit(solution)/shard_map/ppermute | solution.py:334
  82.2 9.1 %collective-permute-start.13 = (f32[8,9,8,256]{3,2,1,0:T(8,128)S(1)}, f32[8,9,8,256]{3,2,1,0:T(8,128)S(1)}, u32[]{:S(2)}, u32[]{:S(2)}) collective-permute-start(f32[8,9,8,256]{3,2,1,0:T(8,128)S(1)} %constant_dynamic-slice_fusion.3), channel_id=1, source_target_pairs={{0,32},{1,33},{2,34},{3,35},{4,36},{5,37},{6,38},{7,39},{8,24},{9,... | collective-permute-start | bytes 1769480 | tf_op jit(solution)/shard_map/ppermute | solution.py:334
  91.4 13.8 %collective-permute-start.14 = (f32[4,9,8,256]{3,2,1,0:T(8,128)S(1)}, f32[4,9,8,256]{3,2,1,0:T(8,128)S(1)}, u32[]{:S(2)}, u32[]{:S(2)}) collective-permute-start(f32[4,9,8,256]{3,2,1,0:T(8,128)S(1)} %constant_dynamic-slice_fusion.2), channel_id=1, source_target_pairs={{0,96},{1,97},{2,98},{3,99},{4,100},{5,101},{6,102},{7,103},{8,28}... | collective-permute-start | bytes 884744 | tf_op jit(solution)/shard_map/ppermute | solution.py:334
  106.0 20.9 %collective-permute-start.15 = (f32[2,9,8,256]{3,2,1,0:T(8,128)}, f32[2,9,8,256]{3,2,1,0:T(8,128)}, u32[]{:S(2)}, u32[]{:S(2)}) collective-permute-start(f32[2,9,8,256]{3,2,1,0:T(8,128)} %constant_dynamic-slice_fusion.1), channel_id=1, source_target_pairs={{0,16},{1,17},{2,18},{3,19},{4,20},{5,21},{6,22},{7,23},{8,40},{9,... | collective-permute-start | bytes 442376 | tf_op jit(solution)/shard_map/ppermute | solution.py:334
  118.1 11.5 %collective-permute-start.6 = (f32[2,3,128,128]{3,2,1,0:T(8,128)}, f32[2,3,128,128]{3,2,1,0:T(8,128)}, u32[]{:S(2)}, u32[]{:S(2)}) collective-permute-start(f32[2,3,128,128]{3,2,1,0:T(8,128)} %get-tuple-element.12), channel_id=1, source_target_pairs={{0,1},{1,2},{2,3},{3,4},{4,5},{5,6},{6,7},{8,9},{9,10},{10,11},{11... | collective-permute-start | bytes 1179656 | tf_op jit(solution)/shard_map/ppermute | solution.py:287
  120.1 14.3 %collective-permute-start.7 = (f32[2,3,128,128]{3,2,1,0:T(8,128)}, f32[2,3,128,128]{3,2,1,0:T(8,128)S(1)}, u32[]{:S(2)}, u32[]{:S(2)}) collective-permute-start(f32[2,3,128,128]{3,2,1,0:T(8,128)} %get-tuple-element.13), channel_id=1, source_target_pairs={{1,0},{2,1},{3,2},{4,3},{5,4},{6,5},{7,6},{9,8},{10,9},{11,10},{12... | collective-permute-start | bytes 1179656 | tf_op jit(solution)/shard_map/ppermute | solution.py:287
  121.4 83.8 %collective-permute-start.10 = (f32[3,128,1024]{2,1,0:T(8,128)}, f32[3,128,1024]{2,1,0:T(8,128)S(1)}, u32[]{:S(2)}, u32[]{:S(2)}) collective-permute-start(f32[3,128,1024]{2,1,0:T(8,128)} %get-tuple-element.15), channel_id=1, source_target_pairs={{0,1},{1,2},{2,3},{3,4},{4,5},{5,6},{6,7},{8,9},{9,10},{10,11},{11... | collective-permute-start | bytes 4718600 | tf_op jit(solution)/shard_map/ppermute | solution.py:287
  125.5 79.7 %collective-permute-start.11 = (f32[3,128,1024]{2,1,0:T(8,128)}, f32[3,128,1024]{2,1,0:T(8,128)S(1)}, u32[]{:S(2)}, u32[]{:S(2)}) collective-permute-start(f32[3,128,1024]{2,1,0:T(8,128)} %get-tuple-element.16), channel_id=1, source_target_pairs={{1,0},{2,1},{3,2},{4,3},{5,4},{6,5},{7,6},{9,8},{10,9},{11,10},{12... | collective-permute-start | bytes 4718600 | tf_op jit(solution)/shard_map/ppermute | solution.py:287
  127.8 58.9 %copy-start.2 = (f32[3,512,128]{2,1,0:T(8,128)S(1)}, f32[3,512,128]{2,1,0:T(8,128)}, u32[]{:S(2)}) copy-start(f32[3,512,128]{2,1,0:T(8,128)} %get-tuple-element.14) | copy-start | bytes 2359300
  127.8 4.5 %collective-permute-start.16 = (f32[1,9,8,256]{3,2,1,0:T(8,128)S(1)}, f32[1,9,8,256]{3,2,1,0:T(8,128)S(1)}, u32[]{:S(2)}, u32[]{:S(2)}) collective-permute-start(f32[1,9,8,256]{3,2,1,0:T(8,128)S(1)} %constant_dynamic-slice_fusion), channel_id=1, source_target_pairs={{0,20},{1,21},{2,22},{3,23},{4,16},{5,17},{6,18},{7,19},{8,104},{9... | collective-permute-start | bytes 221192 | tf_op jit(solution)/shard_map/ppermute | solution.py:334
  132.3 32.1 %collective-permute-start.17 = (f32[1,9,8,256]{3,2,1,0:T(8,128)S(1)}, f32[1,9,8,256]{3,2,1,0:T(8,128)S(1)}, u32[]{:S(2)}, u32[]{:S(2)}) collective-permute-start(f32[1,9,8,256]{3,2,1,0:T(8,128)S(1)} %dynamic-slice_add_fusion.4), channel_id=1, source_target_pairs={{0,1},{1,0},{2,3},{3,2},{4,5},{5,4},{6,7},{7,6},{8,9},{9,8},{10,11... | collective-permute-start | bytes 221192 | tf_op jit(solution)/shard_map/ppermute | solution.py:336
  164.5 19.5 %collective-permute-start.18 = (f32[1,9,8,256]{3,2,1,0:T(8,128)S(1)}, f32[1,9,8,256]{3,2,1,0:T(8,128)S(1)}, u32[]{:S(2)}, u32[]{:S(2)}) collective-permute-start(f32[1,9,8,256]{3,2,1,0:T(8,128)S(1)} %add.185), channel_id=1, source_target_pairs={{0,3},{1,2},{2,1},{3,0},{4,7},{5,6},{6,5},{7,4},{8,11},{9,10},{10,... | collective-permute-start | bytes 221192 | tf_op jit(solution)/shard_map/ppermute | solution.py:336
  167.4 37.8 %collective-permute-start.8 = (f32[3,512,128]{2,1,0:T(8,128)}, f32[3,512,128]{2,1,0:T(8,128)}, u32[]{:S(2)}, u32[]{:S(2)}) collective-permute-start(f32[3,512,128]{2,1,0:T(8,128)} %pad_add_fusion.2), channel_id=1, source_target_pairs={{0,8},{8,16},{16,24},{24,32},{32,40},{40,48},{48,56},{56,64},{64,7... | collective-permute-start | bytes 2359304 | tf_op jit(solution)/shard_map/ppermute | solution.py:287
  184.9 4.7 %collective-permute-start.19 = (f32[8,8,256]{2,1,0:T(8,128)S(1)}, f32[8,8,256]{2,1,0:T(8,128)S(1)}, u32[]{:S(2)}, u32[]{:S(2)}) collective-permute-start(f32[8,8,256]{2,1,0:T(8,128)S(1)} %fusion.3), channel_id=1, source_target_pairs={{0,20},{1,21},{2,22},{3,23},{4,16},{5,17},{6,18},{7,19},{8,104},{9... | collective-permute-start | bytes 196616 | tf_op jit(solution)/shard_map/ppermute | solution.py:342
  187.7 17.5 %collective-permute-start.9 = (f32[3,512,128]{2,1,0:T(8,128)}, f32[3,512,128]{2,1,0:T(8,128)}, u32[]{:S(2)}, u32[]{:S(2)}) collective-permute-start(f32[3,512,128]{2,1,0:T(8,128)} %pad_add_fusion.1), channel_id=1, source_target_pairs={{8,0},{16,8},{24,16},{32,24},{40,32},{48,40},{56,48},{64,56},{72,6... | collective-permute-start | bytes 2359304 | tf_op jit(solution)/shard_map/ppermute | solution.py:287
  189.6 5.5 %collective-permute-start.20 = (f32[8,16,256]{2,1,0:T(8,128)S(1)}, f32[8,16,256]{2,1,0:T(8,128)}, u32[]{:S(2)}, u32[]{:S(2)}) collective-permute-start(f32[8,16,256]{2,1,0:T(8,128)S(1)} %maximum_select_fusion.7), channel_id=1, source_target_pairs={{0,16},{1,17},{2,18},{3,19},{4,20},{5,21},{6,22},{7,23},{8,40},{9,... | collective-permute-start | bytes 393224 | tf_op jit(solution)/shard_map/ppermute | solution.py:342
  196.1 6.6 %collective-permute-start.21 = (f32[8,32,256]{2,1,0:T(8,128)S(1)}, f32[8,32,256]{2,1,0:T(8,128)}, u32[]{:S(2)}, u32[]{:S(2)}) collective-permute-start(f32[8,32,256]{2,1,0:T(8,128)S(1)} %maximum_select_fusion.6), channel_id=1, source_target_pairs={{0,96},{1,97},{2,98},{3,99},{4,100},{5,101},{6,102},{7,103},{8,28}... | collective-permute-start | bytes 786440 | tf_op jit(solution)/shard_map/ppermute | solution.py:342
  203.8 8.3 %collective-permute-start.22 = (f32[8,64,256]{2,1,0:T(8,128)S(1)}, f32[8,64,256]{2,1,0:T(8,128)S(1)}, u32[]{:S(2)}, u32[]{:S(2)}) collective-permute-start(f32[8,64,256]{2,1,0:T(8,128)S(1)} %maximum_select_fusion.4), channel_id=1, source_target_pairs={{0,32},{1,33},{2,34},{3,35},{4,36},{5,37},{6,38},{7,39},{8,24},{9,... | collective-permute-start | bytes 1572872 | tf_op jit(solution)/shard_map/ppermute | solution.py:342
  209.5 13.3 %copy-start = (f32[2,512,1024]{2,1,0:T(8,128)S(1)}, f32[2,512,1024]{2,1,0:T(8,128)}, u32[]{:S(2)}) copy-start(f32[2,512,1024]{2,1,0:T(8,128)} %obj.1) | copy-start | bytes 12582916
  212.2 16.1 %collective-permute-start.23 = (f32[8,128,256]{2,1,0:T(8,128)S(1)}, f32[8,128,256]{2,1,0:T(8,128)S(1)}, u32[]{:S(2)}, u32[]{:S(2)}) collective-permute-start(f32[8,128,256]{2,1,0:T(8,128)S(1)} %maximum_select_fusion.2), channel_id=1, source_target_pairs={{0,8},{1,9},{2,10},{3,11},{4,12},{5,13},{6,14},{7,15},{8,0},{9,1},... | collective-permute-start | bytes 3145736 | tf_op jit(solution)/shard_map/ppermute | solution.py:342

commit v2 on v1

v2 whole, which is shorter than its diff:
```python
import functools

import jax
import jax.numpy as jnp
import numpy as np
from jax import lax
from jax.experimental import pallas as pl
from jax.experimental.pallas import tpu as pltpu
from jax.sharding import PartitionSpec as P

amp_floor = 0.25
step_floor = 1.0
F32 = jnp.float32
BF16 = jnp.bfloat16
BOTH = ("wide", "narrow")
MIB = 1024 * 1024


def tables(length):
    half = length // 2
    row = np.arange(half)[:, None]
    col = np.arange(half)[None, :]
    pairs = []
    for odd in (0, 1):
        angle = -2.0 * np.pi * (row * (2 * col + odd) % length) / length
        re = np.cos(angle) / np.sqrt(length)
        im = np.sin(angle) / np.sqrt(length)
        matrix = np.block([[re, im], [-im, re]]).astype(np.float32)
        for table in (matrix, matrix.T):
            high = table.astype(jnp.bfloat16)
            low = (table - high.astype(np.float32)).astype(jnp.bfloat16)
            pairs.append((high, low))
    m0, m0t, m1, m1t = pairs
    after = np.stack([np.concatenate([h, h, l], 0) for h, l in (m0, m1, m0t, m1t)])
    before = np.stack([np.concatenate([h, h, l], 1) for h, l in (m0t, m1t, m0, m1)])
    order = np.zeros((length, length), np.float32)
    for k in range(half):
        order[2 * k, k] = 1
        order[2 * k + 1, half + k] = 1
    order = np.concatenate([order, order], 0).astype(jnp.bfloat16)
    return jnp.asarray(after), jnp.asarray(before), jnp.asarray(order)


def split(x):
    high = x.astype(BF16)
    return high, (x - high.astype(F32)).astype(BF16)


def dot(a, b):
    return jnp.dot(a, b, preferred_element_type=F32)


def add_shifted(tot, comp, v, r0, r8, rr, q, rem):
    ch, n = v.shape
    h, nb = n // 2, ch // 8
    fwd_lanes = jnp.where(rem == h, 0, rem)
    fwd_rows = jnp.where(rr == 8, 0, rr)
    past = lax.broadcasted_iota(jnp.int32, (ch + 8, h), 1) >= rem
    below = lax.broadcasted_iota(jnp.int32, (nb + 1, 8, h), 1) >= rr

    def lowered(v):
        g = pltpu.roll(v.reshape(nb, 8, h), fwd_rows, axis=1)
        zero = jnp.zeros((1, 8, h), F32)
        here = jnp.concatenate([g, zero], axis=0)
        above = jnp.concatenate([zero, g], axis=0)
        return pltpu.roll(jnp.where(below, here, above).reshape(ch + 8, h), fwd_lanes, axis=1)

    t0, t1 = lowered(v[:, :h]), lowered(v[:, h:])
    zero = jnp.zeros_like(t0)
    full = [jnp.where(past, t0, zero), jnp.where(past, t1, t0), jnp.where(past, zero, t1)]
    tot[comp, pl.ds(r8 + r0, ch + 8), pl.ds(q, 3 * h)] += jnp.concatenate(full, axis=1)


def window_place(offs, s, rows, cols, n):
    h = n // 2
    r, c = offs[0, s], offs[1, s]
    q = jnp.minimum(c // h, (cols - 3 * h) // h)
    rem = c - q * h
    r8 = jnp.minimum(r // 8, (rows - n - 8) // 8)
    rr = r - r8 * 8
    return pl.multiple_of(r8 * 8, 8), rr, pl.multiple_of(q * h, h), rem


def copies(pairs, sems):
    return [pltpu.make_async_copy(a, b, sems.at[i]) for i, (a, b) in enumerate(pairs)]


def illum_kernel(info, probe, out, tot, one, *, modes, n, tr, tc, slots):
    h, ch = n // 2, 64
    tot[...] = jnp.zeros_like(tot)
    for r0 in range(0, n, ch):
        rs = pl.ds(r0, ch)
        acc = jnp.zeros((ch, n), F32)
        for k in range(modes):
            for c in range(2):
                v = probe[k, c, rs, :]
                acc = acc + v * v
        one[rs, :] = acc

    def visit(i, carry):
        t, s = i // slots, i % slots
        live = s < info[t, 0]
        r = jnp.where(live, info[t, 1 + s], 0) + (t // 3 - 1) * tr + h
        c = jnp.where(live, info[t, 1 + slots + s], 0) + (t % 3 - 1) * tc + h

        @pl.when(live & (r > 0) & (r < tr + n) & (c > 0) & (c < tc + n))
        def _():
            r8 = pl.multiple_of(r // 8 * 8, 8)
            q = pl.multiple_of(c // h * h, h)
            for r0 in range(0, n, ch):
                add_shifted(tot, 0, one[pl.ds(r0, ch), :], r0, r8, r - r8, q, c - q)

        return carry

    lax.fori_loop(0, 9 * slots, visit, 0)
    out[...] = tot[0, n : n + tr, n : n + tc] + step_floor


def tile_illum(info, probe, tr, tc, slots):
    modes, _, n, _ = probe.shape
    vmem = pl.BlockSpec(memory_space=pltpu.VMEM)
    smem = pl.BlockSpec(memory_space=pltpu.SMEM)
    return pl.pallas_call(
        functools.partial(illum_kernel, modes=modes, n=n, tr=tr, tc=tc, slots=slots),
        out_shape=jax.ShapeDtypeStruct((tr, tc), F32),
        in_specs=[smem, vmem],
        out_specs=vmem,
        scratch_shapes=[pltpu.VMEM((1, tr + 2 * n, tc + 2 * n), F32), pltpu.VMEM((n, n), F32)],
        compiler_params=pltpu.CompilerParams(vmem_limit_bytes=16 * MIB),
        cost_estimate=pl.CostEstimate(flops=20_000_000, bytes_accessed=8_000_000, transcendentals=0),
        name="tile_illum",
    )(info, probe)


def grads_kernel(
    count, offs, bit, obj, left, right, up, down, probe, amps, after, before, order,
    core_o, left_o, right_o, up_o, down_o, give_o, keep_o,
    ext, tot, pg, win, zs, zd, p0, p1, u, ap, sems, *, modes, n, tr, tc,
):
    h = n // 2
    ch = 64
    nb = ch // 8

    def places(big, core, left, right, up, down):
        rows = pl.ds(h, tr)
        return [
            (core, big.at[:, rows, pl.ds(h, tc)]),
            (left.at[:, pl.ds(0, tr), :], big.at[:, rows, pl.ds(0, h)]),
            (right.at[:, pl.ds(0, tr), :], big.at[:, rows, pl.ds(h + tc, h)]),
            (up.at[:, pl.ds(0, h), :], big.at[:, pl.ds(0, h), :]),
            (down.at[:, pl.ds(0, h), :], big.at[:, pl.ds(h + tr, h), :]),
        ]

    loads = copies(places(ext, obj, left, right, up, down), sems)
    for copy in loads:
        copy.start()
    tot[...] = jnp.zeros_like(tot)
    pg[...] = jnp.zeros_like(pg)
    for copy in loads:
        copy.wait()

    lane = lax.broadcasted_iota(jnp.int32, (ch + 8, h), 1)
    sub = lax.broadcasted_iota(jnp.int32, (nb, 8, h), 1)

    def after_dot(z, i):
        return dot(jnp.concatenate([z[...], z[:, :n]], axis=1), after[i])

    def before_dot(i, y):
        high, low = split(y)
        return dot(before[i], jnp.concatenate([high, low, high], axis=0))

    def slot(s, carry):
        r8, rr, q, rem = window_place(offs, s, tr + n, tc + n, n)
        back_lanes = jnp.where((rem == 0) | (rem == h), 0, h - rem)
        back_rows = jnp.where((rr == 0) | (rr == 8), 0, 8 - rr)
        for r0 in range(0, n, ch):
            rs = pl.ds(r0, ch)
            w = []
            for comp in range(2):
                blk = ext[comp, pl.ds(r8 + r0, ch + 8), pl.ds(q, 3 * h)]
                t = [pltpu.roll(blk[:, j * h : (j + 1) * h], back_lanes, axis=1) for j in range(3)]
                keep = lane < h - rem
                sides = []
                for x, y in ((t[0], t[1]), (t[1], t[2])):
                    g = jnp.where(keep, x, y).reshape(nb + 1, 8, h)
                    g = pltpu.roll(g, back_rows, axis=1)
                    sides.append(jnp.where(sub < 8 - rr, g[:-1], g[1:]).reshape(ch, h))
                v = jnp.concatenate(sides, axis=1)
                win[comp, rs, :] = v
                w.append(v)
            pg[pl.ds(r0 // 8, nb), 2 * modes] += (w[0] * w[0] + w[1] * w[1]).reshape(nb, 8, n)
        for k in range(modes):
            for r0 in range(0, n, ch):
                rs = pl.ds(r0, ch)
                ks = pl.ds(k * n + r0, ch)
                ar, ai = win[0, rs, :], win[1, rs, :]
                pr, pi = probe[k, 0, rs, :], probe[k, 1, rs, :]
                wr = pr * ar - pi * ai
                wi = pr * ai + pi * ar
                z = jnp.concatenate([wr[:, :h] + wr[:, h:], wi[:, :h] + wi[:, h:]], axis=1)
                zs[ks, :n], zs[ks, n:] = split(z)
                z = jnp.concatenate([wr[:, :h] - wr[:, h:], wi[:, :h] - wi[:, h:]], axis=1)
                zd[ks, :n], zd[ks, n:] = split(z)
        p0[...] = after_dot(zs, 0)
        p1[...] = after_dot(zd, 1)
        for k in range(modes):
            top, bot = pl.ds(k * n, h), pl.ds(k * n + h, h)

            def folded(sign):
                parts = []
                for ls in (slice(0, h), slice(h, n)):
                    parts.append(
                        jnp.concatenate([p[top, ls] + sign * p[bot, ls] for p in (p0, p1)], axis=1)
                    )
                return jnp.concatenate(parts, axis=0)

            u[k, 0] = before_dot(0, folded(1.0))
            u[k, 1] = before_dot(1, folded(-1.0))
        am = dot(jnp.concatenate(split(amps[s]), axis=1), order[...])
        ap[0] = am[:, :h]
        ap[1] = am[:, h:]
        factor = []
        for e in range(2):
            power = jnp.zeros((h, n), F32)
            for k in range(modes):
                a, b = u[k, e, :h, :], u[k, e, h:, :]
                power = power + (a * a + b * b)
            am = jnp.concatenate([ap[j, pl.ds(e, h, stride=2), :] for j in range(2)], axis=1)
            factor.append(1.0 - am * lax.rsqrt(power + amp_floor))
        for k in range(modes):
            y = [
                jnp.concatenate([u[k, e, :h, :] * factor[e], u[k, e, h:, :] * factor[e]], axis=0)
                for e in range(2)
            ]
            even, odd = before_dot(2, y[0]), before_dot(3, y[1])
            for half, v in ((0, even + odd), (1, even - odd)):
                ks = pl.ds(k * n + half * h, h)
                for ref, ls in ((zs, slice(0, h)), (zd, slice(h, n))):
                    z = jnp.concatenate([v[:h, ls], v[h:, ls]], axis=1)
                    ref[ks, :n], ref[ks, n:] = split(z)
        p0[...] = after_dot(zs, 2)
        p1[...] = after_dot(zd, 3)
        for r0 in range(0, n, ch):
            rs = pl.ds(r0, ch)
            bs = pl.ds(r0 // 8, nb)
            ar, ai = win[0, rs, :], win[1, rs, :]
            o_re = jnp.zeros((ch, n), F32)
            o_im = jnp.zeros((ch, n), F32)
            for k in range(modes):
                ks = pl.ds(k * n + r0, ch)
                e, o = p0[ks, :], p1[ks, :]
                lhs, rhs = e + o, e - o
                br = jnp.concatenate([lhs[:, :h], rhs[:, :h]], axis=1)
                bi = jnp.concatenate([lhs[:, h:], rhs[:, h:]], axis=1)
                pr, pi = probe[k, 0, rs, :], probe[k, 1, rs, :]
                o_re = o_re + (pr * br + pi * bi)
                o_im = o_im + (pr * bi - pi * br)
                pg[bs, 2 * k] += (ar * br + ai * bi).reshape(nb, 8, n)
                pg[bs, 2 * k + 1] += (ar * bi - ai * br).reshape(nb, 8, n)

            for comp, v in ((0, o_re), (1, o_im)):
                add_shifted(tot, comp, v, r0, r8, rr, q, rem)
        return carry

    lax.fori_loop(0, count[0], slot, 0)
    half = n // 16
    give, keep = pl.ds((1 - bit[0]) * half, half), pl.ds(bit[0] * half, half)
    outs = [(pg.at[give], give_o), (pg.at[keep], keep_o)]
    outs += [(b, a) for a, b in places(tot, core_o, left_o, right_o, up_o, down_o)]
    stores = copies(outs, sems)
    for copy in stores:
        copy.start()
    for copy in stores:
        copy.wait()


def tile_grads(count, offs, bit, obj, halos, probe, amps):
    modes, _, n, _ = probe.shape
    h = n // 2
    _, tr, tc = obj.shape
    vmem = pl.BlockSpec(memory_space=pltpu.VMEM)
    smem = pl.BlockSpec(memory_space=pltpu.SMEM)
    anyw = pl.BlockSpec(memory_space=pl.ANY)
    shape = lambda *dims: jax.ShapeDtypeStruct(dims, F32)
    rows, cols = tr + n, tc + n
    return pl.pallas_call(
        functools.partial(grads_kernel, modes=modes, n=n, tr=tr, tc=tc),
        out_shape=(
            shape(2, tr, tc), shape(2, tr, h), shape(2, tr, h), shape(2, h, cols), shape(2, h, cols),
            shape(n // 16, 2 * modes + 1, 8, n), shape(n // 16, 2 * modes + 1, 8, n),
        ),
        in_specs=[smem, smem, smem] + [anyw] * 5 + [vmem] * 5,
        out_specs=[anyw] * 7,
        scratch_shapes=[
            pltpu.VMEM((2, rows, cols), F32),
            pltpu.VMEM((2, rows, cols), F32),
            pltpu.VMEM((n // 8, 2 * modes + 1, 8, n), F32),
            pltpu.VMEM((2, n, n), F32),
            pltpu.VMEM((modes * n, 2 * n), BF16),
            pltpu.VMEM((modes * n, 2 * n), BF16),
            pltpu.VMEM((modes * n, n), F32),
            pltpu.VMEM((modes * n, n), F32),
            pltpu.VMEM((modes, 2, n, n), F32),
            pltpu.VMEM((2, n, h), F32),
            pltpu.SemaphoreType.DMA((7,)),
        ],
        compiler_params=pltpu.CompilerParams(vmem_limit_bytes=56 * MIB),
        cost_estimate=pl.CostEstimate(flops=40_000_000_000, bytes_accessed=30_000_000, transcendentals=0),
        name="tile_grads",
    )(count, offs, bit, obj, *halos, probe, amps, *tables(n))


def object_update(obj, core, illum, left, right, above, below):
    _, tr, tc = obj.shape
    h = left.shape[-1]
    total = core + jnp.pad(left, ((0, 0), (0, 0), (0, tc - h)))
    total = total + jnp.pad(right, ((0, 0), (0, 0), (tc - h, 0)))
    total = total + jnp.pad(above[:, :, h : h + tc], ((0, 0), (0, tr - h), (0, 0)))
    total = total + jnp.pad(below[:, :, h : h + tc], ((0, 0), (tr - h, 0), (0, 0)))
    return obj - total / illum


def moved(block, axis, distance):
    count = lax.axis_size(axis)
    route = [(i, i + distance) for i in range(count) if 0 <= i + distance < count]
    return lax.ppermute(block, axis, route)


def place(flat):
    w, n = flat // 8, flat % 8
    return {"core": w % 2, "x": w // 4, "y": (n // 4) * 2 + (w // 2) % 2, "z": n % 4}


def flat_of(at):
    w = at["x"] * 4 + (at["y"] % 2) * 2 + at["core"]
    n = (at["y"] // 2) * 4 + at["z"]
    return w * 8 + n


def route(axes, hop):
    pairs = []
    for i in range(128):
        at = place(i)
        axis = axes[at["core"]]
        at[axis] = (at[axis] + hop) % (2 if axis == "core" else 4)
        pairs.append((i, flat_of(at)))
    return pairs


def around(piece, axes):
    return [lax.ppermute(piece, BOTH, route(axes, hop)) for hop in (1, 2, 3)]


def own_core():
    return lax.axis_index("wide") & 1


def probe_update(give, keep, probe, arrived, ready):
    w, n = lax.axis_index("wide"), lax.axis_index("narrow")
    core, x, y = w & 1, w >> 2, ((n >> 2) << 1) | ((w >> 1) & 1)
    v = keep + lax.ppermute(give, BOTH, route(("core", "core"), 1))

    def scattered(v, t, axis):
        size = v.shape[0] // 4
        part = lambda d: lax.dynamic_slice_in_dim(v, (d & 3) * size, size, 0)
        got = [
            lax.ppermute(part(t + hop), BOTH, route((axis, axis), hop)) for hop in (1, 2, 3)
        ]
        return part(t) + got[0] + got[1] + got[2]

    v = scattered(v, x, "x")
    v, arrived = lax.optimization_barrier((v, arrived))
    v = scattered(v, y, "y")
    a, b, c = around(v, ("z", "z"))
    v = (v + a + b + c)[0]
    modes, _, size, _ = probe.shape
    block = core * 16 + x * 4 + y
    mine = lax.dynamic_slice_in_dim(probe.reshape(2 * modes, size, size), block * 8, 8, 1)
    mine = mine - v[: 2 * modes] / (v[2 * modes] + step_floor)

    def gathered(piece, t, axes):
        pieces = [piece, *around(piece, axes)]
        rows = []
        for d in range(4):
            j = (t - d) & 3
            one = jnp.where(j < 2, jnp.where(j == 0, *pieces[:2]), jnp.where(j == 2, *pieces[2:]))
            rows.append(one)
        return jnp.concatenate(rows, axis=1)

    mine, ready = lax.optimization_barrier((mine, ready))
    mine = gathered(mine, jnp.where(core == 0, y, x), ("y", "x"))
    mine = gathered(mine, jnp.where(core == 0, x, y), ("x", "y"))
    got = lax.ppermute(mine, BOTH, route(("core", "core"), 1))
    first = jnp.where(core == 0, mine, got)
    second = jnp.where(core == 0, got, mine)
    second = second.reshape(2 * modes, 4, 4, 8, size).swapaxes(1, 2).reshape(first.shape)
    return jnp.concatenate([first, second], axis=1).reshape(probe.shape), arrived, ready


def label(count, offs, width):
    info = jnp.concatenate([count, offs[0], offs[1]]).astype(F32)
    info = jnp.pad(info, (0, width - info.shape[0]))
    return jnp.broadcast_to(info, (2, 8, width))


def on_device(object_field, probe_modes, amplitudes, offsets, counts):
    h = probe_modes.shape[-1] // 2
    _, tr, tc = object_field.shape
    count, offs = counts[0], offsets[:, 0, 0]
    mine = label(count, offs, h)
    tagged = lambda cols: jnp.concatenate([object_field[:, :, cols], mine], axis=1)
    left = moved(tagged(slice(tc - h, tc)), "wide", 1)
    right = moved(tagged(slice(0, h)), "wide", -1)
    own = jnp.concatenate([object_field, label(count, offs, tc)], axis=1)

    def wider(rows):
        parts = [left, own, right]
        return jnp.concatenate(
            [jnp.concatenate([p[:, rows], p[:, tr:]], axis=1) for p in parts], axis=2
        )

    up = moved(wider(slice(tr - h, tr)), "narrow", 1)
    down = moved(wider(slice(0, h)), "narrow", -1)
    pick = lambda a, row, col: a[0, row, col : col + 16]
    info = [pick(up, h, c) for c in (0, h, h + tc)]
    info += [pick(left, tr, 0), pick(own, tr, 0), pick(right, tr, 0)]
    info += [pick(down, h, c) for c in (0, h, h + tc)]
    info = jnp.stack(info).astype(jnp.int32)
    illum = tile_illum(info, probe_modes, tr, tc, offs.shape[-1])
    core, left_g, right_g, up_g, down_g, give, keep = tile_grads(
        count, offs, own_core()[None], object_field, (left, right, up, down),
        probe_modes, amplitudes[0, 0],
    )
    below = moved(up_g, "narrow", -1)
    above = moved(down_g, "narrow", 1)
    new_probe, (above, below), illum = probe_update(give, keep, probe_modes, (above, below), illum)
    side = lambda strip, cols: (
        strip
        + jnp.pad(above[:, :, cols], ((0, 0), (0, tr - h), (0, 0)))
        + jnp.pad(below[:, :, cols], ((0, 0), (tr - h, 0), (0, 0)))
    )
    from_right = moved(side(left_g, slice(0, h)), "wide", -1)
    from_left = moved(side(right_g, slice(h + tc, 2 * h + tc)), "wide", 1)
    new_object = object_update(object_field, core, illum, from_left, from_right, above, below)
    return (new_object, new_probe)


def solution(mesh):
    return jax.shard_map(
        on_device,
        mesh=mesh,
        in_specs=(
            P(None, "narrow", "wide"),
            P(),
            P("narrow", "wide", None, None, None),
            P(None, "narrow", "wide", None),
            P("narrow", "wide"),
        ),
        out_specs=(P(None, "narrow", "wide"), P()),
        check_vma=False,
    )
```

time: 231 us -> 200 us (0.87)
  starting transfers between devices: 88.7 us -> 61.8 us
  Pallas kernels: 31.4 us -> 43.8 us
  other arithmetic: 20.3 us -> 9.25 us
  waiting for transfers between devices: 80.1 us -> 69.5 us
  local copies, waits for them, and re-layouts: 7.81 us -> 13.6 us
    ppermute x12 -> x17, waiting for transfers between devices: 59.1 us -> 17.6 us  [the longest x6 15.4 us: scattered(): lax.ppermute(part(t + hop), BOTH, route((axis, axis), hop))]
    ppermute x12 -> x8, waiting for transfers between devices: 21 us -> 51.9 us  [moved(): return lax.ppermute(block, axis, route)]
    ppermute x12 -> x8, starting transfers between devices: 45.1 us -> 27.7 us  [moved(): return lax.ppermute(block, axis, route)]
    ppermute x12 -> x17, starting transfers between devices: 43.6 us -> 34.1 us  [the longest x9 18.9 us: around(): return [lax.ppermute(piece, BOTH, route(axes, hop)) for hop in (1, 2, 3)]]
    another operation x2 -> x6, local copies, waits for them, and re-layouts: 0.04 us -> 7.88 us  [on_device(): info = jnp.stack(info).astype(jnp.int32)]
    pallas_call x1, Pallas kernels: 31.4 us -> 39 us  [tile_grads(): pl.pallas_call(functools.partial(grads_kernel, modes=modes, n=n, tr=tr, t...]
    add x10 -> x6, other arithmetic: 9.85 us -> 2.62 us  [the longest x1 1.42 us: probe_update(): v = keep + lax.ppermute(give, BOTH, route(('core', 'core'), 1))]
    select_n x8 -> x4, other arithmetic: 6.02 us -> 0.39 us  [the longest x3 0.21 us: gathered(): jnp.where(j < 2, jnp.where(j == 0, *pieces[:2]), jnp.where(j == 2, *piece...]
  transfers between devices with their start and end apart: 24 -> 25, of which waited for: 10 -> 12; matrix products, arithmetic and copies ran while one was open for 9% -> 8% of each run, Pallas kernels for 0% -> 2%
where the time goes in v2:
time: 200 us
  waiting for transfers between devices  69.5 us (35%)
  starting transfers between devices  61.8 us (31%)
  Pallas kernels  43.8 us (22%)
  local copies, waits for them, and re-layouts  13.6 us (7%)
  other arithmetic  9.25 us (5%)
    ppermute x8, waiting for transfers between devices, moved(): return lax.ppermute(block, axis, route)  51.9 us
    pallas_call x1, Pallas kernels, tile_grads(): pl.pallas_call(functools.partial(grads_kernel, modes=modes, n=n, tr=tr, t...  39 us
    ppermute x8, starting transfers between devices, moved(): return lax.ppermute(block, axis, route)  27.7 us
    ppermute x9, starting transfers between devices, around(): return [lax.ppermute(piece, BOTH, route(axes, hop)) for hop in (1, 2, 3)]  18.9 us
    ppermute x6, waiting for transfers between devices, scattered(): lax.ppermute(part(t + hop), BOTH, route((axis, axis), hop))  15.4 us
    ppermute x6, starting transfers between devices, scattered(): lax.ppermute(part(t + hop), BOTH, route((axis, axis), hop))  12.9 us
    another operation x6, local copies, waits for them, and re-layouts, on_device(): info = jnp.stack(info).astype(jnp.int32)  7.88 us
    pallas_call x1, Pallas kernels, tile_illum(): pl.pallas_call(functools.partial(illum_kernel, modes=modes, n=n, tr=tr, t...  4.71 us
  transfers between devices with their start and end apart: 25, of which 12 were waited for; matrix products, arithmetic and copies ran while one was open for 8% of the time, Pallas kernels for 2%

profile of v2, /device:TPU:1, one launch (start us, length us, event | category | flops | bytes accessed | tf_op | source)
XLA Modules:
  0.0 199.7 jit_solution(10581634683830227033)
XLA Ops:
  1.3 0.7 slice_bitcast_fusion.10
  2.0 1.4 fusion.5
  3.4 0.1 add_convert_fusion
  3.5 0.1 pad_maximum_fusion.3
  3.6 3.3 %collective-permute-start.1 = (f32[2,520,128]{2,1,0:T(8,128)S(1)}, f32[2,520,128]{2,1,0:T(8,128)S(1)}, u32[]{:S(2)}, u32[]{:S(2)}) collective-permute-start(f32[2,520,128]{2,1,0:T(8,128)S(1)} %get-tuple-element.58), channel_id=1, source_target_pairs={{8,0},{16,8},{24,16},{32,24},{40,32},{48,40},{56,48},{64,56},{72,6... | collective-permute-start | bytes 1597448 | tf_op jit(solution)/shard_map/ppermute | solution.py:326
  6.9 3.2 %collective-permute-start = (f32[2,520,128]{2,1,0:T(8,128)S(1)}, f32[2,520,128]{2,1,0:T(8,128)S(1)}, u32[]{:S(2)}, u32[]{:S(2)}) collective-permute-start(f32[2,520,128]{2,1,0:T(8,128)S(1)} %get-tuple-element.59), channel_id=1, source_target_pairs={{0,8},{8,16},{16,24},{24,32},{32,40},{40,48},{48,56},{56,64},{64,7... | collective-permute-start | bytes 1597448 | tf_op jit(solution)/shard_map/ppermute | solution.py:326
  10.2 0.1 fusion.4
  10.3 4.8 %collective-permute-done.1.right = f32[2,520,128]{2,1,0:T(8,128)S(1)} collective-permute-done((f32[2,520,128]{2,1,0:T(8,128)S(1)}, f32[2,520,128]{2,1,0:T(8,128)S(1)}, u32[]{:S(2)}, u32[]{:S(2)}) %collective-permute-start.1) | collective-permute-done | bytes 532512 | tf_op jit(solution)/shard_map/ppermute | solution.py:326
  15.1 5.9 %collective-permute-done.left = f32[2,520,128]{2,1,0:T(8,128)S(1)} collective-permute-done((f32[2,520,128]{2,1,0:T(8,128)S(1)}, f32[2,520,128]{2,1,0:T(8,128)S(1)}, u32[]{:S(2)}, u32[]{:S(2)}) %collective-permute-start) | collective-permute-done | bytes 532512 | tf_op jit(solution)/shard_map/ppermute | solution.py:326
  21.0 0.3 maximum_maximum_fusion
  21.3 0.5 copy-done.7
  21.8 4.6 %collective-permute-start.2 = (f32[2,136,1280]{2,1,0:T(8,128)S(1)}, f32[2,136,1280]{2,1,0:T(8,128)}, u32[]{:S(2)}, u32[]{:S(2)}) collective-permute-start(f32[2,136,1280]{2,1,0:T(8,128)S(1)} %get-tuple-element.50), channel_id=1, source_target_pairs={{0,1},{1,2},{2,3},{3,4},{4,5},{5,6},{6,7},{8,9},{9,10},{10,11},{11... | collective-permute-start | bytes 4177928 | tf_op jit(solution)/shard_map/ppermute | solution.py:326
  26.4 1.3 collective-permute-start.3
  27.7 18.4 %collective-permute-done.2.up = f32[2,136,1280]{2,1,0:T(8,128)} collective-permute-done((f32[2,136,1280]{2,1,0:T(8,128)S(1)}, f32[2,136,1280]{2,1,0:T(8,128)}, u32[]{:S(2)}, u32[]{:S(2)}) %collective-permute-start.2) | collective-permute-done | bytes 1392672 | tf_op jit(solution)/shard_map/ppermute | solution.py:326
  46.1 5.3 %collective-permute-done.3.down = f32[2,136,1280]{2,1,0:T(8,128)} collective-permute-done((f32[2,136,1280]{2,1,0:T(8,128)S(1)}, f32[2,136,1280]{2,1,0:T(8,128)}, u32[]{:S(2)}, u32[]{:S(2)}) %collective-permute-start.3) | collective-permute-done | bytes 1392672 | tf_op jit(solution)/shard_map/ppermute | solution.py:326
  51.4 39.0 %tile_grads.1 = (f32[2,512,1024]{2,1,0:T(8,128)}, f32[2,512,128]{2,1,0:T(8,128)}, f32[2,512,128]{2,1,0:T(8,128)}, f32[2,128,1280]{2,1,0:T(8,128)}, f32[2,128,128...) custom-call(s32[1]{0:T(128)} %bitcast.41.count, s32[2,6]{1,0:T(2,128)} %bitcast.46, ...), custom_call_target="tpu_custom_call" | custom-call | flops 40000000000 | bytes 30000000 | tf_op jit(solution)/shard_map/tile_grads/pallas_call | solution.py:286
  90.5 0.1 collective-permute-start.4
  90.5 1.4 collective-permute-start.8
  91.9 1.3 collective-permute-start.9
  93.3 0.5 fusion.3
  93.8 1.4 add.144
  95.3 2.2 %collective-permute-start.7 = (f32[4,9,8,256]{3,2,1,0:T(8,128)S(1)}, f32[4,9,8,256]{3,2,1,0:T(8,128)S(1)}, u32[]{:S(2)}, u32[]{:S(2)}) collective-permute-start(f32[4,9,8,256]{3,2,1,0:T(8,128)S(1)} %get-tuple-element.43), channel_id=1, source_target_pairs={{0,96},{1,97},{2,98},{3,99},{4,100},{5,101},{6,102},{7,103},{8,104... | collective-permute-start | bytes 884744 | tf_op jit(solution)/shard_map/ppermute | solution.py:367
  97.5 0.7 collective-permute-start.5
  98.2 1.2 slice_bitcast_fusion.5
  99.3 1.2 slice_bitcast_fusion.4
  100.6 9.5 %collective-permute-done.7 = f32[4,9,8,256]{3,2,1,0:T(8,128)S(1)} collective-permute-done((f32[4,9,8,256]{3,2,1,0:T(8,128)S(1)}, f32[4,9,8,256]{3,2,1,0:T(8,128)S(1)}, u32[]{:S(2)}, u32[]{:S(2)}) %collective-permute-start.7) | collective-permute-done | bytes 294944 | tf_op jit(solution)/shard_map/ppermute | solution.py:367
  110.1 3.5 %collective-permute-done.5 = f32[4,9,8,256]{3,2,1,0:T(8,128)S(1)} collective-permute-done((f32[4,9,8,256]{3,2,1,0:T(8,128)S(1)}, f32[4,9,8,256]{3,2,1,0:T(8,128)S(1)}, u32[]{:S(2)}, u32[]{:S(2)}) %collective-permute-start.5) | collective-permute-done | bytes 294944 | tf_op jit(solution)/shard_map/ppermute | solution.py:367
  113.6 0.1 add_add_fusion
  113.7 6.4 %collective-permute-done.8 = f32[2,128,1280]{2,1,0:T(8,128)S(1)} collective-permute-done((f32[2,128,1280]{2,1,0:T(8,128)}, f32[2,128,1280]{2,1,0:T(8,128)S(1)}, u32[]{:S(2)}, u32[]{:S(2)}) %collective-permute-start.8) | collective-permute-done | bytes 1310752 | tf_op jit(solution)/shard_map/ppermute | solution.py:326
  120.1 3.9 %collective-permute-done.9 = f32[2,128,1280]{2,1,0:T(8,128)} collective-permute-done((f32[2,128,1280]{2,1,0:T(8,128)}, f32[2,128,1280]{2,1,0:T(8,128)}, u32[]{:S(2)}, u32[]{:S(2)}) %collective-permute-start.9) | collective-permute-done | bytes 1310752 | tf_op jit(solution)/shard_map/ppermute | solution.py:326
  124.0 4.2 %collective-permute-start.14 = (f32[1,9,8,256]{3,2,1,0:T(8,128)S(1)}, f32[1,9,8,256]{3,2,1,0:T(8,128)S(1)}, u32[]{:S(2)}, u32[]{:S(2)}) collective-permute-start(f32[1,9,8,256]{3,2,1,0:T(8,128)S(1)} %get-tuple-element.52), channel_id=1, source_target_pairs={{0,20},{1,21},{2,22},{3,23},{4,16},{5,17},{6,18},{7,19},{8,28},{9,... | collective-permute-start | bytes 221192 | tf_op jit(solution)/shard_map/ppermute | solution.py:367
  128.2 5.1 %collective-permute-start.13 = (f32[1,9,8,256]{3,2,1,0:T(8,128)S(1)}, f32[1,9,8,256]{3,2,1,0:T(8,128)S(1)}, u32[]{:S(2)}, u32[]{:S(2)}) collective-permute-start(f32[1,9,8,256]{3,2,1,0:T(8,128)S(1)} %get-tuple-element.53), channel_id=1, source_target_pairs={{0,4},{1,5},{2,6},{3,7},{4,0},{5,1},{6,2},{7,3},{8,12},{9,13},{10,... | collective-permute-start | bytes 221192 | tf_op jit(solution)/shard_map/ppermute | solution.py:367
  133.3 0.8 collective-permute-start.12
  134.1 1.3 slice_bitcast_fusion.6
  135.4 2.4 %collective-permute-done.12 = f32[1,9,8,256]{3,2,1,0:T(8,128)S(1)} collective-permute-done((f32[1,9,8,256]{3,2,1,0:T(8,128)S(1)}, f32[1,9,8,256]{3,2,1,0:T(8,128)S(1)}, u32[]{:S(2)}, u32[]{:S(2)}) %collective-permute-start.12) | collective-permute-done | bytes 73760 | tf_op jit(solution)/shard_map/ppermute | solution.py:367
  137.8 2.4 %collective-permute-start.17 = (f32[1,9,8,256]{3,2,1,0:T(8,128)S(1)}, f32[1,9,8,256]{3,2,1,0:T(8,128)S(1)}, u32[]{:S(2)}, u32[]{:S(2)}) collective-permute-start(f32[1,9,8,256]{3,2,1,0:T(8,128)S(1)} %add_add_fusion.2), channel_id=1, source_target_pairs={{0,3},{1,0},{2,1},{3,2},{4,7},{5,4},{6,5},{7,6},{8,11},{9,8},{10,9... | collective-permute-start | bytes 221192 | tf_op jit(solution)/shard_map/ppermute | solution.py:351
  140.2 0.7 collective-permute-start.15
  140.9 1.2 slice_bitcast_fusion.1
  142.1 2.5 %stack.3 = f32[9,16]{1,0:T(8,128)} concatenate(f32[1,16]{1,0:T(1,128)} %get-tuple-element.37, f32[1,16]{1,0:T(1,128)} %get-tuple-element.36, f32[1,16]{1,0:T(1,128)} %get-tuple-element.35, f32[1,16]{1,0:T(1,128)} %slice_bitcast_fusion.5, f32[1,16]{1,0:T(1,128)} %fusion.3, f32[1,16]{1,0:T(1,128)} %slice_bitcast_fusion.4, f32[1,16]{1,0:T(1,128)} %get-tuple-element.34, ...), dimensions={0} | concatenate | bytes 1152 | tf_op jit(solution)/shard_map/stack | solution.py:428
  144.6 0.7 convert_element_type.26.info
  145.3 4.7 %tile_illum.1 = f32[512,1024]{1,0:T(8,128)S(1)} custom-call(s32[9,16]{1,0:T(8,128)S(1)} %convert_element_type.26.info, f32[4,2,256,256]{3,2,1,0:T(8,128)S(1)} %copy-done), custom_call_target="tpu_custom_call" | custom-call | flops 20000000 | bytes 8000000 | tf_op jit(solution)/shard_map/tile_illum/pallas_call | solution.py:123
  150.1 1.0 add_add_fusion.1
  151.1 10.4 %collective-permute-start.19 = (f32[8,8,256]{2,1,0:T(8,128)S(1)}, f32[8,8,256]{2,1,0:T(8,128)S(1)}, u32[]{:S(2)}, u32[]{:S(2)}) collective-permute-start(f32[8,8,256]{2,1,0:T(8,128)S(1)} %fusion.1), channel_id=1, source_target_pairs={{0,4},{1,5},{2,6},{3,7},{4,0},{5,1},{6,2},{7,3},{8,72},{9,73},{10,... | collective-permute-start | bytes 196616 | tf_op jit(solution)/shard_map/ppermute | solution.py:351
  161.5 0.4 collective-permute-start.20
  161.9 1.1 collective-permute-start.18
  163.0 1.0 fusion.6
  164.0 0.6 collective-permute-done.20
  164.6 1.6 collective-permute-done.18
  166.3 1.9 collective-permute-start.22
  168.2 1.4 collective-permute-start.23
  169.6 0.5 collective-permute-start.21
  170.2 10.7 %collective-permute-start.11 = (f32[2,512,128]{2,1,0:T(8,128)S(1)}, f32[2,512,128]{2,1,0:T(8,128)S(1)}, u32[]{:S(2)}, u32[]{:S(2)}) collective-permute-start(f32[2,512,128]{2,1,0:T(8,128)S(1)} %pad_add_fusion), channel_id=1, source_target_pairs={{8,0},{16,8},{24,16},{32,24},{40,32},{48,40},{56,48},{64,56},{72,6... | collective-permute-start | bytes 1572872 | tf_op jit(solution)/shard_map/ppermute | solution.py:326
  180.9 1.9 collective-permute-start.10
  182.9 0.1 select_select_fusion.3
  183.0 0.1 select_select_fusion.2
  183.1 0.1 pad_maximum_fusion.2
  183.2 2.2 %collective-permute-start.24 = (f32[8,128,256]{2,1,0:T(8,128)S(1)}, f32[8,128,256]{2,1,0:T(8,128)S(1)}, u32[]{:S(2)}, u32[]{:S(2)}) collective-permute-start(f32[8,128,256]{2,1,0:T(8,128)S(1)} %pad_maximum_fusion.2), channel_id=1, source_target_pairs={{0,8},{1,9},{2,10},{3,11},{4,12},{5,13},{6,14},{7,15},{8,0},{9,1},... | collective-permute-start | bytes 3145736 | tf_op jit(solution)/shard_map/ppermute | solution.py:393
  185.4 1.4 slice.111
  186.9 0.1 slice.110
  187.0 7.4 %collective-permute-done.10 = f32[2,512,128]{2,1,0:T(8,128)S(1)} collective-permute-done((f32[2,512,128]{2,1,0:T(8,128)S(1)}, f32[2,512,128]{2,1,0:T(8,128)S(1)}, u32[]{:S(2)}, u32[]{:S(2)}) %collective-permute-start.10) | collective-permute-done | bytes 524320 | tf_op jit(solution)/shard_map/ppermute | solution.py:326
  194.3 3.5 %divide_subtract_fusion = f32[2,512,1024]{2,1,0:T(8,128)} fusion(f32[2,512,1024]{2,1,0:T(8,128)S(1)} %copy-done.2, f32[2,128,1024]{2,1,0:T(8,128)S(1)} %slice.111, f32[2,128,1024]{2,1,0:T(8,128)S(1)} %slice.110, f32[2,512,128]{2,1,0:T(8,128)S(1)} %collective-permute-done.11, f32[2,512,1024]{2,1,0:T(8,128)S(1)} %copy-done.3, ...), kind=kLoop, calls=%fused_computation | loop fusion | flops 6291456 | bytes 17825792 | tf_op jit(solution)/shard_map/sub | solution.py:320
  197.8 0.2 broadcast_select_fusion.1
  198.0 0.1 copy.10
  198.1 1.5 pad_maximum_fusion
  (50 shorter events, 0.5 us)
Async XLA Ops:
  2.0 8.2 %copy-start.1 = (f32[2,512,1024]{2,1,0:T(8,128)S(1)}, f32[2,512,1024]{2,1,0:T(8,128)}, u32[]{:S(2)}) copy-start(f32[2,512,1024]{2,1,0:T(8,128)} %obj.1) | copy-start | bytes 12582916
  3.6 11.5 %collective-permute-start.1 = (f32[2,520,128]{2,1,0:T(8,128)S(1)}, f32[2,520,128]{2,1,0:T(8,128)S(1)}, u32[]{:S(2)}, u32[]{:S(2)}) collective-permute-start(f32[2,520,128]{2,1,0:T(8,128)S(1)} %get-tuple-element.58), channel_id=1, source_target_pairs={{8,0},{16,8},{24,16},{32,24},{40,32},{48,40},{56,48},{64,56},{72,6... | collective-permute-start | bytes 1597448 | tf_op jit(solution)/shard_map/ppermute | solution.py:326
  6.9 14.1 %collective-permute-start = (f32[2,520,128]{2,1,0:T(8,128)S(1)}, f32[2,520,128]{2,1,0:T(8,128)S(1)}, u32[]{:S(2)}, u32[]{:S(2)}) collective-permute-start(f32[2,520,128]{2,1,0:T(8,128)S(1)} %get-tuple-element.59), channel_id=1, source_target_pairs={{0,8},{8,16},{16,24},{24,32},{32,40},{40,48},{48,56},{56,64},{64,7... | collective-permute-start | bytes 1597448 | tf_op jit(solution)/shard_map/ppermute | solution.py:326
  15.1 6.2 %copy-start.6 = (f32[2,520,128]{2,1,0:T(8,128)}, f32[2,520,128]{2,1,0:T(8,128)S(1)}, u32[]{:S(2)}) copy-start(f32[2,520,128]{2,1,0:T(8,128)S(1)} %collective-permute-done.1.right) | copy-start | bytes 1597444
  21.0 0.8 copy-start.7
  21.8 24.3 %collective-permute-start.2 = (f32[2,136,1280]{2,1,0:T(8,128)S(1)}, f32[2,136,1280]{2,1,0:T(8,128)}, u32[]{:S(2)}, u32[]{:S(2)}) collective-permute-start(f32[2,136,1280]{2,1,0:T(8,128)S(1)} %get-tuple-element.50), channel_id=1, source_target_pairs={{0,1},{1,2},{2,3},{3,4},{4,5},{5,6},{6,7},{8,9},{9,10},{10,11},{11... | collective-permute-start | bytes 4177928 | tf_op jit(solution)/shard_map/ppermute | solution.py:326
  26.4 24.9 %collective-permute-start.3 = (f32[2,136,1280]{2,1,0:T(8,128)S(1)}, f32[2,136,1280]{2,1,0:T(8,128)}, u32[]{:S(2)}, u32[]{:S(2)}) collective-permute-start(f32[2,136,1280]{2,1,0:T(8,128)S(1)} %get-tuple-element.49), channel_id=1, source_target_pairs={{1,0},{2,1},{3,2},{4,3},{5,4},{6,5},{7,6},{9,8},{10,9},{11,10},{12... | collective-permute-start | bytes 4177928 | tf_op jit(solution)/shard_map/ppermute | solution.py:326
  90.5 3.4 %collective-permute-start.4 = (f32[16,9,8,256]{3,2,1,0:T(8,128)}, f32[16,9,8,256]{3,2,1,0:T(8,128)S(1)}, u32[]{:S(2)}, u32[]{:S(2)}) collective-permute-start(f32[16,9,8,256]{3,2,1,0:T(8,128)} %get-tuple-element.17), channel_id=1, source_target_pairs={{0,8},{1,9},{2,10},{3,11},{4,12},{5,13},{6,14},{7,15},{8,0},{9,1},... | collective-permute-start | bytes 3538952 | tf_op jit(solution)/shard_map/ppermute | solution.py:361
  90.5 29.6 %collective-permute-start.8 = (f32[2,128,1280]{2,1,0:T(8,128)}, f32[2,128,1280]{2,1,0:T(8,128)S(1)}, u32[]{:S(2)}, u32[]{:S(2)}) collective-permute-start(f32[2,128,1280]{2,1,0:T(8,128)} %get-tuple-element.18), channel_id=1, source_target_pairs={{0,1},{1,2},{2,3},{3,4},{4,5},{5,6},{6,7},{8,9},{9,10},{10,11},{11... | collective-permute-start | bytes 3932168 | tf_op jit(solution)/shard_map/ppermute | solution.py:326
  91.9 32.1 %collective-permute-start.9 = (f32[2,128,1280]{2,1,0:T(8,128)}, f32[2,128,1280]{2,1,0:T(8,128)}, u32[]{:S(2)}, u32[]{:S(2)}) collective-permute-start(f32[2,128,1280]{2,1,0:T(8,128)} %get-tuple-element.19), channel_id=1, source_target_pairs={{1,0},{2,1},{3,2},{4,3},{5,4},{6,5},{7,6},{9,8},{10,9},{11,10},{12... | collective-permute-start | bytes 3932168 | tf_op jit(solution)/shard_map/ppermute | solution.py:326
  95.3 50.0 %copy-start = (f32[4,2,256,256]{3,2,1,0:T(8,128)S(1)}, f32[4,2,256,256]{3,2,1,0:T(8,128)}, u32[]{:S(2)}) copy-start(f32[4,2,256,256]{3,2,1,0:T(8,128)} %probe.3) | copy-start | bytes 6291460
  95.3 14.8 %collective-permute-start.7 = (f32[4,9,8,256]{3,2,1,0:T(8,128)S(1)}, f32[4,9,8,256]{3,2,1,0:T(8,128)S(1)}, u32[]{:S(2)}, u32[]{:S(2)}) collective-permute-start(f32[4,9,8,256]{3,2,1,0:T(8,128)S(1)} %get-tuple-element.43), channel_id=1, source_target_pairs={{0,96},{1,97},{2,98},{3,99},{4,100},{5,101},{6,102},{7,103},{8,104... | collective-permute-start | bytes 884744 | tf_op jit(solution)/shard_map/ppermute | solution.py:367
  97.5 12.6 %collective-permute-start.6 = (f32[4,9,8,256]{3,2,1,0:T(8,128)S(1)}, f32[4,9,8,256]{3,2,1,0:T(8,128)S(1)}, u32[]{:S(2)}, u32[]{:S(2)}) collective-permute-start(f32[4,9,8,256]{3,2,1,0:T(8,128)S(1)} %get-tuple-element.44), channel_id=1, source_target_pairs={{0,64},{1,65},{2,66},{3,67},{4,68},{5,69},{6,70},{7,71},{8,72},{9,... | collective-permute-start | bytes 884744 | tf_op jit(solution)/shard_map/ppermute | solution.py:367
  97.5 16.1 %collective-permute-start.5 = (f32[4,9,8,256]{3,2,1,0:T(8,128)S(1)}, f32[4,9,8,256]{3,2,1,0:T(8,128)S(1)}, u32[]{:S(2)}, u32[]{:S(2)}) collective-permute-start(f32[4,9,8,256]{3,2,1,0:T(8,128)S(1)} %get-tuple-element.42), channel_id=1, source_target_pairs={{0,32},{1,33},{2,34},{3,35},{4,36},{5,37},{6,38},{7,39},{8,40},{9,... | collective-permute-start | bytes 884744 | tf_op jit(solution)/shard_map/ppermute | solution.py:367
  124.0 11.3 %collective-permute-start.14 = (f32[1,9,8,256]{3,2,1,0:T(8,128)S(1)}, f32[1,9,8,256]{3,2,1,0:T(8,128)S(1)}, u32[]{:S(2)}, u32[]{:S(2)}) collective-permute-start(f32[1,9,8,256]{3,2,1,0:T(8,128)S(1)} %get-tuple-element.52), channel_id=1, source_target_pairs={{0,20},{1,21},{2,22},{3,23},{4,16},{5,17},{6,18},{7,19},{8,28},{9,... | collective-permute-start | bytes 221192 | tf_op jit(solution)/shard_map/ppermute | solution.py:367
  128.2 7.2 %collective-permute-start.13 = (f32[1,9,8,256]{3,2,1,0:T(8,128)S(1)}, f32[1,9,8,256]{3,2,1,0:T(8,128)S(1)}, u32[]{:S(2)}, u32[]{:S(2)}) collective-permute-start(f32[1,9,8,256]{3,2,1,0:T(8,128)S(1)} %get-tuple-element.53), channel_id=1, source_target_pairs={{0,4},{1,5},{2,6},{3,7},{4,0},{5,1},{6,2},{7,3},{8,12},{9,13},{10,... | collective-permute-start | bytes 221192 | tf_op jit(solution)/shard_map/ppermute | solution.py:367
  133.3 4.4 %collective-permute-start.12 = (f32[1,9,8,256]{3,2,1,0:T(8,128)S(1)}, f32[1,9,8,256]{3,2,1,0:T(8,128)S(1)}, u32[]{:S(2)}, u32[]{:S(2)}) collective-permute-start(f32[1,9,8,256]{3,2,1,0:T(8,128)S(1)} %get-tuple-element.51), channel_id=1, source_target_pairs={{0,16},{1,17},{2,18},{3,19},{4,20},{5,21},{6,22},{7,23},{8,24},{9,... | collective-permute-start | bytes 221192 | tf_op jit(solution)/shard_map/ppermute | solution.py:367
  137.8 12.3 %collective-permute-start.17 = (f32[1,9,8,256]{3,2,1,0:T(8,128)S(1)}, f32[1,9,8,256]{3,2,1,0:T(8,128)S(1)}, u32[]{:S(2)}, u32[]{:S(2)}) collective-permute-start(f32[1,9,8,256]{3,2,1,0:T(8,128)S(1)} %add_add_fusion.2), channel_id=1, source_target_pairs={{0,3},{1,0},{2,1},{3,2},{4,7},{5,4},{6,5},{7,6},{8,11},{9,8},{10,9... | collective-permute-start | bytes 221192 | tf_op jit(solution)/shard_map/ppermute | solution.py:351
  140.2 9.9 %collective-permute-start.16 = (f32[1,9,8,256]{3,2,1,0:T(8,128)S(1)}, f32[1,9,8,256]{3,2,1,0:T(8,128)}, u32[]{:S(2)}, u32[]{:S(2)}) collective-permute-start(f32[1,9,8,256]{3,2,1,0:T(8,128)S(1)} %add_add_fusion.2), channel_id=1, source_target_pairs={{0,2},{1,3},{2,0},{3,1},{4,6},{5,7},{6,4},{7,5},{8,10},{9,11},{10,... | collective-permute-start | bytes 221192 | tf_op jit(solution)/shard_map/ppermute | solution.py:351
  140.2 9.9 %collective-permute-start.15 = (f32[1,9,8,256]{3,2,1,0:T(8,128)S(1)}, f32[1,9,8,256]{3,2,1,0:T(8,128)}, u32[]{:S(2)}, u32[]{:S(2)}) collective-permute-start(f32[1,9,8,256]{3,2,1,0:T(8,128)S(1)} %add_add_fusion.2), channel_id=1, source_target_pairs={{0,1},{1,2},{2,3},{3,0},{4,5},{5,6},{6,7},{7,4},{8,9},{9,10},{10,1... | collective-permute-start | bytes 221192 | tf_op jit(solution)/shard_map/ppermute | solution.py:351
  150.0 20.1 %copy-start.5 = (f32[2,512,128]{2,1,0:T(8,128)S(1)}, f32[2,512,128]{2,1,0:T(8,128)}, u32[]{:S(2)}) copy-start(f32[2,512,128]{2,1,0:T(8,128)} %get-tuple-element.22) | copy-start | bytes 1572868
  151.1 12.9 %collective-permute-start.19 = (f32[8,8,256]{2,1,0:T(8,128)S(1)}, f32[8,8,256]{2,1,0:T(8,128)S(1)}, u32[]{:S(2)}, u32[]{:S(2)}) collective-permute-start(f32[8,8,256]{2,1,0:T(8,128)S(1)} %fusion.1), channel_id=1, source_target_pairs={{0,4},{1,5},{2,6},{3,7},{4,0},{5,1},{6,2},{7,3},{8,72},{9,73},{10,... | collective-permute-start | bytes 196616 | tf_op jit(solution)/shard_map/ppermute | solution.py:351
  161.5 3.1 %collective-permute-start.20 = (f32[8,8,256]{2,1,0:T(8,128)S(1)}, f32[8,8,256]{2,1,0:T(8,128)S(1)}, u32[]{:S(2)}, u32[]{:S(2)}) collective-permute-start(f32[8,8,256]{2,1,0:T(8,128)S(1)} %fusion.1), channel_id=1, source_target_pairs={{0,20},{1,21},{2,22},{3,23},{4,16},{5,17},{6,18},{7,19},{8,104},{9... | collective-permute-start | bytes 196616 | tf_op jit(solution)/shard_map/ppermute | solution.py:351
  161.9 4.3 %collective-permute-start.18 = (f32[8,8,256]{2,1,0:T(8,128)S(1)}, f32[8,8,256]{2,1,0:T(8,128)S(1)}, u32[]{:S(2)}, u32[]{:S(2)}) collective-permute-start(f32[8,8,256]{2,1,0:T(8,128)S(1)} %fusion.1), channel_id=1, source_target_pairs={{0,16},{1,17},{2,18},{3,19},{4,20},{5,21},{6,22},{7,23},{8,40},{9,... | collective-permute-start | bytes 196616 | tf_op jit(solution)/shard_map/ppermute | solution.py:351
  164.0 16.9 %copy-start.4 = (f32[2,512,128]{2,1,0:T(8,128)S(1)}, f32[2,512,128]{2,1,0:T(8,128)}, u32[]{:S(2)}) copy-start(f32[2,512,128]{2,1,0:T(8,128)} %get-tuple-element.15) | copy-start | bytes 1572868
  166.3 16.6 %collective-permute-start.22 = (f32[8,32,256]{2,1,0:T(8,128)S(1)}, f32[8,32,256]{2,1,0:T(8,128)S(1)}, u32[]{:S(2)}, u32[]{:S(2)}) collective-permute-start(f32[8,32,256]{2,1,0:T(8,128)S(1)} %pad_maximum_fusion.5), channel_id=1, source_target_pairs={{0,64},{1,65},{2,66},{3,67},{4,68},{5,69},{6,70},{7,71},{8,12},{9,... | collective-permute-start | bytes 786440 | tf_op jit(solution)/shard_map/ppermute | solution.py:351
  168.2 14.7 %collective-permute-start.23 = (f32[8,32,256]{2,1,0:T(8,128)S(1)}, f32[8,32,256]{2,1,0:T(8,128)S(1)}, u32[]{:S(2)}, u32[]{:S(2)}) collective-permute-start(f32[8,32,256]{2,1,0:T(8,128)S(1)} %pad_maximum_fusion.5), channel_id=1, source_target_pairs={{0,96},{1,97},{2,98},{3,99},{4,100},{5,101},{6,102},{7,103},{8,28}... | collective-permute-start | bytes 786440 | tf_op jit(solution)/shard_map/ppermute | solution.py:351
  169.6 13.3 %collective-permute-start.21 = (f32[8,32,256]{2,1,0:T(8,128)S(1)}, f32[8,32,256]{2,1,0:T(8,128)S(1)}, u32[]{:S(2)}, u32[]{:S(2)}) collective-permute-start(f32[8,32,256]{2,1,0:T(8,128)S(1)} %pad_maximum_fusion.5), channel_id=1, source_target_pairs={{0,32},{1,33},{2,34},{3,35},{4,36},{5,37},{6,38},{7,39},{8,24},{9,... | collective-permute-start | bytes 786440 | tf_op jit(solution)/shard_map/ppermute | solution.py:351
  170.2 16.8 %collective-permute-start.11 = (f32[2,512,128]{2,1,0:T(8,128)S(1)}, f32[2,512,128]{2,1,0:T(8,128)S(1)}, u32[]{:S(2)}, u32[]{:S(2)}) collective-permute-start(f32[2,512,128]{2,1,0:T(8,128)S(1)} %pad_add_fusion), channel_id=1, source_target_pairs={{8,0},{16,8},{24,16},{32,24},{40,32},{48,40},{56,48},{64,56},{72,6... | collective-permute-start | bytes 1572872 | tf_op jit(solution)/shard_map/ppermute | solution.py:326
  180.9 13.4 %collective-permute-start.10 = (f32[2,512,128]{2,1,0:T(8,128)S(1)}, f32[2,512,128]{2,1,0:T(8,128)S(1)}, u32[]{:S(2)}, u32[]{:S(2)}) collective-permute-start(f32[2,512,128]{2,1,0:T(8,128)S(1)} %pad_add_fusion.1), channel_id=1, source_target_pairs={{0,8},{8,16},{16,24},{24,32},{32,40},{40,48},{48,56},{56,64},{64,7... | collective-permute-start | bytes 1572872 | tf_op jit(solution)/shard_map/ppermute | solution.py:326
  182.9 11.4 %copy-start.3 = (f32[2,512,1024]{2,1,0:T(8,128)S(1)}, f32[2,512,1024]{2,1,0:T(8,128)}, u32[]{:S(2)}) copy-start(f32[2,512,1024]{2,1,0:T(8,128)} %get-tuple-element.14) | copy-start | bytes 12582916
  183.2 14.6 %collective-permute-start.24 = (f32[8,128,256]{2,1,0:T(8,128)S(1)}, f32[8,128,256]{2,1,0:T(8,128)S(1)}, u32[]{:S(2)}, u32[]{:S(2)}) collective-permute-start(f32[8,128,256]{2,1,0:T(8,128)S(1)} %pad_maximum_fusion.2), channel_id=1, source_target_pairs={{0,8},{1,9},{2,10},{3,11},{4,12},{5,13},{6,14},{7,15},{8,0},{9,1},... | collective-permute-start | bytes 3145736 | tf_op jit(solution)/shard_map/ppermute | solution.py:393
  185.4 8.9 %copy-start.2 = (f32[2,512,1024]{2,1,0:T(8,128)S(1)}, f32[2,512,1024]{2,1,0:T(8,128)}, u32[]{:S(2)}) copy-start(f32[2,512,1024]{2,1,0:T(8,128)} %obj.1) | copy-start | bytes 12582916

commit v3 on v2

--- a/solution.py
+++ b/solution.py
@@ -30,15 +30,13 @@
             high = table.astype(jnp.bfloat16)
             low = (table - high.astype(np.float32)).astype(jnp.bfloat16)
             pairs.append((high, low))
-    m0, m0t, m1, m1t = pairs
-    after = np.stack([np.concatenate([h, h, l], 0) for h, l in (m0, m1, m0t, m1t)])
-    before = np.stack([np.concatenate([h, h, l], 1) for h, l in (m0t, m1t, m0, m1)])
+    both = np.stack([np.stack(pair) for pair in pairs])
     order = np.zeros((length, length), np.float32)
     for k in range(half):
         order[2 * k, k] = 1
         order[2 * k + 1, half + k] = 1
     order = np.concatenate([order, order], 0).astype(jnp.bfloat16)
-    return jnp.asarray(after), jnp.asarray(before), jnp.asarray(order)
+    return jnp.asarray(both), jnp.asarray(order)
 
 
 def split(x):
@@ -132,30 +130,41 @@
     )(info, probe)
 
 
-def grads_kernel(
-    count, offs, bit, obj, left, right, up, down, probe, amps, after, before, order,
-    core_o, left_o, right_o, up_o, down_o, give_o, keep_o,
-    ext, tot, pg, win, zs, zd, p0, p1, u, ap, sems, *, modes, n, tr, tc,
-):
+def grads_kernel(*refs, modes, n, tr, tc, early):
+    count, offs, bit, obj, left, right, *refs = refs
+    if early:
+        probe, amps, table, order, core_o, left_o, right_o, pg_o, *refs = refs
+    else:
+        up, down, eup, edown, pg_e, probe, amps, table, order, *refs = refs
+        core_o, left_o, right_o, up_o, down_o, give_o, keep_o, *refs = refs
+    ext, tot, pg, win, zs, zd, p0, p1, u, ap, sems = refs
     h = n // 2
     ch = 64
     nb = ch // 8
-
-    def places(big, core, left, right, up, down):
-        rows = pl.ds(h, tr)
-        return [
-            (core, big.at[:, rows, pl.ds(h, tc)]),
-            (left.at[:, pl.ds(0, tr), :], big.at[:, rows, pl.ds(0, h)]),
-            (right.at[:, pl.ds(0, tr), :], big.at[:, rows, pl.ds(h + tc, h)]),
-            (up.at[:, pl.ds(0, h), :], big.at[:, pl.ds(0, h), :]),
-            (down.at[:, pl.ds(0, h), :], big.at[:, pl.ds(h + tr, h), :]),
+    rows, cols = pl.ds(h, tr), pl.ds(h, tc)
+    lo, hi = pl.ds(0, h), pl.ds(h + tc, h)
+    top, bot = pl.ds(0, h), pl.ds(h + tr, h)
+    places_in = [
+        (obj, ext.at[:, rows, cols]),
+        (left.at[:, pl.ds(0, tr), :], ext.at[:, rows, lo]),
+        (right.at[:, pl.ds(0, tr), :], ext.at[:, rows, hi]),
+    ]
+    if not early:
+        places_in += [
+            (up, ext.at[:, top, cols]),
+            (down, ext.at[:, bot, cols]),
+            (eup.at[0, :, lo, :], ext.at[:, top, lo]),
+            (eup.at[1, :, lo, :], ext.at[:, top, hi]),
+            (edown.at[0, :, lo, :], ext.at[:, bot, lo]),
+            (edown.at[1, :, lo, :], ext.at[:, bot, hi]),
+            (pg_e, pg),
         ]
-
-    loads = copies(places(ext, obj, left, right, up, down), sems)
+    loads = copies(places_in, sems)
     for copy in loads:
         copy.start()
     tot[...] = jnp.zeros_like(tot)
-    pg[...] = jnp.zeros_like(pg)
+    if early:
+        pg[...] = jnp.zeros_like(pg)
     for copy in loads:
         copy.wait()
 
@@ -163,13 +172,19 @@
     sub = lax.broadcasted_iota(jnp.int32, (nb, 8, h), 1)
 
     def after_dot(z, i):
-        return dot(jnp.concatenate([z[...], z[:, :n]], axis=1), after[i])
+        high, low = table[i, 0], table[i, 1]
+        return dot(z[:, :n], high) + (dot(z[:, n:], high) + dot(z[:, :n], low))
 
     def before_dot(i, y):
         high, low = split(y)
-        return dot(before[i], jnp.concatenate([high, low, high], axis=0))
-
-    def slot(s, carry):
+        return dot(table[i, 0], high) + (dot(table[i, 0], low) + dot(table[i, 1], high))
+
+    def visit(s, carry):
+        inside = (offs[0, s] >= h) & (offs[0, s] <= tr + h - n)
+        pl.when(inside if early else ~inside)(lambda: slot(s))
+        return carry
+
+    def slot(s):
         r8, rr, q, rem = window_place(offs, s, tr + n, tc + n, n)
         back_lanes = jnp.where((rem == 0) | (rem == h), 0, h - rem)
         back_rows = jnp.where((rr == 0) | (rr == 8), 0, 8 - rr)
@@ -202,7 +217,7 @@
                 z = jnp.concatenate([wr[:, :h] - wr[:, h:], wi[:, :h] - wi[:, h:]], axis=1)
                 zd[ks, :n], zd[ks, n:] = split(z)
         p0[...] = after_dot(zs, 0)
-        p1[...] = after_dot(zd, 1)
+        p1[...] = after_dot(zd, 2)
         for k in range(modes):
             top, bot = pl.ds(k * n, h), pl.ds(k * n + h, h)
 
@@ -214,8 +229,8 @@
                     )
                 return jnp.concatenate(parts, axis=0)
 
-            u[k, 0] = before_dot(0, folded(1.0))
-            u[k, 1] = before_dot(1, folded(-1.0))
+            u[k, 0] = before_dot(1, folded(1.0))
+            u[k, 1] = before_dot(3, folded(-1.0))
         am = dot(jnp.concatenate(split(amps[s]), axis=1), order[...])
         ap[0] = am[:, :h]
         ap[1] = am[:, h:]
@@ -232,13 +247,13 @@
                 jnp.concatenate([u[k, e, :h, :] * factor[e], u[k, e, h:, :] * factor[e]], axis=0)
                 for e in range(2)
             ]
-            even, odd = before_dot(2, y[0]), before_dot(3, y[1])
+            even, odd = before_dot(0, y[0]), before_dot(2, y[1])
             for half, v in ((0, even + odd), (1, even - odd)):
                 ks = pl.ds(k * n + half * h, h)
                 for ref, ls in ((zs, slice(0, h)), (zd, slice(h, n))):
                     z = jnp.concatenate([v[:h, ls], v[h:, ls]], axis=1)
                     ref[ks, :n], ref[ks, n:] = split(z)
-        p0[...] = after_dot(zs, 2)
+        p0[...] = after_dot(zs, 1)
         p1[...] = after_dot(zd, 3)
         for r0 in range(0, n, ch):
             rs = pl.ds(r0, ch)
@@ -260,13 +275,20 @@
 
             for comp, v in ((0, o_re), (1, o_im)):
                 add_shifted(tot, comp, v, r0, r8, rr, q, rem)
-        return carry
-
-    lax.fori_loop(0, count[0], slot, 0)
-    half = n // 16
-    give, keep = pl.ds((1 - bit[0]) * half, half), pl.ds(bit[0] * half, half)
-    outs = [(pg.at[give], give_o), (pg.at[keep], keep_o)]
-    outs += [(b, a) for a, b in places(tot, core_o, left_o, right_o, up_o, down_o)]
+
+    lax.fori_loop(0, count[0], visit, 0)
+    outs = [
+        (tot.at[:, rows, cols], core_o),
+        (tot.at[:, rows, lo], left_o),
+        (tot.at[:, rows, hi], right_o),
+    ]
+    if early:
+        outs += [(pg, pg_o)]
+    else:
+        half = n // 16
+        give, keep = pl.ds((1 - bit[0]) * half, half), pl.ds(bit[0] * half, half)
+        outs += [(pg.at[give], give_o), (pg.at[keep], keep_o)]
+        outs += [(tot.at[:, top, :], up_o), (tot.at[:, bot, :], down_o)]
     stores = copies(outs, sems)
     for copy in stores:
         copy.start()
@@ -275,6 +297,7 @@
 
 
 def tile_grads(count, offs, bit, obj, halos, probe, amps):
+    early = len(halos) == 2
     modes, _, n, _ = probe.shape
     h = n // 2
     _, tr, tc = obj.shape
@@ -283,14 +306,17 @@
     anyw = pl.BlockSpec(memory_space=pl.ANY)
     shape = lambda *dims: jax.ShapeDtypeStruct(dims, F32)
     rows, cols = tr + n, tc + n
+    blocks = n // 8
+    outs = [shape(2, tr, tc), shape(2, tr, h), shape(2, tr, h)]
+    if early:
+        outs += [shape(blocks, 2 * modes + 1, 8, n)]
+    else:
+        outs += [shape(2, h, cols)] * 2 + [shape(blocks // 2, 2 * modes + 1, 8, n)] * 2
     return pl.pallas_call(
-        functools.partial(grads_kernel, modes=modes, n=n, tr=tr, tc=tc),
-        out_shape=(
-            shape(2, tr, tc), shape(2, tr, h), shape(2, tr, h), shape(2, h, cols), shape(2, h, cols),
-            shape(n // 16, 2 * modes + 1, 8, n), shape(n // 16, 2 * modes + 1, 8, n),
-        ),
-        in_specs=[smem, smem, smem] + [anyw] * 5 + [vmem] * 5,
-        out_specs=[anyw] * 7,
+        functools.partial(grads_kernel, modes=modes, n=n, tr=tr, tc=tc, early=early),
+        out_shape=tuple(outs),
+        in_specs=[smem, smem, smem] + [anyw] * (1 + len(halos)) + [vmem] * 4,
+        out_specs=[anyw] * len(outs),
         scratch_shapes=[
             pltpu.VMEM((2, rows, cols), F32),
             pltpu.VMEM((2, rows, cols), F32),
@@ -302,11 +328,11 @@
             pltpu.VMEM((modes * n, n), F32),
             pltpu.VMEM((modes, 2, n, n), F32),
             pltpu.VMEM((2, n, h), F32),
-            pltpu.SemaphoreType.DMA((7,)),
+            pltpu.SemaphoreType.DMA((10,)),
         ],
         compiler_params=pltpu.CompilerParams(vmem_limit_bytes=56 * MIB),
         cost_estimate=pl.CostEstimate(flops=40_000_000_000, bytes_accessed=30_000_000, transcendentals=0),
-        name="tile_grads",
+        name="tile_grads_early" if early else "tile_grads_late",
     )(count, offs, bit, obj, *halos, probe, amps, *tables(n))
 
 
@@ -355,10 +381,15 @@
     return lax.axis_index("wide") & 1
 
 
-def probe_update(give, keep, probe, arrived, ready):
+def probe_update(give, keep, probe, arrived):
     w, n = lax.axis_index("wide"), lax.axis_index("narrow")
-    core, x, y = w & 1, w >> 2, ((n >> 2) << 1) | ((w >> 1) & 1)
-    v = keep + lax.ppermute(give, BOTH, route(("core", "core"), 1))
+    core, x, z = w & 1, w >> 2, n & 3
+    cut = give.shape[0] // 4
+    got = [
+        lax.ppermute(give[i * cut : (i + 1) * cut], BOTH, route(("core", "core"), 1))
+        for i in range(4)
+    ]
+    v = keep + jnp.concatenate(got, axis=0)
 
     def scattered(v, t, axis):
         size = v.shape[0] // 4
@@ -370,11 +401,11 @@
 
     v = scattered(v, x, "x")
     v, arrived = lax.optimization_barrier((v, arrived))
-    v = scattered(v, y, "y")
-    a, b, c = around(v, ("z", "z"))
+    v = scattered(v, z, "z")
+    a, b, c = around(v, ("y", "y"))
     v = (v + a + b + c)[0]
     modes, _, size, _ = probe.shape
-    block = core * 16 + x * 4 + y
+    block = core * 16 + x * 4 + z
     mine = lax.dynamic_slice_in_dim(probe.reshape(2 * modes, size, size), block * 8, 8, 1)
     mine = mine - v[: 2 * modes] / (v[2 * modes] + step_floor)
 
@@ -387,62 +418,76 @@
             rows.append(one)
         return jnp.concatenate(rows, axis=1)
 
-    mine, ready = lax.optimization_barrier((mine, ready))
-    mine = gathered(mine, jnp.where(core == 0, y, x), ("y", "x"))
-    mine = gathered(mine, jnp.where(core == 0, x, y), ("x", "y"))
+    return mine, arrived, gathered
+
+
+def probe_gather(mine, gathered, sides, update):
+    w, n = lax.axis_index("wide"), lax.axis_index("narrow")
+    core, x, z = w & 1, w >> 2, n & 3
+    mine = gathered(mine, jnp.where(core == 0, z, x), ("z", "x"))
+    mine, sides = lax.optimization_barrier((mine, sides))
+    new_object = update(*sides)
+    mine = gathered(mine, jnp.where(core == 0, x, z), ("x", "z"))
+    mine, new_object = lax.optimization_barrier((mine, new_object))
     got = lax.ppermute(mine, BOTH, route(("core", "core"), 1))
     first = jnp.where(core == 0, mine, got)
     second = jnp.where(core == 0, got, mine)
-    second = second.reshape(2 * modes, 4, 4, 8, size).swapaxes(1, 2).reshape(first.shape)
-    return jnp.concatenate([first, second], axis=1).reshape(probe.shape), arrived, ready
-
-
-def label(count, offs, width):
-    info = jnp.concatenate([count, offs[0], offs[1]]).astype(F32)
-    info = jnp.pad(info, (0, width - info.shape[0]))
-    return jnp.broadcast_to(info, (2, 8, width))
+    planes, _, size = mine.shape
+    second = second.reshape(planes, 4, 4, 8, size).swapaxes(1, 2).reshape(first.shape)
+    return jnp.concatenate([first, second], axis=1), new_object
 
 
 def on_device(object_field, probe_modes, amplitudes, offsets, counts):
     h = probe_modes.shape[-1] // 2
     _, tr, tc = object_field.shape
-    count, offs = counts[0], offsets[:, 0, 0]
-    mine = label(count, offs, h)
+    count, offs, bit = counts[0], offsets[:, 0, 0], own_core()[None]
+    mine = jnp.concatenate([count, offs[0], offs[1]]).astype(F32)
+    mine = jnp.broadcast_to(jnp.pad(mine, (0, h - mine.shape[0])), (2, 8, h))
+    up = moved(object_field[:, tr - h :], "narrow", 1)
+    down = moved(object_field[:, :h], "narrow", -1)
     tagged = lambda cols: jnp.concatenate([object_field[:, :, cols], mine], axis=1)
     left = moved(tagged(slice(tc - h, tc)), "wide", 1)
     right = moved(tagged(slice(0, h)), "wide", -1)
-    own = jnp.concatenate([object_field, label(count, offs, tc)], axis=1)
-
-    def wider(rows):
-        parts = [left, own, right]
-        return jnp.concatenate(
-            [jnp.concatenate([p[:, rows], p[:, tr:]], axis=1) for p in parts], axis=2
-        )
-
-    up = moved(wider(slice(tr - h, tr)), "narrow", 1)
-    down = moved(wider(slice(0, h)), "narrow", -1)
-    pick = lambda a, row, col: a[0, row, col : col + 16]
-    info = [pick(up, h, c) for c in (0, h, h + tc)]
-    info += [pick(left, tr, 0), pick(own, tr, 0), pick(right, tr, 0)]
-    info += [pick(down, h, c) for c in (0, h, h + tc)]
+    tags = jnp.stack([left[:1, tr:], right[:1, tr:]])
+    corner = lambda rows: jnp.concatenate(
+        [
+            jnp.stack([left[:, rows], right[:, rows]]),
+            jnp.concatenate([tags, jnp.stack([mine[:1]] * 2)], axis=1),
+        ],
+        axis=2,
+    )
+    eup = moved(corner(slice(tr - h, tr)), "narrow", 1)
+    edown = moved(corner(slice(0, h)), "narrow", -1)
+    core_e, left_e, right_e, pg_e = tile_grads(
+        count, offs, bit, object_field, (left, right), probe_modes, amplitudes[0, 0]
+    )
+    row = lambda e: [e[0, 0, h, :16], e[0, 1, h, :16], e[1, 0, h, :16]]
+    info = row(eup) + [left[0, tr, :16], mine[0, 0, :16], right[0, tr, :16]] + row(edown)
     info = jnp.stack(info).astype(jnp.int32)
     illum = tile_illum(info, probe_modes, tr, tc, offs.shape[-1])
     core, left_g, right_g, up_g, down_g, give, keep = tile_grads(
-        count, offs, own_core()[None], object_field, (left, right, up, down),
+        count, offs, bit, object_field, (left, right, up, down, eup, edown, pg_e),
         probe_modes, amplitudes[0, 0],
     )
     below = moved(up_g, "narrow", -1)
     above = moved(down_g, "narrow", 1)
-    new_probe, (above, below), illum = probe_update(give, keep, probe_modes, (above, below), illum)
+    arrived = (above, below, illum)
+    block, (above, below, illum), gathered = probe_update(give, keep, probe_modes, arrived)
     side = lambda strip, cols: (
         strip
         + jnp.pad(above[:, :, cols], ((0, 0), (0, tr - h), (0, 0)))
         + jnp.pad(below[:, :, cols], ((0, 0), (tr - h, 0), (0, 0)))
     )
-    from_right = moved(side(left_g, slice(0, h)), "wide", -1)
-    from_left = moved(side(right_g, slice(h + tc, 2 * h + tc)), "wide", 1)
-    new_object = object_update(object_field, core, illum, from_left, from_right, above, below)
-    return (new_object, new_probe)
+    sides = (
+        side(left_e + left_g, slice(0, h)),
+        side(right_e + right_g, slice(h + tc, 2 * h + tc)),
+    )
+    block, sides = lax.optimization_barrier((block, sides))
+    from_right = moved(sides[0], "wide", -1)
+    from_left = moved(sides[1], "wide", 1)
+    update = lambda a, b: object_update(object_field, core_e + core, illum, a, b, above, below)
+    new_probe, new_object = probe_gather(block, gathered, (from_left, from_right), update)
+    return (new_object, new_probe.reshape(probe_modes.shape))
 
 
 def solution(mesh):

time: 200 us -> 180 us (0.900)
  the two profiles are of different devices: /device:TPU:1 before, /device:TPU:9 now
where the time goes in v3:
time: 180 us; the launch traced here: 177 us
  starting transfers between devices  67 us (37%)
  Pallas kernels  51.8 us (29%)
  waiting for transfers between devices  27.3 us (15%)
  local copies, waits for them, and re-layouts  18.3 us (10%)
  other arithmetic  11.1 us (6%)
    pallas_call x2, Pallas kernels, tile_grads(): pl.pallas_call(functools.partial(grads_kernel, modes=modes, n=n, tr=tr, t...  47.5 us
    ppermute x10, starting transfers between devices, moved(): return lax.ppermute(block, axis, route)  34.9 us
    ppermute x9, starting transfers between devices, around(): return [lax.ppermute(piece, BOTH, route(axes, hop)) for hop in (1, 2, 3)]  13.9 us
    ppermute x6, starting transfers between devices, scattered(): lax.ppermute(part(t + hop), BOTH, route((axis, axis), hop))  12.3 us
    ppermute x10, waiting for transfers between devices, moved(): return lax.ppermute(block, axis, route)  10.3 us
    ppermute x6, waiting for transfers between devices, scattered(): lax.ppermute(part(t + hop), BOTH, route((axis, axis), hop))  9.29 us
    sub x1, other arithmetic, object_update(): return obj - total / illum  6.47 us
    ppermute x9, waiting for transfers between devices, around(): return [lax.ppermute(piece, BOTH, route(axes, hop)) for hop in (1, 2, 3)]  5.35 us
  transfers between devices with their start and end apart: 30, of which 11 were waited for; matrix products, arithmetic and copies ran while one was open for 11% of the time, Pallas kernels for 18%

profile of v3, /device:TPU:9, one launch (start us, length us, event | category | flops | bytes accessed | tf_op | source)
XLA Modules:
  0.0 177.2 jit_solution(16771871293003305574)
XLA Ops:
  1.3 0.7 slice_bitcast_fusion.17
  2.0 1.4 fusion.6
  3.6 2.6 %collective-permute-start.1 = (f32[2,520,128]{2,1,0:T(8,128)S(1)}, f32[2,520,128]{2,1,0:T(8,128)}, u32[]{:S(2)}, u32[]{:S(2)}) collective-permute-start(f32[2,520,128]{2,1,0:T(8,128)S(1)} %get-tuple-element.88), channel_id=1, source_target_pairs={{8,0},{16,8},{24,16},{32,24},{40,32},{48,40},{56,48},{64,56},{72,6... | collective-permute-start | bytes 1597448 | tf_op jit(solution)/shard_map/ppermute | solution.py:352
  6.1 3.9 %collective-permute-start = (f32[2,520,128]{2,1,0:T(8,128)S(1)}, f32[2,520,128]{2,1,0:T(8,128)}, u32[]{:S(2)}, u32[]{:S(2)}) collective-permute-start(f32[2,520,128]{2,1,0:T(8,128)S(1)} %get-tuple-element.89), channel_id=1, source_target_pairs={{0,8},{8,16},{16,24},{24,32},{32,40},{40,48},{48,56},{56,64},{64,7... | collective-permute-start | bytes 1597448 | tf_op jit(solution)/shard_map/ppermute | solution.py:352
  10.0 0.2 fusion.5
  10.3 4.5 %collective-permute-start.2 = (f32[2,128,1024]{2,1,0:T(8,128)S(1)}, f32[2,128,1024]{2,1,0:T(8,128)}, u32[]{:S(2)}, u32[]{:S(2)}) collective-permute-start(f32[2,128,1024]{2,1,0:T(8,128)S(1)} %get-tuple-element.49), channel_id=1, source_target_pairs={{0,1},{1,2},{2,3},{3,4},{4,5},{5,6},{6,7},{8,9},{9,10},{10,11},{11... | collective-permute-start | bytes 3145736 | tf_op jit(solution)/shard_map/ppermute | solution.py:352
  14.8 1.3 collective-permute-start.3
  16.1 0.7 slice_bitcast_fusion.5
  16.8 1.0 slice_bitcast_fusion
  17.8 0.7 slice_bitcast_fusion.6
  18.5 1.0 slice_bitcast_fusion.1
  19.5 4.0 %collective-permute-start.4 = (f32[2,2,136,128]{3,2,1,0:T(8,128)S(1)}, f32[2,2,136,128]{3,2,1,0:T(8,128)S(1)}, u32[]{:S(2)}, u32[]{:S(2)}) collective-permute-start(f32[2,2,136,128]{3,2,1,0:T(8,128)S(1)} %get-tuple-element.87), channel_id=1, source_target_pairs={{0,1},{1,2},{2,3},{3,4},{4,5},{5,6},{6,7},{8,9},{9,10},{10,11},{11... | collective-permute-start | bytes 835592 | tf_op jit(solution)/shard_map/ppermute | solution.py:352
  23.5 1.3 collective-permute-start.5
  24.8 27.4 %tile_grads_early.1 = (f32[2,512,1024]{2,1,0:T(8,128)}, f32[2,512,128]{2,1,0:T(8,128)}, f32[2,512,128]{2,1,0:T(8,128)}, f32[32,9,8,256]{3,2,1,0:T(8,128)}) custom-call(s32[1]{0:T(128)} %bitcast.53.refs_0_, s32[2,6]{1,0:T(2,128)} %bitcast.59, s32[1]{0:T(128)} %bitcast.3.refs_2_, f32[2,512,1024]{2,1,0:T(8,128)} %refs_3_.3, ...), custom_call_target="tpu_custom_call" | custom-call | flops 40000000000 | bytes 30000000 | tf_op jit(solution)/shard_map/tile_grads_early/pallas_call | solution.py:315
  52.3 0.7 copy-done.8
  53.1 20.1 %tile_grads_late.1 = (f32[2,512,1024]{2,1,0:T(8,128)}, f32[2,512,128]{2,1,0:T(8,128)}, f32[2,512,128]{2,1,0:T(8,128)}, f32[2,128,1280]{2,1,0:T(8,128)}, f32[2,12...) custom-call(s32[1]{0:T(128)} %bitcast.54.refs_0_, s32[2,6]{1,0:T(2,128)} %bitcast.60, ...), custom_call_target="tpu_custom_call" | custom-call | flops 40000000000 | bytes 30000000 | tf_op jit(solution)/shard_map/tile_grads_late/pallas_call | solution.py:315
  73.2 1.4 fusion.9
  74.6 0.3 collective-permute-start.9
  74.9 0.5 collective-permute-start.8
  75.5 0.4 collective-permute-start.6
  75.9 0.7 slice_bitcast_fusion.11
  76.6 8.5 %collective-permute-start.13 = (f32[2,128,1280]{2,1,0:T(8,128)}, f32[2,128,1280]{2,1,0:T(8,128)}, u32[]{:S(2)}, u32[]{:S(2)}) collective-permute-start(f32[2,128,1280]{2,1,0:T(8,128)} %get-tuple-element.28), channel_id=1, source_target_pairs={{0,1},{1,2},{2,3},{3,4},{4,5},{5,6},{6,7},{8,9},{9,10},{10,11},{11... | collective-permute-start | bytes 3932168 | tf_op jit(solution)/shard_map/ppermute | solution.py:352
  85.1 1.3 collective-permute-start.14
  86.4 0.7 slice_bitcast_fusion.10
  87.1 0.2 maximum_add_fusion
  87.3 1.0 constant_dynamic-slice_fusion.5
  88.3 3.0 %collective-permute-start.11 = (f32[4,9,8,256]{3,2,1,0:T(8,128)}, f32[4,9,8,256]{3,2,1,0:T(8,128)}, u32[]{:S(2)}, u32[]{:S(2)}) collective-permute-start(f32[4,9,8,256]{3,2,1,0:T(8,128)} %get-tuple-element.60), channel_id=1, source_target_pairs={{0,64},{1,65},{2,66},{3,67},{4,68},{5,69},{6,70},{7,71},{8,72},{9,... | collective-permute-start | bytes 884744 | tf_op jit(solution)/shard_map/ppermute | solution.py:398
  91.3 0.7 slice_bitcast_fusion.12
  92.0 0.7 slice_bitcast_fusion.7
  92.8 1.6 copy-done
  94.3 4.3 %tile_illum.1 = f32[512,1024]{1,0:T(8,128)S(1)} custom-call(s32[9,16]{1,0:T(8,128)S(1)} %convert_element_type.23.info, f32[4,2,256,256]{3,2,1,0:T(8,128)S(1)} %copy-done), custom_call_target="tpu_custom_call" | custom-call | flops 20000000 | bytes 8000000 | tf_op jit(solution)/shard_map/tile_illum/pallas_call | solution.py:121
  98.7 6.7 %collective-permute-done.10 = f32[4,9,8,256]{3,2,1,0:T(8,128)} collective-permute-done((f32[4,9,8,256]{3,2,1,0:T(8,128)}, f32[4,9,8,256]{3,2,1,0:T(8,128)}, u32[]{:S(2)}, u32[]{:S(2)}) %collective-permute-start.10) | collective-permute-done | bytes 294944 | tf_op jit(solution)/shard_map/ppermute | solution.py:398
  105.4 1.2 add_add_fusion
  106.6 5.5 %collective-permute-done.13 = f32[2,128,1280]{2,1,0:T(8,128)} collective-permute-done((f32[2,128,1280]{2,1,0:T(8,128)}, f32[2,128,1280]{2,1,0:T(8,128)}, u32[]{:S(2)}, u32[]{:S(2)}) %collective-permute-start.13) | collective-permute-done | bytes 1310752 | tf_op jit(solution)/shard_map/ppermute | solution.py:352
  112.1 4.9 %collective-permute-done.14 = f32[2,128,1280]{2,1,0:T(8,128)} collective-permute-done((f32[2,128,1280]{2,1,0:T(8,128)}, f32[2,128,1280]{2,1,0:T(8,128)}, u32[]{:S(2)}, u32[]{:S(2)}) %collective-permute-start.14) | collective-permute-done | bytes 1310752 | tf_op jit(solution)/shard_map/ppermute | solution.py:352
  117.0 8.6 %collective-permute-start.17 = (f32[1,9,8,256]{3,2,1,0:T(8,128)S(1)}, f32[1,9,8,256]{3,2,1,0:T(8,128)S(1)}, u32[]{:S(2)}, u32[]{:S(2)}) collective-permute-start(f32[1,9,8,256]{3,2,1,0:T(8,128)S(1)} %get-tuple-element.74), channel_id=1, source_target_pairs={{0,3},{1,0},{2,1},{3,2},{4,7},{5,4},{6,5},{7,6},{8,11},{9,8},{10,9... | collective-permute-start | bytes 221192 | tf_op jit(solution)/shard_map/ppermute | solution.py:398
  125.6 0.7 collective-permute-start.15
  126.3 1.0 fusion.8
  127.3 1.0 fusion.7
  128.3 2.1 %collective-permute-done.16 = f32[1,9,8,256]{3,2,1,0:T(8,128)S(1)} collective-permute-done((f32[1,9,8,256]{3,2,1,0:T(8,128)S(1)}, f32[1,9,8,256]{3,2,1,0:T(8,128)S(1)}, u32[]{:S(2)}, u32[]{:S(2)}) %collective-permute-start.16) | collective-permute-done | bytes 73760 | tf_op jit(solution)/shard_map/ppermute | solution.py:398
  130.4 0.4 collective-permute-done.15
  130.9 1.1 collective-permute-start.20
  132.0 1.3 collective-permute-start.18
  133.4 0.7 collective-permute-done.20
  134.1 2.6 %collective-permute-done.19 = f32[1,9,8,256]{3,2,1,0:T(8,128)S(1)} collective-permute-done((f32[1,9,8,256]{3,2,1,0:T(8,128)S(1)}, f32[1,9,8,256]{3,2,1,0:T(8,128)S(1)}, u32[]{:S(2)}, u32[]{:S(2)}) %collective-permute-start.19) | collective-permute-done | bytes 73760 | tf_op jit(solution)/shard_map/ppermute | solution.py:377
  136.7 0.3 collective-permute-done.18
  137.0 0.9 fusion.3
  137.9 2.1 %collective-permute-start.24 = (f32[2,512,128]{2,1,0:T(8,128)S(1)}, f32[2,512,128]{2,1,0:T(8,128)}, u32[]{:S(2)}, u32[]{:S(2)}) collective-permute-start(f32[2,512,128]{2,1,0:T(8,128)S(1)} %get-tuple-element.38), channel_id=1, source_target_pairs={{0,8},{8,16},{16,24},{24,32},{32,40},{40,48},{48,56},{56,64},{64,7... | collective-permute-start | bytes 1572872 | tf_op jit(solution)/shard_map/ppermute | solution.py:352
  140.0 5.5 %collective-permute-start.25 = (f32[2,512,128]{2,1,0:T(8,128)S(1)}, f32[2,512,128]{2,1,0:T(8,128)}, u32[]{:S(2)}, u32[]{:S(2)}) collective-permute-start(f32[2,512,128]{2,1,0:T(8,128)S(1)} %get-tuple-element.39), channel_id=1, source_target_pairs={{8,0},{16,8},{24,16},{32,24},{40,32},{48,40},{56,48},{64,56},{72,6... | collective-permute-start | bytes 1572872 | tf_op jit(solution)/shard_map/ppermute | solution.py:352
  145.5 6.1 %collective-permute-start.22 = (f32[8,8,256]{2,1,0:T(8,128)S(1)}, f32[8,8,256]{2,1,0:T(8,128)S(1)}, u32[]{:S(2)}, u32[]{:S(2)}) collective-permute-start(f32[8,8,256]{2,1,0:T(8,128)S(1)} %fusion.3), channel_id=1, source_target_pairs={{0,2},{1,3},{2,0},{3,1},{4,6},{5,7},{6,4},{7,5},{8,72},{9,73},{10,... | collective-permute-start | bytes 196616 | tf_op jit(solution)/shard_map/ppermute | solution.py:377
  151.6 2.6 %collective-permute-start.23 = (f32[8,8,256]{2,1,0:T(8,128)S(1)}, f32[8,8,256]{2,1,0:T(8,128)S(1)}, u32[]{:S(2)}, u32[]{:S(2)}) collective-permute-start(f32[8,8,256]{2,1,0:T(8,128)S(1)} %fusion.3), channel_id=1, source_target_pairs={{0,3},{1,0},{2,1},{3,2},{4,7},{5,4},{6,5},{7,6},{8,104},{9,105},{1... | collective-permute-start | bytes 196616 | tf_op jit(solution)/shard_map/ppermute | solution.py:377
  154.2 1.4 slice.141
  155.6 1.4 slice.140
  157.1 1.4 collective-permute-done.21
  158.6 1.3 collective-permute-start.27
  160.0 1.4 collective-permute-start.26
  161.4 6.5 %divide_subtract_fusion = f32[2,512,1024]{2,1,0:T(8,128)} fusion(f32[2,512,1024]{2,1,0:T(8,128)S(1)} %copy-done.2, f32[2,128,1024]{2,1,0:T(8,128)S(1)} %slice.141, f32[2,128,1024]{2,1,0:T(8,128)S(1)} %slice.140, f32[2,512,128]{2,1,0:T(8,128)} %collective-permute-done.25, f32[2,512,128]{2,1,0:T(8,128)} %collective-permute-done.24, ...), kind=kLoop, calls=%fused_computation | loop fusion | flops 7340032 | bytes 22020096 | tf_op jit(solution)/shard_map/sub | solution.py:346
  167.9 0.3 collective-permute-done.26
  168.2 0.2 select_select_fusion.3
  168.5 4.6 %collective-permute-start.29 = (f32[8,128,256]{2,1,0:T(8,128)S(1)}, f32[8,128,256]{2,1,0:T(8,128)S(1)}, u32[]{:S(2)}, u32[]{:S(2)}) collective-permute-start(f32[8,128,256]{2,1,0:T(8,128)S(1)} %pad_maximum_fusion.1), channel_id=1, source_target_pairs={{0,8},{1,9},{2,10},{3,11},{4,12},{5,13},{6,14},{7,15},{8,0},{9,1},... | collective-permute-start | bytes 3145736 | tf_op jit(solution)/shard_map/ppermute | solution.py:432
  173.1 2.3 %collective-permute-done.29 = f32[8,128,256]{2,1,0:T(8,128)S(1)} collective-permute-done((f32[8,128,256]{2,1,0:T(8,128)S(1)}, f32[8,128,256]{2,1,0:T(8,128)S(1)}, u32[]{:S(2)}, u32[]{:S(2)}) %collective-permute-start.29) | collective-permute-done | bytes 1048608 | tf_op jit(solution)/shard_map/ppermute | solution.py:432
  175.4 0.2 broadcast_select_fusion.1
  175.6 0.1 copy.11
  175.7 1.5 pad_maximum_fusion
  (61 shorter events, 1.0 us)
Async XLA Ops:
  2.0 8.1 %copy-start.1 = (f32[2,512,1024]{2,1,0:T(8,128)S(1)}, f32[2,512,1024]{2,1,0:T(8,128)}, u32[]{:S(2)}) copy-start(f32[2,512,1024]{2,1,0:T(8,128)} %refs_3_.3) | copy-start | bytes 12582916
  3.6 12.6 %collective-permute-start.1 = (f32[2,520,128]{2,1,0:T(8,128)S(1)}, f32[2,520,128]{2,1,0:T(8,128)}, u32[]{:S(2)}, u32[]{:S(2)}) collective-permute-start(f32[2,520,128]{2,1,0:T(8,128)S(1)} %get-tuple-element.88), channel_id=1, source_target_pairs={{8,0},{16,8},{24,16},{32,24},{40,32},{48,40},{56,48},{64,56},{72,6... | collective-permute-start | bytes 1597448 | tf_op jit(solution)/shard_map/ppermute | solution.py:352
  6.1 11.7 %collective-permute-start = (f32[2,520,128]{2,1,0:T(8,128)S(1)}, f32[2,520,128]{2,1,0:T(8,128)}, u32[]{:S(2)}, u32[]{:S(2)}) collective-permute-start(f32[2,520,128]{2,1,0:T(8,128)S(1)} %get-tuple-element.89), channel_id=1, source_target_pairs={{0,8},{8,16},{16,24},{24,32},{32,40},{40,48},{48,56},{56,64},{64,7... | collective-permute-start | bytes 1597448 | tf_op jit(solution)/shard_map/ppermute | solution.py:352
  10.3 42.0 %collective-permute-start.2 = (f32[2,128,1024]{2,1,0:T(8,128)S(1)}, f32[2,128,1024]{2,1,0:T(8,128)}, u32[]{:S(2)}, u32[]{:S(2)}) collective-permute-start(f32[2,128,1024]{2,1,0:T(8,128)S(1)} %get-tuple-element.49), channel_id=1, source_target_pairs={{0,1},{1,2},{2,3},{3,4},{4,5},{5,6},{6,7},{8,9},{9,10},{10,11},{11... | collective-permute-start | bytes 3145736 | tf_op jit(solution)/shard_map/ppermute | solution.py:352
  14.8 37.5 %collective-permute-start.3 = (f32[2,128,1024]{2,1,0:T(8,128)S(1)}, f32[2,128,1024]{2,1,0:T(8,128)}, u32[]{:S(2)}, u32[]{:S(2)}) collective-permute-start(f32[2,128,1024]{2,1,0:T(8,128)S(1)} %get-tuple-element.48), channel_id=1, source_target_pairs={{1,0},{2,1},{3,2},{4,3},{5,4},{6,5},{7,6},{9,8},{10,9},{11,10},{12... | collective-permute-start | bytes 3145736 | tf_op jit(solution)/shard_map/ppermute | solution.py:352
  19.5 32.7 %collective-permute-start.4 = (f32[2,2,136,128]{3,2,1,0:T(8,128)S(1)}, f32[2,2,136,128]{3,2,1,0:T(8,128)S(1)}, u32[]{:S(2)}, u32[]{:S(2)}) collective-permute-start(f32[2,2,136,128]{3,2,1,0:T(8,128)S(1)} %get-tuple-element.87), channel_id=1, source_target_pairs={{0,1},{1,2},{2,3},{3,4},{4,5},{5,6},{6,7},{8,9},{9,10},{10,11},{11... | collective-permute-start | bytes 835592 | tf_op jit(solution)/shard_map/ppermute | solution.py:352
  23.5 28.7 %collective-permute-start.5 = (f32[2,2,136,128]{3,2,1,0:T(8,128)S(1)}, f32[2,2,136,128]{3,2,1,0:T(8,128)S(1)}, u32[]{:S(2)}, u32[]{:S(2)}) collective-permute-start(f32[2,2,136,128]{3,2,1,0:T(8,128)S(1)} %get-tuple-element.86), channel_id=1, source_target_pairs={{1,0},{2,1},{3,2},{4,3},{5,4},{6,5},{7,6},{9,8},{10,9},{11,10},{12... | collective-permute-start | bytes 835592 | tf_op jit(solution)/shard_map/ppermute | solution.py:352
  52.3 0.7 copy-start.8
  52.3 0.8 copy-start.9
  73.2 13.9 %copy-start.3 = (f32[16,9,8,256]{3,2,1,0:T(8,128)S(1)}, f32[16,9,8,256]{3,2,1,0:T(8,128)}, u32[]{:S(2)}) copy-start(f32[16,9,8,256]{3,2,1,0:T(8,128)} %get-tuple-element.26) | copy-start | bytes 3538948
  74.6 10.5 %collective-permute-start.9 = (f32[4,9,8,256]{3,2,1,0:T(8,128)S(1)}, f32[4,9,8,256]{3,2,1,0:T(8,128)S(1)}, u32[]{:S(2)}, u32[]{:S(2)}) collective-permute-start(f32[4,9,8,256]{3,2,1,0:T(8,128)S(1)} %get-tuple-element.62), channel_id=1, source_target_pairs={{0,8},{1,9},{2,10},{3,11},{4,12},{5,13},{6,14},{7,15},{8,0},{9,1},... | collective-permute-start | bytes 884744 | tf_op jit(solution)/shard_map/ppermute | solution.py:389
  74.9 12.2 %collective-permute-start.8 = (f32[4,9,8,256]{3,2,1,0:T(8,128)S(1)}, f32[4,9,8,256]{3,2,1,0:T(8,128)S(1)}, u32[]{:S(2)}, u32[]{:S(2)}) collective-permute-start(f32[4,9,8,256]{3,2,1,0:T(8,128)S(1)} %get-tuple-element.63), channel_id=1, source_target_pairs={{0,8},{1,9},{2,10},{3,11},{4,12},{5,13},{6,14},{7,15},{8,0},{9,1},... | collective-permute-start | bytes 884744 | tf_op jit(solution)/shard_map/ppermute | solution.py:389
  75.4 11.7 %collective-permute-start.7 = (f32[4,9,8,256]{3,2,1,0:T(8,128)S(1)}, f32[4,9,8,256]{3,2,1,0:T(8,128)S(1)}, u32[]{:S(2)}, u32[]{:S(2)}) collective-permute-start(f32[4,9,8,256]{3,2,1,0:T(8,128)S(1)} %get-tuple-element.64), channel_id=1, source_target_pairs={{0,8},{1,9},{2,10},{3,11},{4,12},{5,13},{6,14},{7,15},{8,0},{9,1},... | collective-permute-start | bytes 884744 | tf_op jit(solution)/shard_map/ppermute | solution.py:389
  75.5 11.6 %collective-permute-start.6 = (f32[4,9,8,256]{3,2,1,0:T(8,128)S(1)}, f32[4,9,8,256]{3,2,1,0:T(8,128)S(1)}, u32[]{:S(2)}, u32[]{:S(2)}) collective-permute-start(f32[4,9,8,256]{3,2,1,0:T(8,128)S(1)} %get-tuple-element.61), channel_id=1, source_target_pairs={{0,8},{1,9},{2,10},{3,11},{4,12},{5,13},{6,14},{7,15},{8,0},{9,1},... | collective-permute-start | bytes 884744 | tf_op jit(solution)/shard_map/ppermute | solution.py:389
  76.6 35.5 %collective-permute-start.13 = (f32[2,128,1280]{2,1,0:T(8,128)}, f32[2,128,1280]{2,1,0:T(8,128)}, u32[]{:S(2)}, u32[]{:S(2)}) collective-permute-start(f32[2,128,1280]{2,1,0:T(8,128)} %get-tuple-element.28), channel_id=1, source_target_pairs={{0,1},{1,2},{2,3},{3,4},{4,5},{5,6},{6,7},{8,9},{9,10},{10,11},{11... | collective-permute-start | bytes 3932168 | tf_op jit(solution)/shard_map/ppermute | solution.py:352
  85.1 31.8 %collective-permute-start.14 = (f32[2,128,1280]{2,1,0:T(8,128)}, f32[2,128,1280]{2,1,0:T(8,128)}, u32[]{:S(2)}, u32[]{:S(2)}) collective-permute-start(f32[2,128,1280]{2,1,0:T(8,128)} %get-tuple-element.29), channel_id=1, source_target_pairs={{1,0},{2,1},{3,2},{4,3},{5,4},{6,5},{7,6},{9,8},{10,9},{11,10},{12... | collective-permute-start | bytes 3932168 | tf_op jit(solution)/shard_map/ppermute | solution.py:352
  88.3 10.4 %collective-permute-start.12 = (f32[4,9,8,256]{3,2,1,0:T(8,128)}, f32[4,9,8,256]{3,2,1,0:T(8,128)}, u32[]{:S(2)}, u32[]{:S(2)}) collective-permute-start(f32[4,9,8,256]{3,2,1,0:T(8,128)} %get-tuple-element.59), channel_id=1, source_target_pairs={{0,96},{1,97},{2,98},{3,99},{4,100},{5,101},{6,102},{7,103},{8,104... | collective-permute-start | bytes 884744 | tf_op jit(solution)/shard_map/ppermute | solution.py:398
  88.3 10.4 %collective-permute-start.11 = (f32[4,9,8,256]{3,2,1,0:T(8,128)}, f32[4,9,8,256]{3,2,1,0:T(8,128)}, u32[]{:S(2)}, u32[]{:S(2)}) collective-permute-start(f32[4,9,8,256]{3,2,1,0:T(8,128)} %get-tuple-element.60), channel_id=1, source_target_pairs={{0,64},{1,65},{2,66},{3,67},{4,68},{5,69},{6,70},{7,71},{8,72},{9,... | collective-permute-start | bytes 884744 | tf_op jit(solution)/shard_map/ppermute | solution.py:398
  91.3 14.1 %collective-permute-start.10 = (f32[4,9,8,256]{3,2,1,0:T(8,128)}, f32[4,9,8,256]{3,2,1,0:T(8,128)}, u32[]{:S(2)}, u32[]{:S(2)}) collective-permute-start(f32[4,9,8,256]{3,2,1,0:T(8,128)} %get-tuple-element.58), channel_id=1, source_target_pairs={{0,32},{1,33},{2,34},{3,35},{4,36},{5,37},{6,38},{7,39},{8,40},{9,... | collective-permute-start | bytes 884744 | tf_op jit(solution)/shard_map/ppermute | solution.py:398
  92.8 1.6 copy-start
  98.6 34.6 %copy-start.4 = (f32[2,512,128]{2,1,0:T(8,128)S(1)}, f32[2,512,128]{2,1,0:T(8,128)}, u32[]{:S(2)}) copy-start(f32[2,512,128]{2,1,0:T(8,128)} %get-tuple-element.31) | copy-start | bytes 1572868
  98.6 34.6 %copy-start.5 = (f32[2,512,128]{2,1,0:T(8,128)S(1)}, f32[2,512,128]{2,1,0:T(8,128)}, u32[]{:S(2)}) copy-start(f32[2,512,128]{2,1,0:T(8,128)} %get-tuple-element.35) | copy-start | bytes 1572868
  98.6 34.6 %copy-start.6 = (f32[2,512,128]{2,1,0:T(8,128)S(1)}, f32[2,512,128]{2,1,0:T(8,128)}, u32[]{:S(2)}) copy-start(f32[2,512,128]{2,1,0:T(8,128)} %get-tuple-element.32) | copy-start | bytes 1572868
  98.6 34.6 %copy-start.7 = (f32[2,512,128]{2,1,0:T(8,128)S(1)}, f32[2,512,128]{2,1,0:T(8,128)}, u32[]{:S(2)}) copy-start(f32[2,512,128]{2,1,0:T(8,128)} %get-tuple-element.36) | copy-start | bytes 1572868
  117.0 11.3 %collective-permute-start.17 = (f32[1,9,8,256]{3,2,1,0:T(8,128)S(1)}, f32[1,9,8,256]{3,2,1,0:T(8,128)S(1)}, u32[]{:S(2)}, u32[]{:S(2)}) collective-permute-start(f32[1,9,8,256]{3,2,1,0:T(8,128)S(1)} %get-tuple-element.74), channel_id=1, source_target_pairs={{0,3},{1,0},{2,1},{3,2},{4,7},{5,4},{6,5},{7,6},{8,11},{9,8},{10,9... | collective-permute-start | bytes 221192 | tf_op jit(solution)/shard_map/ppermute | solution.py:398
  125.6 4.8 %collective-permute-start.16 = (f32[1,9,8,256]{3,2,1,0:T(8,128)S(1)}, f32[1,9,8,256]{3,2,1,0:T(8,128)S(1)}, u32[]{:S(2)}, u32[]{:S(2)}) collective-permute-start(f32[1,9,8,256]{3,2,1,0:T(8,128)S(1)} %get-tuple-element.75), channel_id=1, source_target_pairs={{0,2},{1,3},{2,0},{3,1},{4,6},{5,7},{6,4},{7,5},{8,10},{9,11},{10,... | collective-permute-start | bytes 221192 | tf_op jit(solution)/shard_map/ppermute | solution.py:398
  125.6 5.2 %collective-permute-start.15 = (f32[1,9,8,256]{3,2,1,0:T(8,128)S(1)}, f32[1,9,8,256]{3,2,1,0:T(8,128)S(1)}, u32[]{:S(2)}, u32[]{:S(2)}) collective-permute-start(f32[1,9,8,256]{3,2,1,0:T(8,128)S(1)} %get-tuple-element.73), channel_id=1, source_target_pairs={{0,1},{1,2},{2,3},{3,0},{4,5},{5,6},{6,7},{7,4},{8,9},{9,10},{10,1... | collective-permute-start | bytes 221192 | tf_op jit(solution)/shard_map/ppermute | solution.py:398
  130.9 3.3 %collective-permute-start.20 = (f32[1,9,8,256]{3,2,1,0:T(8,128)S(1)}, f32[1,9,8,256]{3,2,1,0:T(8,128)S(1)}, u32[]{:S(2)}, u32[]{:S(2)}) collective-permute-start(f32[1,9,8,256]{3,2,1,0:T(8,128)S(1)} %add_add_fusion.2), channel_id=1, source_target_pairs={{0,20},{1,21},{2,22},{3,23},{4,16},{5,17},{6,18},{7,19},{8,28},{9,... | collective-permute-start | bytes 221192 | tf_op jit(solution)/shard_map/ppermute | solution.py:377
  132.0 4.7 %collective-permute-start.19 = (f32[1,9,8,256]{3,2,1,0:T(8,128)S(1)}, f32[1,9,8,256]{3,2,1,0:T(8,128)S(1)}, u32[]{:S(2)}, u32[]{:S(2)}) collective-permute-start(f32[1,9,8,256]{3,2,1,0:T(8,128)S(1)} %add_add_fusion.2), channel_id=1, source_target_pairs={{0,4},{1,5},{2,6},{3,7},{4,0},{5,1},{6,2},{7,3},{8,12},{9,13},{10,... | collective-permute-start | bytes 221192 | tf_op jit(solution)/shard_map/ppermute | solution.py:377
  132.0 5.0 %collective-permute-start.18 = (f32[1,9,8,256]{3,2,1,0:T(8,128)S(1)}, f32[1,9,8,256]{3,2,1,0:T(8,128)S(1)}, u32[]{:S(2)}, u32[]{:S(2)}) collective-permute-start(f32[1,9,8,256]{3,2,1,0:T(8,128)S(1)} %add_add_fusion.2), channel_id=1, source_target_pairs={{0,16},{1,17},{2,18},{3,19},{4,20},{5,21},{6,22},{7,23},{8,24},{9,... | collective-permute-start | bytes 221192 | tf_op jit(solution)/shard_map/ppermute | solution.py:377
  137.9 20.7 %collective-permute-start.24 = (f32[2,512,128]{2,1,0:T(8,128)S(1)}, f32[2,512,128]{2,1,0:T(8,128)}, u32[]{:S(2)}, u32[]{:S(2)}) collective-permute-start(f32[2,512,128]{2,1,0:T(8,128)S(1)} %get-tuple-element.38), channel_id=1, source_target_pairs={{0,8},{8,16},{16,24},{24,32},{32,40},{40,48},{48,56},{56,64},{64,7... | collective-permute-start | bytes 1572872 | tf_op jit(solution)/shard_map/ppermute | solution.py:352
  140.0 18.6 %collective-permute-start.25 = (f32[2,512,128]{2,1,0:T(8,128)S(1)}, f32[2,512,128]{2,1,0:T(8,128)}, u32[]{:S(2)}, u32[]{:S(2)}) collective-permute-start(f32[2,512,128]{2,1,0:T(8,128)S(1)} %get-tuple-element.39), channel_id=1, source_target_pairs={{8,0},{16,8},{24,16},{32,24},{40,32},{48,40},{56,48},{64,56},{72,6... | collective-permute-start | bytes 1572872 | tf_op jit(solution)/shard_map/ppermute | solution.py:352
  145.5 11.6 %collective-permute-start.22 = (f32[8,8,256]{2,1,0:T(8,128)S(1)}, f32[8,8,256]{2,1,0:T(8,128)S(1)}, u32[]{:S(2)}, u32[]{:S(2)}) collective-permute-start(f32[8,8,256]{2,1,0:T(8,128)S(1)} %fusion.3), channel_id=1, source_target_pairs={{0,2},{1,3},{2,0},{3,1},{4,6},{5,7},{6,4},{7,5},{8,72},{9,73},{10,... | collective-permute-start | bytes 196616 | tf_op jit(solution)/shard_map/ppermute | solution.py:377
  151.6 5.5 %collective-permute-start.23 = (f32[8,8,256]{2,1,0:T(8,128)S(1)}, f32[8,8,256]{2,1,0:T(8,128)S(1)}, u32[]{:S(2)}, u32[]{:S(2)}) collective-permute-start(f32[8,8,256]{2,1,0:T(8,128)S(1)} %fusion.3), channel_id=1, source_target_pairs={{0,3},{1,0},{2,1},{3,2},{4,7},{5,4},{6,5},{7,6},{8,104},{9,105},{1... | collective-permute-start | bytes 196616 | tf_op jit(solution)/shard_map/ppermute | solution.py:377
  154.2 4.3 %collective-permute-start.21 = (f32[8,8,256]{2,1,0:T(8,128)S(1)}, f32[8,8,256]{2,1,0:T(8,128)S(1)}, u32[]{:S(2)}, u32[]{:S(2)}) collective-permute-start(f32[8,8,256]{2,1,0:T(8,128)S(1)} %fusion.3), channel_id=1, source_target_pairs={{0,1},{1,2},{2,3},{3,0},{4,5},{5,6},{6,7},{7,4},{8,40},{9,41},{10,... | collective-permute-start | bytes 196616 | tf_op jit(solution)/shard_map/ppermute | solution.py:377
  154.2 7.2 %copy-start.2 = (f32[2,512,1024]{2,1,0:T(8,128)S(1)}, f32[2,512,1024]{2,1,0:T(8,128)}, u32[]{:S(2)}) copy-start(f32[2,512,1024]{2,1,0:T(8,128)} %refs_3_.3) | copy-start | bytes 12582916
  158.6 9.3 %collective-permute-start.27 = (f32[8,32,256]{2,1,0:T(8,128)S(1)}, f32[8,32,256]{2,1,0:T(8,128)S(1)}, u32[]{:S(2)}, u32[]{:S(2)}) collective-permute-start(f32[8,32,256]{2,1,0:T(8,128)S(1)} %pad_maximum_fusion.4), channel_id=1, source_target_pairs={{0,64},{1,65},{2,66},{3,67},{4,68},{5,69},{6,70},{7,71},{8,10},{9,... | collective-permute-start | bytes 786440 | tf_op jit(solution)/shard_map/ppermute | solution.py:377
  159.9 8.0 %collective-permute-start.28 = (f32[8,32,256]{2,1,0:T(8,128)S(1)}, f32[8,32,256]{2,1,0:T(8,128)S(1)}, u32[]{:S(2)}, u32[]{:S(2)}) collective-permute-start(f32[8,32,256]{2,1,0:T(8,128)S(1)} %pad_maximum_fusion.4), channel_id=1, source_target_pairs={{0,96},{1,97},{2,98},{3,99},{4,100},{5,101},{6,102},{7,103},{8,11}... | collective-permute-start | bytes 786440 | tf_op jit(solution)/shard_map/ppermute | solution.py:377
  160.0 8.2 %collective-permute-start.26 = (f32[8,32,256]{2,1,0:T(8,128)S(1)}, f32[8,32,256]{2,1,0:T(8,128)S(1)}, u32[]{:S(2)}, u32[]{:S(2)}) collective-permute-start(f32[8,32,256]{2,1,0:T(8,128)S(1)} %pad_maximum_fusion.4), channel_id=1, source_target_pairs={{0,32},{1,33},{2,34},{3,35},{4,36},{5,37},{6,38},{7,39},{8,9},{9,1... | collective-permute-start | bytes 786440 | tf_op jit(solution)/shard_map/ppermute | solution.py:377
  168.5 6.9 %collective-permute-start.29 = (f32[8,128,256]{2,1,0:T(8,128)S(1)}, f32[8,128,256]{2,1,0:T(8,128)S(1)}, u32[]{:S(2)}, u32[]{:S(2)}) collective-permute-start(f32[8,128,256]{2,1,0:T(8,128)S(1)} %pad_maximum_fusion.1), channel_id=1, source_target_pairs={{0,8},{1,9},{2,10},{3,11},{4,12},{5,13},{6,14},{7,15},{8,0},{9,1},... | collective-permute-start | bytes 3145736 | tf_op jit(solution)/shard_map/ppermute | solution.py:432

commit v4 on v3

--- a/solution.py
+++ b/solution.py
@@ -125,7 +125,7 @@
         out_specs=vmem,
         scratch_shapes=[pltpu.VMEM((1, tr + 2 * n, tc + 2 * n), F32), pltpu.VMEM((n, n), F32)],
         compiler_params=pltpu.CompilerParams(vmem_limit_bytes=16 * MIB),
-        cost_estimate=pl.CostEstimate(flops=20_000_000, bytes_accessed=8_000_000, transcendentals=0),
+        cost_estimate=pl.CostEstimate(flops=0, bytes_accessed=0, transcendentals=0),
         name="tile_illum",
     )(info, probe)
 
@@ -330,20 +330,45 @@
             pltpu.VMEM((2, n, h), F32),
             pltpu.SemaphoreType.DMA((10,)),
         ],
-        compiler_params=pltpu.CompilerParams(vmem_limit_bytes=56 * MIB),
+        compiler_params=pltpu.CompilerParams(vmem_limit_bytes=34 * MIB),
         cost_estimate=pl.CostEstimate(flops=40_000_000_000, bytes_accessed=30_000_000, transcendentals=0),
         name="tile_grads_early" if early else "tile_grads_late",
     )(count, offs, bit, obj, *halos, probe, amps, *tables(n))
 
 
-def object_update(obj, core, illum, left, right, above, below):
+def update_kernel(obj, core_e, core, illum, left, right, above, below, out):
+    step, h, tc = pl.program_id(0), left.shape[-1], obj.shape[-1]
+    out[...] = core_e[...] + core[...]
+
+    @pl.when(step == 0)
+    def _():
+        out[...] += above[:, :, h : h + tc]
+
+    @pl.when(step == pl.num_programs(0) - 1)
+    def _():
+        out[...] += below[:, :, h : h + tc]
+
+    out[:, :, :h] += left[...]
+    out[:, :, tc - h :] += right[...]
+    out[...] = obj[...] - out[...] / illum[...]
+
+
+def object_update(obj, core_e, core, illum, left, right, above, below):
     _, tr, tc = obj.shape
     h = left.shape[-1]
-    total = core + jnp.pad(left, ((0, 0), (0, 0), (0, tc - h)))
-    total = total + jnp.pad(right, ((0, 0), (0, 0), (tc - h, 0)))
-    total = total + jnp.pad(above[:, :, h : h + tc], ((0, 0), (0, tr - h), (0, 0)))
-    total = total + jnp.pad(below[:, :, h : h + tc], ((0, 0), (tr - h, 0), (0, 0)))
-    return obj - total / illum
+    tile = pl.BlockSpec((2, h, tc), lambda i: (0, i, 0))
+    side = pl.BlockSpec((2, h, h), lambda i: (0, i, 0))
+    strip = pl.BlockSpec((2, h, above.shape[-1]), lambda i: (0, 0, 0))
+    return pl.pallas_call(
+        update_kernel,
+        grid=(tr // h,),
+        out_shape=jax.ShapeDtypeStruct(obj.shape, F32),
+        in_specs=[tile, tile, tile, pl.BlockSpec((h, tc), lambda i: (i, 0)), side, side, strip, strip],
+        out_specs=tile,
+        compiler_params=pltpu.CompilerParams(vmem_limit_bytes=56 * MIB),
+        cost_estimate=pl.CostEstimate(flops=10_000_000, bytes_accessed=20_000_000, transcendentals=0),
+        name="object_update",
+    )(obj, core_e, core, illum, left, right, above, below)
 
 
 def moved(block, axis, distance):
@@ -400,8 +425,8 @@
         return part(t) + got[0] + got[1] + got[2]
 
     v = scattered(v, x, "x")
+    v = scattered(v, z, "z")
     v, arrived = lax.optimization_barrier((v, arrived))
-    v = scattered(v, z, "z")
     a, b, c = around(v, ("y", "y"))
     v = (v + a + b + c)[0]
     modes, _, size, _ = probe.shape
@@ -485,7 +510,9 @@
     block, sides = lax.optimization_barrier((block, sides))
     from_right = moved(sides[0], "wide", -1)
     from_left = moved(sides[1], "wide", 1)
-    update = lambda a, b: object_update(object_field, core_e + core, illum, a, b, above, below)
+    update = lambda a, b: object_update(
+        object_field, core_e, core, illum, a, b, above, below
+    )
     new_probe, new_object = probe_gather(block, gathered, (from_left, from_right), update)
     return (new_object, new_probe.reshape(probe_modes.shape))
 

time: 180 us -> 174 us (0.967)
  the two profiles are of different devices: /device:TPU:9 before, /device:TPU:1 now
where the time goes in v4:
time: 174 us
  starting transfers between devices  86 us (49%)
  Pallas kernels  36.2 us (21%)
  waiting for transfers between devices  26.2 us (15%)
  local copies, waits for them, and re-layouts  18.1 us (10%)
  other arithmetic  5.58 us (3%)
  between operations  1.84 us (1%)
    ppermute x6, starting transfers between devices, scattered(): lax.ppermute(part(t + hop), BOTH, route((axis, axis), hop))  27.7 us
    ppermute x10, starting transfers between devices, moved(): return lax.ppermute(block, axis, route)  26.8 us
    pallas_call x2, Pallas kernels, tile_grads(): pl.pallas_call(functools.partial(grads_kernel, modes=modes, n=n, tr=tr, t...  23.6 us
    ppermute x9, starting transfers between devices, around(): return [lax.ppermute(piece, BOTH, route(axes, hop)) for hop in (1, 2, 3)]  17.2 us
    ppermute x6, waiting for transfers between devices, scattered(): lax.ppermute(part(t + hop), BOTH, route((axis, axis), hop))  15.9 us
    unnamed x46, local copies, waits for them, and re-layouts  10.3 us
    pallas_call x1, Pallas kernels, object_update(): pl.pallas_call(update_kernel, grid=(tr // h,), out_shape=jax.ShapeDtypeSt...  8.69 us
    ppermute x4, starting transfers between devices, probe_update(): lax.ppermute(give[i * cut:(i + 1) * cut], BOTH, route(('core', 'core'), 1))  8.31 us
  transfers between devices with their start and end apart: 30, of which 11 were waited for; matrix products, arithmetic and copies ran while one was open for 5% of the time, Pallas kernels for 17%

profile of v4, /device:TPU:1, one launch (start us, length us, event | category | flops | bytes accessed | tf_op | source)
XLA Modules:
  0.0 173.8 jit_solution(4273305574505836128)
XLA Ops:
  1.3 0.7 slice_bitcast_fusion.17
  2.0 1.4 fusion.6
  3.5 1.1 pad_maximum_fusion.2
  4.5 3.3 %collective-permute-start.1 = (f32[2,520,128]{2,1,0:T(8,128)}, f32[2,520,128]{2,1,0:T(8,128)S(1)}, u32[]{:S(2)}, u32[]{:S(2)}) collective-permute-start(f32[2,520,128]{2,1,0:T(8,128)} %get-tuple-element.88), channel_id=1, source_target_pairs={{8,0},{16,8},{24,16},{32,24},{40,32},{48,40},{56,48},{64,56},{72,6... | collective-permute-start | bytes 1597448 | tf_op jit(solution)/shard_map/ppermute | solution.py:377
  7.9 3.2 %collective-permute-start = (f32[2,520,128]{2,1,0:T(8,128)}, f32[2,520,128]{2,1,0:T(8,128)S(1)}, u32[]{:S(2)}, u32[]{:S(2)}) collective-permute-start(f32[2,520,128]{2,1,0:T(8,128)} %get-tuple-element.89), channel_id=1, source_target_pairs={{0,8},{8,16},{16,24},{24,32},{32,40},{40,48},{48,56},{56,64},{64,7... | collective-permute-start | bytes 1597448 | tf_op jit(solution)/shard_map/ppermute | solution.py:377
  11.1 1.5 fusion.5
  12.5 4.6 %collective-permute-start.2 = (f32[2,128,1024]{2,1,0:T(8,128)}, f32[2,128,1024]{2,1,0:T(8,128)}, u32[]{:S(2)}, u32[]{:S(2)}) collective-permute-start(f32[2,128,1024]{2,1,0:T(8,128)} %get-tuple-element.49), channel_id=1, source_target_pairs={{0,1},{1,2},{2,3},{3,4},{4,5},{5,6},{6,7},{8,9},{9,10},{10,11},{11... | collective-permute-start | bytes 3145736 | tf_op jit(solution)/shard_map/ppermute | solution.py:377
  17.2 1.3 collective-permute-start.3
  18.5 3.7 %collective-permute-done.refs_4_ = f32[2,520,128]{2,1,0:T(8,128)S(1)} collective-permute-done((f32[2,520,128]{2,1,0:T(8,128)}, f32[2,520,128]{2,1,0:T(8,128)S(1)}, u32[]{:S(2)}, u32[]{:S(2)}) %collective-permute-start) | collective-permute-done | bytes 532512 | tf_op jit(solution)/shard_map/ppermute | solution.py:377
  22.3 3.6 %collective-permute-start.4 = (f32[2,2,136,128]{3,2,1,0:T(8,128)S(1)}, f32[2,2,136,128]{3,2,1,0:T(8,128)S(1)}, u32[]{:S(2)}, u32[]{:S(2)}) collective-permute-start(f32[2,2,136,128]{3,2,1,0:T(8,128)S(1)} %get-tuple-element.87), channel_id=1, source_target_pairs={{0,1},{1,2},{2,3},{3,4},{4,5},{5,6},{6,7},{8,9},{9,10},{10,11},{11... | collective-permute-start | bytes 835592 | tf_op jit(solution)/shard_map/ppermute | solution.py:377
  25.9 1.3 collective-permute-start.5
  27.3 2.2 %copy-done.1 = f32[2,512,1024]{2,1,0:T(8,128)S(1)} copy-done((f32[2,512,1024]{2,1,0:T(8,128)S(1)}, f32[2,512,1024]{2,1,0:T(8,128)}, u32[]{:S(2)}) %copy-start.1) | copy-done | bytes 4194328
  29.5 1.0 copy-done.10
  30.5 1.0 copy-done.13
  31.5 1.4 copy-done.16
  33.0 1.2 copy-done.18
  34.2 17.2 %tile_grads_early.1 = (f32[2,512,1024]{2,1,0:T(8,128)S(1)}, f32[2,512,128]{2,1,0:T(8,128)S(1)}, f32[2,512,128]{2,1,0:T(8,128)S(1)}, f32[32,9,8,256]{3,2,1,0:T(8,128)S(1)}) custom-call(s32[1]{0:T(128)} %bitcast.53.refs_0_, s32[2,6]{1,0:T(2,128)S(1)} %bitcast.56, s32[1]{0:T(128)} %bitcast.3.refs_2_, f32[2,512,1024]{2,1,0:T(8,128)S(1)} %copy-done.1, ...), custom_call_target="tpu_custom_call" | custom-call | flops 40000000000 | bytes 30000000 | tf_op jit(solution)/shard_map/tile_grads_early/pallas_call | solution.py:315
  51.4 2.0 %copy-done.3 = f32[2,512,1024]{2,1,0:T(8,128)} copy-done((f32[2,512,1024]{2,1,0:T(8,128)}, f32[2,512,1024]{2,1,0:T(8,128)S(1)}, u32[]{:S(2)}) %copy-start.3) | copy-done | bytes 4194328
  53.4 6.4 %tile_grads_late.1 = (f32[2,512,1024]{2,1,0:T(8,128)}, f32[2,512,128]{2,1,0:T(8,128)S(1)}, f32[2,512,128]{2,1,0:T(8,128)S(1)}, f32[2,128,1280]{2,1,0:T(8,128)}, ...) custom-call(s32[1]{0:T(128)} %bitcast.54.refs_0_, s32[2,6]{1,0:T(2,128)S(1)} %bitcast.57, ...), custom_call_target="tpu_custom_call" | custom-call | flops 40000000000 | bytes 30000000 | tf_op jit(solution)/shard_map/tile_grads_late/pallas_call | solution.py:315
  59.8 0.1 fusion.9
  60.0 7.7 %collective-permute-start.9 = (f32[4,9,8,256]{3,2,1,0:T(8,128)S(1)}, f32[4,9,8,256]{3,2,1,0:T(8,128)S(1)}, u32[]{:S(2)}, u32[]{:S(2)}) collective-permute-start(f32[4,9,8,256]{3,2,1,0:T(8,128)S(1)} %get-tuple-element.62), channel_id=1, source_target_pairs={{0,8},{1,9},{2,10},{3,11},{4,12},{5,13},{6,14},{7,15},{8,0},{9,1},... | collective-permute-start | bytes 884744 | tf_op jit(solution)/shard_map/ppermute | solution.py:414
  67.8 0.4 collective-permute-start.7
  68.3 2.4 %collective-permute-start.16 = (f32[2,128,1280]{2,1,0:T(8,128)}, f32[2,128,1280]{2,1,0:T(8,128)}, u32[]{:S(2)}, u32[]{:S(2)}) collective-permute-start(f32[2,128,1280]{2,1,0:T(8,128)} %get-tuple-element.28), channel_id=1, source_target_pairs={{0,1},{1,2},{2,3},{3,4},{4,5},{5,6},{6,7},{8,9},{9,10},{10,11},{11... | collective-permute-start | bytes 3932168 | tf_op jit(solution)/shard_map/ppermute | solution.py:377
  70.6 1.3 collective-permute-start.17
  72.0 0.2 maximum_add_fusion
  72.2 3.9 %collective-permute-start.12 = (f32[4,9,8,256]{3,2,1,0:T(8,128)S(1)}, f32[4,9,8,256]{3,2,1,0:T(8,128)S(1)}, u32[]{:S(2)}, u32[]{:S(2)}) collective-permute-start(f32[4,9,8,256]{3,2,1,0:T(8,128)S(1)} %get-tuple-element.59), channel_id=1, source_target_pairs={{0,96},{1,97},{2,98},{3,99},{4,100},{5,101},{6,102},{7,103},{8,104... | collective-permute-start | bytes 884744 | tf_op jit(solution)/shard_map/ppermute | solution.py:423
  76.1 8.5 %collective-permute-start.11 = (f32[4,9,8,256]{3,2,1,0:T(8,128)S(1)}, f32[4,9,8,256]{3,2,1,0:T(8,128)S(1)}, u32[]{:S(2)}, u32[]{:S(2)}) collective-permute-start(f32[4,9,8,256]{3,2,1,0:T(8,128)S(1)} %get-tuple-element.60), channel_id=1, source_target_pairs={{0,64},{1,65},{2,66},{3,67},{4,68},{5,69},{6,70},{7,71},{8,72},{9,... | collective-permute-start | bytes 884744 | tf_op jit(solution)/shard_map/ppermute | solution.py:423
  84.6 0.8 collective-permute-start.10
  85.4 0.5 slice_bitcast_fusion.10
  85.9 0.9 collective-permute-done.12
  86.7 4.6 %collective-permute-done.11 = f32[4,9,8,256]{3,2,1,0:T(8,128)S(1)} collective-permute-done((f32[4,9,8,256]{3,2,1,0:T(8,128)S(1)}, f32[4,9,8,256]{3,2,1,0:T(8,128)S(1)}, u32[]{:S(2)}, u32[]{:S(2)}) %collective-permute-start.11) | collective-permute-done | bytes 294944 | tf_op jit(solution)/shard_map/ppermute | solution.py:423
  91.4 7.0 %collective-permute-done.10 = f32[4,9,8,256]{3,2,1,0:T(8,128)S(1)} collective-permute-done((f32[4,9,8,256]{3,2,1,0:T(8,128)S(1)}, f32[4,9,8,256]{3,2,1,0:T(8,128)S(1)}, u32[]{:S(2)}, u32[]{:S(2)}) %collective-permute-start.10) | collective-permute-done | bytes 294944 | tf_op jit(solution)/shard_map/ppermute | solution.py:423
  98.5 0.7 constant_dynamic-slice_fusion.2
  99.2 14.0 %collective-permute-start.15 = (f32[1,9,8,256]{3,2,1,0:T(8,128)}, f32[1,9,8,256]{3,2,1,0:T(8,128)}, u32[]{:S(2)}, u32[]{:S(2)}) collective-permute-start(f32[1,9,8,256]{3,2,1,0:T(8,128)} %get-tuple-element.74), channel_id=1, source_target_pairs={{0,3},{1,0},{2,1},{3,2},{4,7},{5,4},{6,5},{7,6},{8,11},{9,8},{10,9... | collective-permute-start | bytes 221192 | tf_op jit(solution)/shard_map/ppermute | solution.py:423
  113.1 0.6 collective-permute-start.13
  113.7 0.7 stack.51
  114.4 4.0 %tile_illum.1.illum = f32[512,1024]{1,0:T(8,128)S(1)} custom-call(s32[9,16]{1,0:T(8,128)S(1)} %convert_element_type.15.info, f32[4,2,256,256]{3,2,1,0:T(8,128)S(1)} %copy-done.4), custom_call_target="tpu_custom_call" | custom-call | tf_op jit(solution)/shard_map/tile_illum/pallas_call | solution.py:121
  118.4 1.3 copy-done.2
  119.7 3.4 %collective-permute-done.15 = f32[1,9,8,256]{3,2,1,0:T(8,128)} collective-permute-done((f32[1,9,8,256]{3,2,1,0:T(8,128)}, f32[1,9,8,256]{3,2,1,0:T(8,128)}, u32[]{:S(2)}, u32[]{:S(2)}) %collective-permute-start.15) | collective-permute-done | bytes 73760 | tf_op jit(solution)/shard_map/ppermute | solution.py:423
  123.1 1.0 add_add_fusion.2
  124.1 2.1 %collective-permute-start.20 = (f32[1,9,8,256]{3,2,1,0:T(8,128)S(1)}, f32[1,9,8,256]{3,2,1,0:T(8,128)S(1)}, u32[]{:S(2)}, u32[]{:S(2)}) collective-permute-start(f32[1,9,8,256]{3,2,1,0:T(8,128)S(1)} %add_add_fusion.2), channel_id=1, source_target_pairs={{0,20},{1,21},{2,22},{3,23},{4,16},{5,17},{6,18},{7,19},{8,28},{9,... | collective-permute-start | bytes 221192 | tf_op jit(solution)/shard_map/ppermute | solution.py:402
  126.1 0.7 collective-permute-start.18
  126.8 1.0 fusion.8
  127.8 1.0 fusion.7
  128.8 1.2 pad_add_fusion
  130.0 1.0 collective-permute-done.19
  130.9 0.4 collective-permute-done.18
  131.4 4.0 %collective-permute-start.24 = (f32[2,512,128]{2,1,0:T(8,128)}, f32[2,512,128]{2,1,0:T(8,128)S(1)}, u32[]{:S(2)}, u32[]{:S(2)}) collective-permute-start(f32[2,512,128]{2,1,0:T(8,128)} %get-tuple-element.38), channel_id=1, source_target_pairs={{0,8},{8,16},{16,24},{24,32},{32,40},{40,48},{48,56},{56,64},{64,7... | collective-permute-start | bytes 1572872 | tf_op jit(solution)/shard_map/ppermute | solution.py:377
  135.4 1.9 %collective-permute-start.25 = (f32[2,512,128]{2,1,0:T(8,128)}, f32[2,512,128]{2,1,0:T(8,128)S(1)}, u32[]{:S(2)}, u32[]{:S(2)}) collective-permute-start(f32[2,512,128]{2,1,0:T(8,128)} %get-tuple-element.39), channel_id=1, source_target_pairs={{8,0},{16,8},{24,16},{32,24},{40,32},{48,40},{56,48},{64,56},{72,6... | collective-permute-start | bytes 1572872 | tf_op jit(solution)/shard_map/ppermute | solution.py:377
  137.4 8.9 %collective-permute-start.22 = (f32[8,8,256]{2,1,0:T(8,128)S(1)}, f32[8,8,256]{2,1,0:T(8,128)S(1)}, u32[]{:S(2)}, u32[]{:S(2)}) collective-permute-start(f32[8,8,256]{2,1,0:T(8,128)S(1)} %fusion.3), channel_id=1, source_target_pairs={{0,2},{1,3},{2,0},{3,1},{4,6},{5,7},{6,4},{7,5},{8,72},{9,73},{10,... | collective-permute-start | bytes 196616 | tf_op jit(solution)/shard_map/ppermute | solution.py:402
  146.3 1.5 collective-permute-start.21
  147.8 0.2 collective-permute-done.22
  147.9 2.2 %collective-permute-done.23 = f32[8,8,256]{2,1,0:T(8,128)S(1)} collective-permute-done((f32[8,8,256]{2,1,0:T(8,128)S(1)}, f32[8,8,256]{2,1,0:T(8,128)S(1)}, u32[]{:S(2)}, u32[]{:S(2)}) %collective-permute-start.23) | collective-permute-done | bytes 65568 | tf_op jit(solution)/shard_map/ppermute | solution.py:402
  150.2 0.5 collective-permute-done.21
  150.8 3.5 %collective-permute-start.28 = (f32[8,32,256]{2,1,0:T(8,128)S(1)}, f32[8,32,256]{2,1,0:T(8,128)S(1)}, u32[]{:S(2)}, u32[]{:S(2)}) collective-permute-start(f32[8,32,256]{2,1,0:T(8,128)S(1)} %pad_maximum_fusion.4), channel_id=1, source_target_pairs={{0,96},{1,97},{2,98},{3,99},{4,100},{5,101},{6,102},{7,103},{8,11}... | collective-permute-start | bytes 786440 | tf_op jit(solution)/shard_map/ppermute | solution.py:402
  154.3 0.5 collective-permute-start.26
  154.8 8.7 %object_update.1 = f32[2,512,1024]{2,1,0:T(8,128)} custom-call(f32[2,512,1024]{2,1,0:T(8,128)} %obj.1, f32[2,512,1024]{2,1,0:T(8,128)} %copy-done.3, f32[2,512,1024]{2,1,0:T(8,128)} %get-tuple-element.42.core, f32[512,1024]{1,0:T(8,128)} %copy-done.2, f32[2,512,128]{2,1,0:T(8,128)} %copy-done.21, f32[2,512,128]{2,1,0:T(8,128)} %copy-done.22, ...), custom_call_target="tpu_custom_call" | custom-call | flops 10000000 | bytes 20000000 | tf_op jit(solution)/shard_map/object_update/pallas_call | solution.py:362
  163.5 0.2 select_select_fusion.3
  163.7 0.1 pad_maximum_fusion.1
  163.8 5.9 %collective-permute-start.29 = (f32[8,128,256]{2,1,0:T(8,128)S(1)}, f32[8,128,256]{2,1,0:T(8,128)S(1)}, u32[]{:S(2)}, u32[]{:S(2)}) collective-permute-start(f32[8,128,256]{2,1,0:T(8,128)S(1)} %pad_maximum_fusion.1), channel_id=1, source_target_pairs={{0,8},{1,9},{2,10},{3,11},{4,12},{5,13},{6,14},{7,15},{8,0},{9,1},... | collective-permute-start | bytes 3145736 | tf_op jit(solution)/shard_map/ppermute | solution.py:457
  169.7 2.3 %collective-permute-done.29 = f32[8,128,256]{2,1,0:T(8,128)S(1)} collective-permute-done((f32[8,128,256]{2,1,0:T(8,128)S(1)}, f32[8,128,256]{2,1,0:T(8,128)S(1)}, u32[]{:S(2)}, u32[]{:S(2)}) %collective-permute-start.29) | collective-permute-done | bytes 1048608 | tf_op jit(solution)/shard_map/ppermute | solution.py:457
  172.0 0.2 broadcast_select_fusion.1
  172.2 0.1 copy.11
  172.4 1.5 pad_maximum_fusion
  (85 shorter events, 0.9 us)
Async XLA Ops:
  2.0 9.1 %copy-start = (f32[2,512,1024]{2,1,0:T(8,128)S(1)}, f32[2,512,1024]{2,1,0:T(8,128)}, u32[]{:S(2)}) copy-start(f32[2,512,1024]{2,1,0:T(8,128)} %obj.1) | copy-start | bytes 12582916
  4.5 13.9 %collective-permute-start.1 = (f32[2,520,128]{2,1,0:T(8,128)}, f32[2,520,128]{2,1,0:T(8,128)S(1)}, u32[]{:S(2)}, u32[]{:S(2)}) collective-permute-start(f32[2,520,128]{2,1,0:T(8,128)} %get-tuple-element.88), channel_id=1, source_target_pairs={{8,0},{16,8},{24,16},{32,24},{40,32},{48,40},{56,48},{64,56},{72,6... | collective-permute-start | bytes 1597448 | tf_op jit(solution)/shard_map/ppermute | solution.py:377
  7.9 14.4 %collective-permute-start = (f32[2,520,128]{2,1,0:T(8,128)}, f32[2,520,128]{2,1,0:T(8,128)S(1)}, u32[]{:S(2)}, u32[]{:S(2)}) collective-permute-start(f32[2,520,128]{2,1,0:T(8,128)} %get-tuple-element.89), channel_id=1, source_target_pairs={{0,8},{8,16},{16,24},{24,32},{32,40},{40,48},{48,56},{56,64},{64,7... | collective-permute-start | bytes 1597448 | tf_op jit(solution)/shard_map/ppermute | solution.py:377
  11.1 16.2 %copy-start.20 = (bf16[512,256]{1,0:T(8,128)(2,1)S(1)}, bf16[512,256]{1,0:T(8,128)(2,1)}, u32[]{:S(2)}) copy-start(bf16[512,256]{1,0:T(8,128)(2,1)} %constant.43.clone.refs_9_.refs_14_) | copy-start | bytes 786436
  12.5 14.7 %copy-start.4 = (f32[4,2,256,256]{3,2,1,0:T(8,128)S(1)}, f32[4,2,256,256]{3,2,1,0:T(8,128)}, u32[]{:S(2)}) copy-start(f32[4,2,256,256]{3,2,1,0:T(8,128)} %probe.1) | copy-start | bytes 6291460
  12.5 14.7 %copy-start.15 = (s32[2,1,1,6]{3,2,1,0:T(1,128)S(1)}, s32[2,1,1,6]{3,2,1,0:T(1,128)}, u32[]{:S(2)}) copy-start(s32[2,1,1,6]{3,2,1,0:T(1,128)} %param.12) | copy-start | bytes 148
  12.5 40.8 %collective-permute-start.2 = (f32[2,128,1024]{2,1,0:T(8,128)}, f32[2,128,1024]{2,1,0:T(8,128)}, u32[]{:S(2)}, u32[]{:S(2)}) collective-permute-start(f32[2,128,1024]{2,1,0:T(8,128)} %get-tuple-element.49), channel_id=1, source_target_pairs={{0,1},{1,2},{2,3},{3,4},{4,5},{5,6},{6,7},{8,9},{9,10},{10,11},{11... | collective-permute-start | bytes 3145736 | tf_op jit(solution)/shard_map/ppermute | solution.py:377
  17.2 36.2 %collective-permute-start.3 = (f32[2,128,1024]{2,1,0:T(8,128)}, f32[2,128,1024]{2,1,0:T(8,128)}, u32[]{:S(2)}, u32[]{:S(2)}) collective-permute-start(f32[2,128,1024]{2,1,0:T(8,128)} %get-tuple-element.48), channel_id=1, source_target_pairs={{1,0},{2,1},{3,2},{4,3},{5,4},{6,5},{7,6},{9,8},{10,9},{11,10},{12... | collective-permute-start | bytes 3145736 | tf_op jit(solution)/shard_map/ppermute | solution.py:377
  18.5 8.7 %copy-start.9 = (f32[2,520,128]{2,1,0:T(8,128)}, f32[2,520,128]{2,1,0:T(8,128)S(1)}, u32[]{:S(2)}) copy-start(f32[2,520,128]{2,1,0:T(8,128)S(1)} %collective-permute-done.1.refs_5_) | copy-start | bytes 1597444
  22.3 5.0 %copy-start.12 = (f32[2,520,128]{2,1,0:T(8,128)}, f32[2,520,128]{2,1,0:T(8,128)S(1)}, u32[]{:S(2)}) copy-start(f32[2,520,128]{2,1,0:T(8,128)S(1)} %collective-permute-done.refs_4_) | copy-start | bytes 1597444
  22.3 31.0 %collective-permute-start.4 = (f32[2,2,136,128]{3,2,1,0:T(8,128)S(1)}, f32[2,2,136,128]{3,2,1,0:T(8,128)S(1)}, u32[]{:S(2)}, u32[]{:S(2)}) collective-permute-start(f32[2,2,136,128]{3,2,1,0:T(8,128)S(1)} %get-tuple-element.87), channel_id=1, source_target_pairs={{0,1},{1,2},{2,3},{3,4},{4,5},{5,6},{6,7},{8,9},{9,10},{10,11},{11... | collective-permute-start | bytes 835592 | tf_op jit(solution)/shard_map/ppermute | solution.py:377
  25.9 27.5 %collective-permute-start.5 = (f32[2,2,136,128]{3,2,1,0:T(8,128)S(1)}, f32[2,2,136,128]{3,2,1,0:T(8,128)S(1)}, u32[]{:S(2)}, u32[]{:S(2)}) collective-permute-start(f32[2,2,136,128]{3,2,1,0:T(8,128)S(1)} %get-tuple-element.86), channel_id=1, source_target_pairs={{1,0},{2,1},{3,2},{4,3},{5,4},{6,5},{7,6},{9,8},{10,9},{11,10},{12... | collective-permute-start | bytes 835592 | tf_op jit(solution)/shard_map/ppermute | solution.py:377
  27.3 2.2 %copy-start.1 = (f32[2,512,1024]{2,1,0:T(8,128)S(1)}, f32[2,512,1024]{2,1,0:T(8,128)}, u32[]{:S(2)}) copy-start(f32[2,512,1024]{2,1,0:T(8,128)} %obj.1) | copy-start | bytes 12582916
  29.5 1.0 copy-start.10
  30.5 1.0 copy-start.13
  31.5 1.4 copy-start.16
  33.0 1.2 copy-start.18
  34.2 19.2 %copy-start.11 = (f32[2,520,128]{2,1,0:T(8,128)S(1)}, f32[2,520,128]{2,1,0:T(8,128)}, u32[]{:S(2)}) copy-start(f32[2,520,128]{2,1,0:T(8,128)} %copy-done.9) | copy-start | bytes 1597444
  34.2 19.2 %copy-start.14 = (f32[2,520,128]{2,1,0:T(8,128)S(1)}, f32[2,520,128]{2,1,0:T(8,128)}, u32[]{:S(2)}) copy-start(f32[2,520,128]{2,1,0:T(8,128)} %copy-done.12) | copy-start | bytes 1597444
  34.2 19.2 %copy-start.17 = (f32[1,1,6,256,256]{4,3,2,1,0:T(8,128)S(1)}, f32[1,1,6,256,256]{4,3,2,1,0:T(8,128)}, u32[]{:S(2)}) copy-start(f32[1,1,6,256,256]{4,3,2,1,0:T(8,128)} %param.11) | copy-start | bytes 4718596
  34.2 19.2 %copy-start.19 = (bf16[4,2,256,256]{3,2,1,0:T(8,128)(2,1)S(1)}, bf16[4,2,256,256]{3,2,1,0:T(8,128)(2,1)}, u32[]{:S(2)}) copy-start(bf16[4,2,256,256]{3,2,1,0:T(8,128)(2,1)} %constant.42.clone.refs_8_.refs_13_) | copy-start | bytes 3145732
  51.4 2.0 %copy-start.3 = (f32[2,512,1024]{2,1,0:T(8,128)}, f32[2,512,1024]{2,1,0:T(8,128)S(1)}, u32[]{:S(2)}) copy-start(f32[2,512,1024]{2,1,0:T(8,128)S(1)} %get-tuple-element.41.core_e) | copy-start | bytes 12582916
  59.8 12.3 %copy-start.5 = (f32[2,512,128]{2,1,0:T(8,128)}, f32[2,512,128]{2,1,0:T(8,128)S(1)}, u32[]{:S(2)}) copy-start(f32[2,512,128]{2,1,0:T(8,128)S(1)} %get-tuple-element.32) | copy-start | bytes 1572868
  59.8 12.3 %copy-start.7 = (f32[2,512,128]{2,1,0:T(8,128)}, f32[2,512,128]{2,1,0:T(8,128)S(1)}, u32[]{:S(2)}) copy-start(f32[2,512,128]{2,1,0:T(8,128)S(1)} %get-tuple-element.36) | copy-start | bytes 1572868
  60.0 10.7 %collective-permute-start.9 = (f32[4,9,8,256]{3,2,1,0:T(8,128)S(1)}, f32[4,9,8,256]{3,2,1,0:T(8,128)S(1)}, u32[]{:S(2)}, u32[]{:S(2)}) collective-permute-start(f32[4,9,8,256]{3,2,1,0:T(8,128)S(1)} %get-tuple-element.62), channel_id=1, source_target_pairs={{0,8},{1,9},{2,10},{3,11},{4,12},{5,13},{6,14},{7,15},{8,0},{9,1},... | collective-permute-start | bytes 884744 | tf_op jit(solution)/shard_map/ppermute | solution.py:414
  67.7 4.3 %collective-permute-start.8 = (f32[4,9,8,256]{3,2,1,0:T(8,128)S(1)}, f32[4,9,8,256]{3,2,1,0:T(8,128)S(1)}, u32[]{:S(2)}, u32[]{:S(2)}) collective-permute-start(f32[4,9,8,256]{3,2,1,0:T(8,128)S(1)} %get-tuple-element.63), channel_id=1, source_target_pairs={{0,8},{1,9},{2,10},{3,11},{4,12},{5,13},{6,14},{7,15},{8,0},{9,1},... | collective-permute-start | bytes 884744 | tf_op jit(solution)/shard_map/ppermute | solution.py:414
  67.8 4.2 %collective-permute-start.7 = (f32[4,9,8,256]{3,2,1,0:T(8,128)S(1)}, f32[4,9,8,256]{3,2,1,0:T(8,128)S(1)}, u32[]{:S(2)}, u32[]{:S(2)}) collective-permute-start(f32[4,9,8,256]{3,2,1,0:T(8,128)S(1)} %get-tuple-element.64), channel_id=1, source_target_pairs={{0,8},{1,9},{2,10},{3,11},{4,12},{5,13},{6,14},{7,15},{8,0},{9,1},... | collective-permute-start | bytes 884744 | tf_op jit(solution)/shard_map/ppermute | solution.py:414
  68.2 3.8 %collective-permute-start.6 = (f32[4,9,8,256]{3,2,1,0:T(8,128)S(1)}, f32[4,9,8,256]{3,2,1,0:T(8,128)S(1)}, u32[]{:S(2)}, u32[]{:S(2)}) collective-permute-start(f32[4,9,8,256]{3,2,1,0:T(8,128)S(1)} %get-tuple-element.61), channel_id=1, source_target_pairs={{0,8},{1,9},{2,10},{3,11},{4,12},{5,13},{6,14},{7,15},{8,0},{9,1},... | collective-permute-start | bytes 884744 | tf_op jit(solution)/shard_map/ppermute | solution.py:414
  68.3 55.8 %collective-permute-start.16 = (f32[2,128,1280]{2,1,0:T(8,128)}, f32[2,128,1280]{2,1,0:T(8,128)}, u32[]{:S(2)}, u32[]{:S(2)}) collective-permute-start(f32[2,128,1280]{2,1,0:T(8,128)} %get-tuple-element.28), channel_id=1, source_target_pairs={{0,1},{1,2},{2,3},{3,4},{4,5},{5,6},{6,7},{8,9},{9,10},{10,11},{11... | collective-permute-start | bytes 3932168 | tf_op jit(solution)/shard_map/ppermute | solution.py:377
  70.6 53.4 %collective-permute-start.17 = (f32[2,128,1280]{2,1,0:T(8,128)}, f32[2,128,1280]{2,1,0:T(8,128)}, u32[]{:S(2)}, u32[]{:S(2)}) collective-permute-start(f32[2,128,1280]{2,1,0:T(8,128)} %get-tuple-element.29), channel_id=1, source_target_pairs={{1,0},{2,1},{3,2},{4,3},{5,4},{6,5},{7,6},{9,8},{10,9},{11,10},{12... | collective-permute-start | bytes 3932168 | tf_op jit(solution)/shard_map/ppermute | solution.py:377
  72.2 14.5 %collective-permute-start.12 = (f32[4,9,8,256]{3,2,1,0:T(8,128)S(1)}, f32[4,9,8,256]{3,2,1,0:T(8,128)S(1)}, u32[]{:S(2)}, u32[]{:S(2)}) collective-permute-start(f32[4,9,8,256]{3,2,1,0:T(8,128)S(1)} %get-tuple-element.59), channel_id=1, source_target_pairs={{0,96},{1,97},{2,98},{3,99},{4,100},{5,101},{6,102},{7,103},{8,104... | collective-permute-start | bytes 884744 | tf_op jit(solution)/shard_map/ppermute | solution.py:423
  76.1 15.3 %collective-permute-start.11 = (f32[4,9,8,256]{3,2,1,0:T(8,128)S(1)}, f32[4,9,8,256]{3,2,1,0:T(8,128)S(1)}, u32[]{:S(2)}, u32[]{:S(2)}) collective-permute-start(f32[4,9,8,256]{3,2,1,0:T(8,128)S(1)} %get-tuple-element.60), channel_id=1, source_target_pairs={{0,64},{1,65},{2,66},{3,67},{4,68},{5,69},{6,70},{7,71},{8,72},{9,... | collective-permute-start | bytes 884744 | tf_op jit(solution)/shard_map/ppermute | solution.py:423
  84.6 13.8 %collective-permute-start.10 = (f32[4,9,8,256]{3,2,1,0:T(8,128)S(1)}, f32[4,9,8,256]{3,2,1,0:T(8,128)S(1)}, u32[]{:S(2)}, u32[]{:S(2)}) collective-permute-start(f32[4,9,8,256]{3,2,1,0:T(8,128)S(1)} %get-tuple-element.58), channel_id=1, source_target_pairs={{0,32},{1,33},{2,34},{3,35},{4,36},{5,37},{6,38},{7,39},{8,40},{9,... | collective-permute-start | bytes 884744 | tf_op jit(solution)/shard_map/ppermute | solution.py:423
  99.2 23.9 %collective-permute-start.15 = (f32[1,9,8,256]{3,2,1,0:T(8,128)}, f32[1,9,8,256]{3,2,1,0:T(8,128)}, u32[]{:S(2)}, u32[]{:S(2)}) collective-permute-start(f32[1,9,8,256]{3,2,1,0:T(8,128)} %get-tuple-element.74), channel_id=1, source_target_pairs={{0,3},{1,0},{2,1},{3,2},{4,7},{5,4},{6,5},{7,6},{8,11},{9,8},{10,9... | collective-permute-start | bytes 221192 | tf_op jit(solution)/shard_map/ppermute | solution.py:423
  113.1 9.9 %collective-permute-start.14 = (f32[1,9,8,256]{3,2,1,0:T(8,128)}, f32[1,9,8,256]{3,2,1,0:T(8,128)}, u32[]{:S(2)}, u32[]{:S(2)}) collective-permute-start(f32[1,9,8,256]{3,2,1,0:T(8,128)} %get-tuple-element.75), channel_id=1, source_target_pairs={{0,2},{1,3},{2,0},{3,1},{4,6},{5,7},{6,4},{7,5},{8,10},{9,11},{10,... | collective-permute-start | bytes 221192 | tf_op jit(solution)/shard_map/ppermute | solution.py:423
  113.1 9.9 %collective-permute-start.13 = (f32[1,9,8,256]{3,2,1,0:T(8,128)S(1)}, f32[1,9,8,256]{3,2,1,0:T(8,128)}, u32[]{:S(2)}, u32[]{:S(2)}) collective-permute-start(f32[1,9,8,256]{3,2,1,0:T(8,128)S(1)} %get-tuple-element.73), channel_id=1, source_target_pairs={{0,1},{1,2},{2,3},{3,0},{4,5},{5,6},{6,7},{7,4},{8,9},{9,10},{10,1... | collective-permute-start | bytes 221192 | tf_op jit(solution)/shard_map/ppermute | solution.py:423
  118.4 1.3 copy-start.2
  119.7 9.1 %copy-start.6 = (f32[2,512,128]{2,1,0:T(8,128)S(1)}, f32[2,512,128]{2,1,0:T(8,128)}, u32[]{:S(2)}) copy-start(f32[2,512,128]{2,1,0:T(8,128)} %copy-done.5) | copy-start | bytes 1572868
  119.7 9.1 %copy-start.8 = (f32[2,512,128]{2,1,0:T(8,128)S(1)}, f32[2,512,128]{2,1,0:T(8,128)}, u32[]{:S(2)}) copy-start(f32[2,512,128]{2,1,0:T(8,128)} %copy-done.7) | copy-start | bytes 1572868
  124.1 5.9 %collective-permute-start.20 = (f32[1,9,8,256]{3,2,1,0:T(8,128)S(1)}, f32[1,9,8,256]{3,2,1,0:T(8,128)S(1)}, u32[]{:S(2)}, u32[]{:S(2)}) collective-permute-start(f32[1,9,8,256]{3,2,1,0:T(8,128)S(1)} %add_add_fusion.2), channel_id=1, source_target_pairs={{0,20},{1,21},{2,22},{3,23},{4,16},{5,17},{6,18},{7,19},{8,28},{9,... | collective-permute-start | bytes 221192 | tf_op jit(solution)/shard_map/ppermute | solution.py:402
  126.1 4.8 %collective-permute-start.19 = (f32[1,9,8,256]{3,2,1,0:T(8,128)S(1)}, f32[1,9,8,256]{3,2,1,0:T(8,128)S(1)}, u32[]{:S(2)}, u32[]{:S(2)}) collective-permute-start(f32[1,9,8,256]{3,2,1,0:T(8,128)S(1)} %add_add_fusion.2), channel_id=1, source_target_pairs={{0,4},{1,5},{2,6},{3,7},{4,0},{5,1},{6,2},{7,3},{8,12},{9,13},{10,... | collective-permute-start | bytes 221192 | tf_op jit(solution)/shard_map/ppermute | solution.py:402
  126.1 5.2 %collective-permute-start.18 = (f32[1,9,8,256]{3,2,1,0:T(8,128)S(1)}, f32[1,9,8,256]{3,2,1,0:T(8,128)S(1)}, u32[]{:S(2)}, u32[]{:S(2)}) collective-permute-start(f32[1,9,8,256]{3,2,1,0:T(8,128)S(1)} %add_add_fusion.2), channel_id=1, source_target_pairs={{0,16},{1,17},{2,18},{3,19},{4,20},{5,21},{6,22},{7,23},{8,24},{9,... | collective-permute-start | bytes 221192 | tf_op jit(solution)/shard_map/ppermute | solution.py:402
  131.4 19.3 %collective-permute-start.24 = (f32[2,512,128]{2,1,0:T(8,128)}, f32[2,512,128]{2,1,0:T(8,128)S(1)}, u32[]{:S(2)}, u32[]{:S(2)}) collective-permute-start(f32[2,512,128]{2,1,0:T(8,128)} %get-tuple-element.38), channel_id=1, source_target_pairs={{0,8},{8,16},{16,24},{24,32},{32,40},{40,48},{48,56},{56,64},{64,7... | collective-permute-start | bytes 1572872 | tf_op jit(solution)/shard_map/ppermute | solution.py:377
  135.4 15.3 %collective-permute-start.25 = (f32[2,512,128]{2,1,0:T(8,128)}, f32[2,512,128]{2,1,0:T(8,128)S(1)}, u32[]{:S(2)}, u32[]{:S(2)}) collective-permute-start(f32[2,512,128]{2,1,0:T(8,128)} %get-tuple-element.39), channel_id=1, source_target_pairs={{8,0},{16,8},{24,16},{32,24},{40,32},{48,40},{56,48},{64,56},{72,6... | collective-permute-start | bytes 1572872 | tf_op jit(solution)/shard_map/ppermute | solution.py:377
  137.4 10.6 %collective-permute-start.22 = (f32[8,8,256]{2,1,0:T(8,128)S(1)}, f32[8,8,256]{2,1,0:T(8,128)S(1)}, u32[]{:S(2)}, u32[]{:S(2)}) collective-permute-start(f32[8,8,256]{2,1,0:T(8,128)S(1)} %fusion.3), channel_id=1, source_target_pairs={{0,2},{1,3},{2,0},{3,1},{4,6},{5,7},{6,4},{7,5},{8,72},{9,73},{10,... | collective-permute-start | bytes 196616 | tf_op jit(solution)/shard_map/ppermute | solution.py:402
  146.3 3.9 %collective-permute-start.23 = (f32[8,8,256]{2,1,0:T(8,128)S(1)}, f32[8,8,256]{2,1,0:T(8,128)S(1)}, u32[]{:S(2)}, u32[]{:S(2)}) collective-permute-start(f32[8,8,256]{2,1,0:T(8,128)S(1)} %fusion.3), channel_id=1, source_target_pairs={{0,3},{1,0},{2,1},{3,2},{4,7},{5,4},{6,5},{7,6},{8,104},{9,105},{1... | collective-permute-start | bytes 196616 | tf_op jit(solution)/shard_map/ppermute | solution.py:402
  146.3 4.3 %collective-permute-start.21 = (f32[8,8,256]{2,1,0:T(8,128)S(1)}, f32[8,8,256]{2,1,0:T(8,128)S(1)}, u32[]{:S(2)}, u32[]{:S(2)}) collective-permute-start(f32[8,8,256]{2,1,0:T(8,128)S(1)} %fusion.3), channel_id=1, source_target_pairs={{0,1},{1,2},{2,3},{3,0},{4,5},{5,6},{6,7},{7,4},{8,40},{9,41},{10,... | collective-permute-start | bytes 196616 | tf_op jit(solution)/shard_map/ppermute | solution.py:402
  150.7 4.1 %copy-start.21 = (f32[2,512,128]{2,1,0:T(8,128)}, f32[2,512,128]{2,1,0:T(8,128)S(1)}, u32[]{:S(2)}) copy-start(f32[2,512,128]{2,1,0:T(8,128)S(1)} %collective-permute-done.24.left) | copy-start | bytes 1572868
  150.7 4.1 %copy-start.22 = (f32[2,512,128]{2,1,0:T(8,128)}, f32[2,512,128]{2,1,0:T(8,128)S(1)}, u32[]{:S(2)}) copy-start(f32[2,512,128]{2,1,0:T(8,128)S(1)} %collective-permute-done.25.right) | copy-start | bytes 1572868
  150.7 12.8 %collective-permute-start.27 = (f32[8,32,256]{2,1,0:T(8,128)S(1)}, f32[8,32,256]{2,1,0:T(8,128)S(1)}, u32[]{:S(2)}, u32[]{:S(2)}) collective-permute-start(f32[8,32,256]{2,1,0:T(8,128)S(1)} %pad_maximum_fusion.4), channel_id=1, source_target_pairs={{0,64},{1,65},{2,66},{3,67},{4,68},{5,69},{6,70},{7,71},{8,10},{9,... | collective-permute-start | bytes 786440 | tf_op jit(solution)/shard_map/ppermute | solution.py:402
  150.8 12.7 %collective-permute-start.28 = (f32[8,32,256]{2,1,0:T(8,128)S(1)}, f32[8,32,256]{2,1,0:T(8,128)S(1)}, u32[]{:S(2)}, u32[]{:S(2)}) collective-permute-start(f32[8,32,256]{2,1,0:T(8,128)S(1)} %pad_maximum_fusion.4), channel_id=1, source_target_pairs={{0,96},{1,97},{2,98},{3,99},{4,100},{5,101},{6,102},{7,103},{8,11}... | collective-permute-start | bytes 786440 | tf_op jit(solution)/shard_map/ppermute | solution.py:402
  154.3 9.2 %collective-permute-start.26 = (f32[8,32,256]{2,1,0:T(8,128)S(1)}, f32[8,32,256]{2,1,0:T(8,128)S(1)}, u32[]{:S(2)}, u32[]{:S(2)}) collective-permute-start(f32[8,32,256]{2,1,0:T(8,128)S(1)} %pad_maximum_fusion.4), channel_id=1, source_target_pairs={{0,32},{1,33},{2,34},{3,35},{4,36},{5,37},{6,38},{7,39},{8,9},{9,1... | collective-permute-start | bytes 786440 | tf_op jit(solution)/shard_map/ppermute | solution.py:402
  163.8 8.2 %collective-permute-start.29 = (f32[8,128,256]{2,1,0:T(8,128)S(1)}, f32[8,128,256]{2,1,0:T(8,128)S(1)}, u32[]{:S(2)}, u32[]{:S(2)}) collective-permute-start(f32[8,128,256]{2,1,0:T(8,128)S(1)} %pad_maximum_fusion.1), channel_id=1, source_target_pairs={{0,8},{1,9},{2,10},{3,11},{4,12},{5,13},{6,14},{7,15},{8,0},{9,1},... | collective-permute-start | bytes 3145736 | tf_op jit(solution)/shard_map/ppermute | solution.py:457
